TPU v7x, 256 devices: a whole 4x4x8 slice. The times are simulated.
256 devices in a mesh: vocab: 64 (over x, z, core), rows: 4 (over y).
Axes of the slice: x: 4, y: 4, z: 8, core: 2. Of those that a mesh axis runs over, the one named last changes fastest.
Arguments:
- hidden: bfloat16 [1024, 4608], P('rows'), may hold values from -6 to 6
- norm_gain: bfloat16 [4608], replicated, may hold values from 0.5 to 1.5
- embed_table: bfloat16 [131072, 4608], P('vocab', 'rows'), may hold values from -1 to 1
- tokens: int32 [1024], P('rows'), may hold values from 0 to 131071
- parents: int32 [1024], P('rows'), may hold values from 0 to 7
- prev_scores: float32 [1024], P('rows'), may hold values from -30 to -1
- lengths: int32 [1024], P('rows'), may hold values from 1 to 128
Outputs:
- log_probs: float32 [1024, 131072], P('rows', 'vocab')
- chosen_lp: float32 [1024], P('rows')
- normalized: float32 [1024], P('rows')
- next_embed: bfloat16 [1024, 4608], P('rows')
All inputs are finite; a program needn't handle non-finite values.
Results may differ from a plain program's by a relative error of at most 0.0045.
Values may be sent and summed in bfloat16 or wider, within the bound.
No kernel may reach another device: no remote copies, remote signals or barrier semaphores. Data moves between devices by JAX's collectives and lax.ppermute only.
A program may use at most 128 MiB of HBM per device.

v0:
```python
import math

import jax
import jax.numpy as jnp
from jax import lax
from jax.sharding import PartitionSpec as P

BEAMS = 8


soft_cap = 30.0
length_power = 0.6
norm_eps = 1e-06


def spread(partial_value, scale):
    terms = partial_value.astype(jnp.float32)
    total = lax.psum(terms, "vocab")
    return (total * scale).astype(jnp.bfloat16)


def local(hidden, norm_gain, embed_table, tokens, parents, prev_scores, lengths):
    shard_index = lax.axis_index("vocab")
    voc_rows = embed_table.shape[0]
    row_count = hidden.shape[0]
    width = hidden.shape[1]
    scale = math.sqrt(width)
    states = hidden.astype(jnp.float32)
    meansq = jnp.mean(states * states, axis=-1, keepdims=True)
    normed = (states * lax.rsqrt(meansq + norm_eps) * norm_gain.astype(jnp.float32)).astype(
        jnp.bfloat16
    )
    local_col = tokens - shard_index * voc_rows
    inside = (local_col >= 0) & (local_col < voc_rows)
    clipped_col = jnp.clip(local_col, 0, voc_rows - 1)
    zero_half = jnp.zeros((), jnp.bfloat16)
    all_tokens = lax.all_gather(tokens, "rows", axis=0, tiled=True)
    feature_cols = lax.all_to_all(normed, "rows", split_axis=1, concat_axis=0, tiled=True)
    logits = lax.psum_scatter(
        lax.dot_general(
            feature_cols, embed_table, (((1,), (1,)), ((), ())), preferred_element_type=jnp.float32
        ).astype(jnp.bfloat16),
        "rows",
        scatter_dimension=0,
        tiled=True,
    ).astype(jnp.float32)
    all_col = all_tokens - shard_index * voc_rows
    all_inside = (all_col >= 0) & (all_col < voc_rows)
    picked = jnp.take(embed_table, jnp.clip(all_col, 0, voc_rows - 1), axis=0)
    picked = jnp.where(all_inside[:, None], picked, zero_half)
    quarters = spread(picked, scale)
    next_embed = lax.all_to_all(quarters, "rows", split_axis=0, concat_axis=1, tiled=True)
    capped = soft_cap * jnp.tanh(logits / soft_cap)
    sum_exp = jnp.sum(jnp.exp(capped), axis=1)
    parent_rows = jnp.arange(row_count, dtype=jnp.int32) // BEAMS * BEAMS + parents
    chosen_local = jnp.where(inside, capped[parent_rows, clipped_col], 0.0)
    total_exp, chosen_logit = lax.psum((sum_exp, chosen_local), "vocab")
    lse = jnp.log(total_exp)
    log_probs = capped - lse[:, None]
    chosen_lp = chosen_logit - lse[parent_rows]
    penalty = jnp.power((5.0 + lengths.astype(jnp.float32)) / 6.0, length_power)
    normalized = (prev_scores[parent_rows] + chosen_lp) / penalty
    return (log_probs, chosen_lp, normalized, next_embed)


def solution(mesh):
    placed = (P("rows", None), P(), P("vocab", "rows"), P("rows"), P("rows"), P("rows"), P("rows"))
    return jax.shard_map(
        local,
        mesh=mesh,
        in_specs=placed,
        out_specs=(P("rows", "vocab"), P("rows"), P("rows"), P("rows", None)),
        check_vma=False,
    )
```

profile of v0, /device:TPU:1, one launch (start us, length us, event | category | flops | bytes accessed | tf_op | source)
XLA Modules:
  0.0 441.0 jit_solution(7517882210156455546)
XLA Ops:
  8.0 0.7 convert_element_type.25
  8.7 2.8 copy.16
  11.6 0.6 fusion
  12.2 3.0 fusion.2
  15.2 5.1 %all-to-all-start = ((bf16[256,4,1152]{0,2,1:T(8,128)(2,1)}), bf16[256,4,1152]{0,2,1:T(8,128)(2,1)S(1)}, u32[]{:S(2)}, u32[]{:S(2)}) async-start(bf16[256,4,1152]{0,2,1:T(8,128)(2,1)} %bitcast.12), calls=%async_computation | async-start | bytes 4718592 | tf_op jit(solution)/shard_map/all_to_all | solution.py:38
  20.4 29.0 %all-gather = s32[4,1,256]{2,1,0:T(1,128)S(1)} all-gather(s32[1,1,256]{2,1,0:T(1,128)S(1)} %bitcast.18), channel_id=1, replica_groups=mesh['vocab'=64,'rows'=4] {'rows'}, dimensions={0}, use_global_device_ids=true | all-gather | bytes 5120 | tf_op jit(solution)/shard_map/all_gather | solution.py:37
  49.4 9.3 %gather_fusion.3 = bf16[1024,1152]{1,0:T(8,128)(2,1)} fusion(bf16[2048,1152]{1,0:T(8,128)(2,1)} %param.9, s32[1024]{0:T(1024)S(1)} %fusion.3), kind=kCustom, calls=%fused_computation.3 | custom fusion | bytes 4722688 | tf_op jit(solution)/shard_map/jit(_take)/gather | solution.py:49
  58.7 3.9 select_convert_fusion
  62.6 0.0 reduce-scatter.2.cloned.1.call-start
  62.7 2.4 copy.17
  65.1 9.6 %convolution_convert_fusion = bf16[1024,2048]{1,0:T(8,128)(2,1)} fusion(bf16[1024,1152]{1,0:T(8,128)(2,1)} %bitcast.15, bf16[2048,1152]{1,0:T(8,128)(2,1)} %param.9), kind=kOutput, calls=%fused_computation.10 | convolution fusion | flops 4833935360 | bytes 11272192 | tf_op jit(solution)/shard_map/dot_general | solution.py:40
  74.7 0.0 reduce-scatter.2.cloned.1.call-update
  74.7 186.8 %all-reduce.3.cloned.1.call-done = f32[1024,1152]{1,0:T(8,128)} async-done(((f32[1024,1152]{1,0:T(8,128)}), f32[1024,1152]{1,0:T(8,128)}) %all-reduce.3.cloned.1.call-update) | async-done | bytes 4718608 | tf_op jit(solution)/shard_map/psum | solution.py:18
  261.6 4.2 multiply_convert_fusion
  265.7 4.1 all-to-all-start.1
  269.9 1.9 gather_fusion.2
  271.9 24.7 %all-to-all-done.1 = bf16[4,256,1152]{2,1,0:T(8,128)(2,1)S(1)} async-done(((bf16[4,256,1152]{2,1,0:T(8,128)(2,1)}), bf16[4,256,1152]{2,1,0:T(8,128)(2,1)S(1)}, u32[]{:S(2)}, u32[]{:S(2)}) %all-to-all-start.1) | async-done | bytes 2359328 | tf_op jit(solution)/shard_map/all_to_all | solution.py:52
  296.5 1.6 copy.19
  298.1 1.9 tanh_multiply_fusion
  300.1 2.3 gather_fusion
  302.4 126.9 %all-reduce = (f32[256]{0:T(256)S(1)}, f32[256]{0:T(256)S(1)}) all-reduce(f32[256]{0:T(256)S(1)} %get-tuple-element.11, f32[256]{0:T(256)S(1)} %and_select_fusion.1), channel_id=1, replica_groups=mesh['vocab'=64,'rows'=4] {'vocab'}, use_global_device_ids=true, to_apply=%region_3.4 | all-reduce | flops 512 | bytes 4096 | tf_op jit(solution)/shard_map/psum | solution.py:57
  429.3 2.0 gather_fusion.1
  431.3 0.6 power_multiply_fusion
  431.9 1.7 broadcast_subtract_fusion
  (24 shorter events, 0.1 us)
Async XLA Ops:
  8.0 261.9 %copy-start = (f32[256]{0:T(256)S(1)}, f32[256]{0:T(256)}, u32[]{:S(2)}) copy-start(f32[256]{0:T(256)} %param.12) | copy-start | bytes 3076
  15.2 5.2 %copy-start.2 = (s32[256]{0:T(256)S(1)}, s32[256]{0:T(256)}, u32[]{:S(2)}) copy-start(s32[256]{0:T(256)} %param.10) | copy-start | bytes 3076
  15.2 47.5 %all-to-all-start = ((bf16[256,4,1152]{0,2,1:T(8,128)(2,1)}), bf16[256,4,1152]{0,2,1:T(8,128)(2,1)S(1)}, u32[]{:S(2)}, u32[]{:S(2)}) async-start(bf16[256,4,1152]{0,2,1:T(8,128)(2,1)} %bitcast.12), calls=%async_computation | async-start | bytes 4718592 | tf_op jit(solution)/shard_map/all_to_all | solution.py:38
  20.4 241.2 %all-reduce.3.cloned.1.call-start = ((), (), s32[]{:S(2)}) async-start(), calls=%async_computation.4 | async-start | bytes 9437184 | tf_op jit(solution)/shard_map/psum | solution.py:18
  62.6 235.5 %reduce-scatter.2.cloned.1.call-start = ((), (), s32[]{:S(2)}) async-start(), calls=%async_computation.3 | async-start | bytes 5242880 | tf_op jit(solution)/shard_map/reduce_scatter | solution.py:39
  265.7 4.1 copy-start.3
  265.7 30.8 %all-to-all-start.1 = ((bf16[4,256,1152]{2,1,0:T(8,128)(2,1)}), bf16[4,256,1152]{2,1,0:T(8,128)(2,1)S(1)}, u32[]{:S(2)}, u32[]{:S(2)}) async-start(bf16[4,256,1152]{2,1,0:T(8,128)(2,1)} %bitcast.5), calls=%async_computation.2 | async-start | bytes 4718592 | tf_op jit(solution)/shard_map/all_to_all | solution.py:52
  298.1 133.1 %copy-start.4 = (s32[256]{0:T(256)S(1)}, s32[256]{0:T(256)}, u32[]{:S(2)}) copy-start(s32[256]{0:T(256)} %param.13) | copy-start | bytes 3076
  298.1 133.7 %copy-start.1 = (bf16[256,2048]{1,0:T(8,128)(2,1)S(1)}, bf16[256,2048]{1,0:T(8,128)(2,1)}, u32[]{:S(2)}) copy-start(bf16[256,2048]{1,0:T(8,128)(2,1)} %reduce-scatter.2.cloned.1.call-done) | copy-start | bytes 3145732
Sparse Core Ops, SparseCore 0:
  62.8 198.7 all-reduce.2
Sparse Core Ops, SparseCore 1:
  74.8 52.7 reduce-scatter.1
where the time goes:
time: 443 us; the launch traced here: 441 us
  waiting for transfers between devices  212 us (48%)
  blocking collectives  156 us (35%)
  local copies, waits for them, and re-layouts  22.5 us (5%)
  other arithmetic  16.7 us (4%)
  between operations  15.6 us (4%)
  matrix products  9.56 us (2%)
  starting transfers between devices  9.32 us (2%)
    psum x1, waiting for transfers between devices, spread(): total = lax.psum(terms, 'vocab')  187 us
    psum x1, blocking collectives, local(): total_exp, chosen_logit = lax.psum((sum_exp, chosen_local), 'vocab')  127 us
    all_gather x1, blocking collectives, local(): all_tokens = lax.all_gather(tokens, 'rows', axis=0, tiled=True)  29 us
    all_to_all x1, waiting for transfers between devices, local(): lax.all_to_all(quarters, 'rows', split_axis=0, concat_axis=1, tiled=True)  24.7 us
    dot_general x1, matrix products, local(): lax.dot_general(feature_cols, embed_table, (((1,), (1,)), ((), ())), pref...  9.56 us
    gather x1, local copies, waits for them, and re-layouts, local(): picked = jnp.take(embed_table, jnp.clip(all_col, 0, voc_rows - 1), axis=0)  9.31 us
  transfers between devices with their start and end apart: 4, of which 2 were waited for; matrix products, arithmetic and copies ran while one was open for 7% of the time, Pallas kernels for 0%

commit v1 on v0

v1 whole, which is shorter than its diff:
```python
import math

import jax
import jax.numpy as jnp
from jax import lax
from jax.sharding import Mesh, PartitionSpec as P

BEAMS = 8

soft_cap = 30.0
length_power = 0.6
norm_eps = 1e-06

VOC = ("x", "z", "c")
NX, NZ, NC, NY = 4, 8, 2, 4


def shift(value, axis, size, step):
    return lax.ppermute(value, axis, [(i, (i + step) % size) for i in range(size)])


def exchange(value, axes):
    return lax.all_to_all(value, axes, 0, 0, tiled=True)


def dot_nt(left, right):
    return lax.dot_general(left, right, (((1,), (1,)), ((), ())), preferred_element_type=jnp.float32)


def lookup(tokens, embed_table, scale):
    voc_rows, depth = embed_table.shape
    shard = lax.axis_index(VOC)
    core = lax.axis_index("c")
    rows = tokens.shape[0]
    part = rows // (NC * NX)
    halves = tokens.reshape(NC, NX, 1, part)
    ordered = jnp.where(core == 0, halves, halves[::-1])
    both = jnp.concatenate(
        [ordered] + [shift(ordered, "y", NY, step) for step in (1, 2, 3)], axis=2
    )
    y = lax.axis_index("y")
    order = (y - jnp.arange(NY)) % NY
    planes = sum(
        jnp.where((order == j)[None, None, :, None], both[:, :, j : j + 1], 0) for j in range(NY)
    )
    local_col = (planes - shard * voc_rows).reshape(NC, rows * NY // NC)

    def rows_of(col):
        hot = (col[:, None] == jnp.arange(voc_rows, dtype=jnp.int32)[None, :]).astype(jnp.bfloat16)
        found = jnp.dot(hot, embed_table, preferred_element_type=jnp.float32)
        return (found * scale).astype(jnp.bfloat16)

    other = shift(rows_of(local_col[1]), "c", NC, 1)
    mine = (rows_of(local_col[0]) + other).reshape(NX, NY * part, depth)
    mine = jnp.sum(exchange(mine, "x"), axis=0)
    mine = exchange(mine.reshape(NY, part, depth), "y")
    mine = jnp.sum(exchange(mine.reshape(NZ, NY * part // NZ, depth), "z"), axis=0)
    mine = exchange(jnp.broadcast_to(mine[None], (NZ,) + mine.shape), "z")
    mine = lax.all_gather(mine.reshape(NY, part, depth), "x")
    other = shift(mine, "c", NC, 1)
    full = jnp.stack([jnp.where(core == 0, mine, other), jnp.where(core == 0, other, mine)])
    return full.transpose(0, 1, 3, 2, 4).reshape(rows, NY * depth)


def local(hidden, norm_gain, embed_table, tokens, parents, prev_scores, lengths):
    shard = lax.axis_index(VOC)
    core = lax.axis_index("c")
    y = lax.axis_index("y")
    voc_rows, depth = embed_table.shape
    row_count, width = hidden.shape
    half = row_count // NC
    half_voc = voc_rows // 2
    scale = math.sqrt(width)

    gain_part = lax.dynamic_slice(norm_gain, (y * depth,), (depth,)).astype(jnp.float32)

    def gained(features):
        return (features.astype(jnp.float32) * gain_part).astype(jnp.bfloat16)

    def fetch(step):
        there = (y + step) % NY
        piece = lax.dynamic_slice(hidden, (core * half, there * depth), (half, depth))
        mine = shift(piece, "y", NY, step)
        other = shift(mine, "c", NC, 1)
        return gained(
            jnp.concatenate(
                [jnp.where(core == 0, mine, other), jnp.where(core == 0, other, mine)], axis=0
            )
        )

    upper, lower = embed_table[:half_voc], embed_table[half_voc:]
    far = fetch(2)
    far_a = shift(dot_nt(far, upper).astype(jnp.bfloat16), "y", NY, 1)
    far_b = shift(dot_nt(far, lower).astype(jnp.bfloat16), "y", NY, 3)
    ahead = fetch(3)
    behind = fetch(1)
    left_b = shift(dot_nt(ahead, lower).astype(jnp.bfloat16), "y", NY, 1)
    right_a = shift(dot_nt(behind, upper).astype(jnp.bfloat16), "y", NY, 3)
    left_a = shift((dot_nt(ahead, upper) + far_a.astype(jnp.float32)).astype(jnp.bfloat16), "y", NY, 1)
    right_b = shift((dot_nt(behind, lower) + far_b.astype(jnp.float32)).astype(jnp.bfloat16), "y", NY, 3)
    own = gained(lax.dynamic_slice(hidden, (0, y * depth), (row_count, depth)))
    states = hidden.astype(jnp.float32)
    meansq = jnp.mean(states * states, axis=-1, keepdims=True)
    row_scale = lax.rsqrt(meansq + norm_eps)

    def total(part, table_part, one, two):
        return dot_nt(part, table_part) + one.astype(jnp.float32) + two.astype(jnp.float32)

    logits = row_scale * jnp.concatenate(
        [total(own, upper, left_a, right_a), total(own, lower, left_b, right_b)], axis=1
    )

    local_col = tokens - shard * voc_rows
    inside = (local_col >= 0) & (local_col < voc_rows)
    clipped_col = jnp.clip(local_col, 0, voc_rows - 1)
    capped = soft_cap * jnp.tanh(logits / soft_cap)
    sum_exp = jnp.sum(jnp.exp(capped), axis=1)
    parent_rows = jnp.arange(row_count, dtype=jnp.int32) // BEAMS * BEAMS + parents
    chosen_local = jnp.where(inside, capped[parent_rows, clipped_col], 0.0)
    sums = jnp.concatenate([sum_exp, chosen_local])[None]
    sums = jnp.sum(exchange(jnp.broadcast_to(sums, (NX * NZ * NC, 2 * row_count)), VOC), axis=0)
    lse = jnp.log(sums[:row_count])
    log_probs = capped - lse[:, None]
    chosen_lp = sums[row_count:] - lse[parent_rows]
    penalty = jnp.power((5.0 + lengths.astype(jnp.float32)) / 6.0, length_power)
    normalized = (prev_scores[parent_rows] + chosen_lp) / penalty
    next_embed = lookup(tokens, embed_table, scale)
    return (log_probs, chosen_lp, normalized, next_embed)


def solution(mesh):
    split = Mesh(mesh.devices.reshape(NX, NZ, NC, NY), VOC + ("y",))
    placed = (P("y", None), P(), P(VOC, "y"), P("y"), P("y"), P("y"), P("y"))
    return jax.shard_map(
        local,
        mesh=split,
        in_specs=placed,
        out_specs=(P("y", VOC), P("y"), P("y"), P("y", None)),
        check_vma=False,
    )
```

time: 443 us -> 163 us (0.37)
  waiting for transfers between devices: 212 us -> 36.4 us
  blocking collectives: 156 us -> 0 us
  starting transfers between devices: 9.32 us -> 50 us
  matrix products: 9.56 us -> 37.8 us
  local copies, waits for them, and re-layouts: 22.5 us -> 13.6 us
  other arithmetic: 16.7 us -> 10.2 us
    psum x1 -> x0, waiting for transfers between devices: 187 us -> none  [spread(): total = lax.psum(terms, 'vocab')]
    psum x1 -> x0, blocking collectives: 127 us -> none  [local(): total_exp, chosen_logit = lax.psum((sum_exp, chosen_local), 'vocab')]
    all_gather x1 -> x0, blocking collectives: 29 us -> none  [local(): all_tokens = lax.all_gather(tokens, 'rows', axis=0, tiled=True)]
    dot_general x1 -> x10, matrix products: 9.56 us -> 37.8 us  [the longest x8 24.6 us: dot_nt(): lax.dot_general(left, right, (((1,), (1,)), ((), ())), preferred_element_...]
    all_to_all x2 -> x5, starting transfers between devices: 9.28 us -> 31.9 us  [exchange(): return lax.all_to_all(value, axes, 0, 0, tiled=True)]
    ppermute x0 -> x17, starting transfers between devices: none -> 18 us  [shift(): lax.ppermute(value, axis, [(i, (i + step) % size) for i in range(size)])]
    convert_element_type x4 -> x1, other arithmetic: 11.7 us -> 0.77 us  [local(): lax.dynamic_slice(norm_gain, (y * depth,), (depth,)).astype(jnp.float32)]
    ppermute x0 -> x17, waiting for transfers between devices: none -> 9.92 us  [shift(): lax.ppermute(value, axis, [(i, (i + step) % size) for i in range(size)])]
  transfers between devices with their start and end apart: 4 -> 23, of which waited for: 2 -> 7; matrix products, arithmetic and copies ran while one was open for 7% -> 35% of each run, Pallas kernels for 0% -> 0%
where the time goes in v1:
time: 163 us; the launch traced here: 162 us
  starting transfers between devices  50 us (31%)
  matrix products  37.8 us (23%)
  waiting for transfers between devices  36.4 us (22%)
  between operations  14.4 us (9%)
  local copies, waits for them, and re-layouts  13.6 us (8%)
  other arithmetic  10.2 us (6%)
    all_to_all x5, starting transfers between devices, exchange(): return lax.all_to_all(value, axes, 0, 0, tiled=True)  31.9 us
    all_to_all x5, waiting for transfers between devices, exchange(): return lax.all_to_all(value, axes, 0, 0, tiled=True)  26.4 us
    dot_general x8, matrix products, dot_nt(): lax.dot_general(left, right, (((1,), (1,)), ((), ())), preferred_element_...  24.6 us
    ppermute x17, starting transfers between devices, shift(): lax.ppermute(value, axis, [(i, (i + step) % size) for i in range(size)])  18 us
    dot_general x2, matrix products, rows_of(): found = jnp.dot(hot, embed_table, preferred_element_type=jnp.float32)  13.2 us
    ppermute x17, waiting for transfers between devices, shift(): lax.ppermute(value, axis, [(i, (i + step) % size) for i in range(size)])  9.92 us
  transfers between devices with their start and end apart: 23, of which 7 were waited for; matrix products, arithmetic and copies ran while one was open for 35% of the time, Pallas kernels for 0%

profile of v1, /device:TPU:1, one launch (start us, length us, event | category | flops | bytes accessed | tf_op | source)
XLA Modules:
  0.0 162.5 jit_solution(14812654455768343589)
XLA Ops:
  10.1 2.6 %collective-permute-start.13 = (s32[2,4,1,32]{3,1,0,2:T(4,128)S(1)}, s32[2,4,1,32]{3,1,0,2:T(4,128)S(1)}, u32[]{:S(2)}, u32[]{:S(2)}) collective-permute-start(s32[2,4,1,32]{3,1,0,2:T(4,128)S(1)} %reverse_select_fusion), channel_id=1, source_target_pairs={{0,2},{1,3},{2,0},{3,1},{4,6},{5,7},{6,4},{7,5},{8,10},{9,11},{10,... | collective-permute-start | bytes 3080 | tf_op jit(solution)/shard_map/ppermute | solution.py:19
  15.3 2.6 %collective-permute-start = (bf16[128,1152]{1,0:T(8,128)(2,1)S(1)}, bf16[128,1152]{1,0:T(8,128)(2,1)S(1)}, u32[]{:S(2)}, u32[]{:S(2)}) collective-permute-start(bf16[128,1152]{1,0:T(8,128)(2,1)S(1)} %get-tuple-element.12), channel_id=1, source_target_pairs={{0,3},{1,0},{2,1},{3,2},{4,7},{5,4},{6,5},{7,6},{8,11},{9,8},{10,9... | collective-permute-start | bytes 884744 | tf_op jit(solution)/shard_map/ppermute | solution.py:19
  18.2 6.5 %fusion.5 = bf16[512,1152]{1,0:T(8,128)(2,1)} fusion(bf16[2048,1152]{1,0:T(8,128)(2,1)} %param.9, s32[512]{0:T(512)S(1)} %eq.84), kind=kOutput, calls=%fused_computation.11 | convolution fusion | flops 2418147328 | bytes 5900288 | tf_op jit(solution)/shard_map/dot_general | solution.py:50
  24.8 2.8 %collective-permute-start.15 = (bf16[512,1152]{1,0:T(8,128)(2,1)}, bf16[512,1152]{1,0:T(8,128)(2,1)}, u32[]{:S(2)}, u32[]{:S(2)}) collective-permute-start(bf16[512,1152]{1,0:T(8,128)(2,1)} %fusion.5), channel_id=1, source_target_pairs={{0,4},{4,0},{1,5},{5,1},{2,6},{6,2},{3,7},{7,3},{8,12},{12,8},{9,1... | collective-permute-start | bytes 3538952 | tf_op jit(solution)/shard_map/ppermute | solution.py:19
  28.9 3.7 %fusion.26 = f32[256,1024]{1,0:T(8,128)} fusion(bf16[2048,1152]{1,0:T(8,128)(2,1)} %param.9, f32[1152]{0:T(1024)S(1)} %dynamic-slice_convert_fusion, bf16[256,4608]{1,0:T(8,128)(2,1)S(1)} %copy-done.1, s32[]{:T(128)S(6)} %select_n.130), kind=kOutput, calls=%fused_computation.35 | convolution fusion | flops 604864512 | bytes 4005892 | tf_op jit(solution)/shard_map/dot_general | solution.py:27
  34.4 6.7 %fusion.6 = bf16[512,1152]{1,0:T(8,128)(2,1)} fusion(bf16[512,1152]{1,0:T(8,128)(2,1)} %collective-permute-done.15, bf16[2048,1152]{1,0:T(8,128)(2,1)} %param.9, s32[512]{0:T(512)S(1)} %eq.80), kind=kOutput, calls=%fused_computation.12 | convolution fusion | flops 2418737152 | bytes 7079936 | tf_op jit(solution)/shard_map/dot_general | solution.py:50
  41.0 3.5 %all-to-all-start.1 = ((bf16[4,128,1152]{2,1,0:T(8,128)(2,1)}), bf16[4,128,1152]{2,1,0:T(8,128)(2,1)S(1)}, u32[]{:S(2)}, u32[]{:S(2)}) async-start(bf16[4,128,1152]{2,1,0:T(8,128)(2,1)} %bitcast.4), calls=%async_computation.1 | async-start | bytes 2359296 | tf_op jit(solution)/shard_map/all_to_all | solution.py:23
  44.7 3.6 %fusion.28 = bf16[256,1024]{1,0:T(8,128)(2,1)} fusion(bf16[2048,1152]{1,0:T(8,128)(2,1)} %param.9, bf16[128,1152]{1,0:T(8,128)(2,1)S(1)} %get-tuple-element.20, bf16[128,1152]{1,0:T(8,128)(2,1)S(1)} %get-tuple-element.19, f32[1152]{0:T(1024)S(1)} %dynamic-slice_convert_fusion), kind=kOutput, calls=%fused_computation.37 | convolution fusion | flops 606011392 | bytes 3478016 | tf_op jit(solution)/shard_map/dot_general | solution.py:27
  49.3 11.5 %all-to-all-done.1 = bf16[4,128,1152]{2,1,0:T(8,128)(2,1)S(1)} async-done(((bf16[4,128,1152]{2,1,0:T(8,128)(2,1)}), bf16[4,128,1152]{2,1,0:T(8,128)(2,1)S(1)}, u32[]{:S(2)}, u32[]{:S(2)}) %all-to-all-start.1) | async-done | bytes 1179680 | tf_op jit(solution)/shard_map/all_to_all | solution.py:23
  61.8 4.1 %all-to-all-start.2 = ((bf16[4,32,1152]{2,1,0:T(8,128)(2,1)}), bf16[4,32,1152]{2,1,0:T(8,128)(2,1)}, u32[]{:S(2)}, u32[]{:S(2)}) async-start(bf16[4,32,1152]{2,1,0:T(8,128)(2,1)} %bitcast.5), calls=%async_computation.2 | async-start | bytes 589824 | tf_op jit(solution)/shard_map/all_to_all | solution.py:23
  65.9 3.5 %fusion.37 = bf16[256,1024]{1,0:T(8,128)(2,1)} fusion(bf16[2048,1152]{1,0:T(8,128)(2,1)} %param.9, bf16[128,1152]{1,0:T(8,128)(2,1)} %copy-done.9, bf16[128,1152]{1,0:T(8,128)(2,1)} %copy-done.8, f32[1152]{0:T(1024)S(1)} %dynamic-slice_convert_fusion), kind=kOutput, calls=%fused_computation.40 | convolution fusion | flops 606011392 | bytes 3478016 | tf_op jit(solution)/shard_map/dot_general | solution.py:27
  69.5 2.2 %all-to-all-done.2 = bf16[4,32,1152]{2,1,0:T(8,128)(2,1)} async-done(((bf16[4,32,1152]{2,1,0:T(8,128)(2,1)}), bf16[4,32,1152]{2,1,0:T(8,128)(2,1)}, u32[]{:S(2)}, u32[]{:S(2)}) %all-to-all-start.2) | async-done | bytes 294944 | tf_op jit(solution)/shard_map/all_to_all | solution.py:23
  71.7 7.9 %all-to-all-start.3 = ((bf16[8,16,1152]{2,1,0:T(8,128)(2,1)}), bf16[8,16,1152]{2,1,0:T(8,128)(2,1)S(1)}, u32[]{:S(2)}, u32[]{:S(2)}) async-start(bf16[8,16,1152]{2,1,0:T(8,128)(2,1)} %bitcast.6), calls=%async_computation.3 | async-start | bytes 589824 | tf_op jit(solution)/shard_map/all_to_all | solution.py:23
  79.6 3.4 %fusion.31 = bf16[256,1024]{1,0:T(8,128)(2,1)} fusion(bf16[2048,1152]{1,0:T(8,128)(2,1)} %param.9, bf16[128,1152]{1,0:T(8,128)(2,1)S(1)} %get-tuple-element.18, bf16[128,1152]{1,0:T(8,128)(2,1)S(1)} %get-tuple-element.17, f32[1152]{0:T(1024)S(1)} %dynamic-slice_convert_fusion), kind=kOutput, calls=%fused_computation.38 | convolution fusion | flops 606011392 | bytes 3478016 | tf_op jit(solution)/shard_map/dot_general | solution.py:27
  85.7 3.6 %all-to-all-done.3 = bf16[8,16,1152]{2,1,0:T(8,128)(2,1)S(1)} async-done(((bf16[8,16,1152]{2,1,0:T(8,128)(2,1)}), bf16[8,16,1152]{2,1,0:T(8,128)(2,1)S(1)}, u32[]{:S(2)}, u32[]{:S(2)}) %all-to-all-start.3) | async-done | bytes 294944 | tf_op jit(solution)/shard_map/all_to_all | solution.py:23
  90.1 3.4 %all-to-all-start.4 = ((bf16[8,16,1152]{2,1,0:T(8,128)(2,1)}), bf16[8,16,1152]{2,1,0:T(8,128)(2,1)S(1)}, u32[]{:S(2)}, u32[]{:S(2)}) async-start(bf16[8,16,1152]{2,1,0:T(8,128)(2,1)} %broadcast_in_dim.114), calls=%async_computation.4 | async-start | bytes 589824 | tf_op jit(solution)/shard_map/all_to_all | solution.py:23
  93.6 3.5 %fusion.34 = bf16[256,1024]{1,0:T(8,128)(2,1)} fusion(bf16[2048,1152]{1,0:T(8,128)(2,1)} %param.9, bf16[128,1152]{1,0:T(8,128)(2,1)} %get-tuple-element.16, bf16[128,1152]{1,0:T(8,128)(2,1)S(1)} %get-tuple-element.15, f32[1152]{0:T(1024)S(1)} %dynamic-slice_convert_fusion), kind=kOutput, calls=%fused_computation.39 | convolution fusion | flops 606011392 | bytes 3478016 | tf_op jit(solution)/shard_map/dot_general | solution.py:27
  98.1 3.4 %add_convert_fusion.1 = bf16[256,1024]{1,0:T(8,128)(2,1)} fusion(bf16[256,1024]{1,0:T(8,128)(2,1)} %collective-permute-done.4, bf16[2048,1152]{1,0:T(8,128)(2,1)} %param.9, bf16[128,1152]{1,0:T(8,128)(2,1)S(1)} %copy-done.7, bf16[128,1152]{1,0:T(8,128)(2,1)S(1)} %get-tuple-element.15, f32[1152]{0:T(1024)S(1)} %dynamic-slice_convert_fusion), kind=kOutput, calls=%fused_computation.51 | convolution fusion | flops 606535680 | bytes 4002304 | tf_op jit(solution)/shard_map/dot_general | solution.py:27
  104.8 2.6 %add_convert_fusion = bf16[256,1024]{1,0:T(8,128)(2,1)S(1)} fusion(bf16[256,1024]{1,0:T(8,128)(2,1)} %collective-permute-done.10, bf16[2048,1152]{1,0:T(8,128)(2,1)} %param.9, bf16[128,1152]{1,0:T(8,128)(2,1)S(1)} %get-tuple-element.18, bf16[128,1152]{1,0:T(8,128)(2,1)S(1)} %get-tuple-element.17, f32[1152]{0:T(1024)S(1)} %dynamic-slice_convert_fusion), kind=kOutput, calls=%fused_computation.49 | convolution fusion | flops 606535680 | bytes 4002304 | tf_op jit(solution)/shard_map/dot_general | solution.py:27
  107.5 2.6 %collective-permute-start.11 = (bf16[256,1024]{1,0:T(8,128)(2,1)S(1)}, bf16[256,1024]{1,0:T(8,128)(2,1)S(1)}, u32[]{:S(2)}, u32[]{:S(2)}) collective-permute-start(bf16[256,1024]{1,0:T(8,128)(2,1)S(1)} %add_convert_fusion), channel_id=1, source_target_pairs={{0,3},{1,0},{2,1},{3,2},{4,7},{5,4},{6,5},{7,6},{8,11},{9,8},{10,9... | collective-permute-start | bytes 1572872 | tf_op jit(solution)/shard_map/ppermute | solution.py:19
  110.1 9.0 %collective-permute-done.5 = bf16[256,1024]{1,0:T(8,128)(2,1)} collective-permute-done((bf16[256,1024]{1,0:T(8,128)(2,1)}, bf16[256,1024]{1,0:T(8,128)(2,1)}, u32[]{:S(2)}, u32[]{:S(2)}) %collective-permute-start.5) | collective-permute-done | bytes 524320 | tf_op jit(solution)/shard_map/ppermute | solution.py:19
  121.4 2.3 %gather_fusion = f32[256]{0:T(256)S(1)} fusion(f32[256,2048]{1,0:T(8,128)S(1)} %get-tuple-element.7, s32[256]{0:T(256)S(1)} %get-tuple-element.8), kind=kCustom, calls=%fused_computation | custom fusion | bytes 4096 | tf_op jit(solution)/shard_map/gather | solution.py:119
  124.5 13.0 %all-to-all-start = ((f32[64,1,512]{2,1,0:T(1,128)}), f32[64,1,512]{2,1,0:T(1,128)S(1)}, u32[]{:S(2)}, u32[]{:S(2)}) async-start(f32[64,1,512]{2,1,0:T(1,128)} %broadcast_in_dim.100), calls=%async_computation | async-start | bytes 262144 | tf_op jit(solution)/shard_map/all_to_all | solution.py:23
  140.1 7.8 %all-to-all-done = f32[64,1,512]{2,1,0:T(1,128)S(1)} async-done(((f32[64,1,512]{2,1,0:T(1,128)}), f32[64,1,512]{2,1,0:T(1,128)S(1)}, u32[]{:S(2)}, u32[]{:S(2)}) %all-to-all-start) | async-done | bytes 131104 | tf_op jit(solution)/shard_map/all_to_all | solution.py:23
  (99 shorter events, 32.0 us)
Async XLA Ops:
  7.2 131.0 %copy-start = (f32[256]{0:T(256)S(1)}, f32[256]{0:T(256)}, u32[]{:S(2)}) copy-start(f32[256]{0:T(256)} %param.12) | copy-start | bytes 3076
  8.0 10.0 %collective-permute-start.12 = (s32[2,4,1,32]{3,1,0,2:T(4,128)S(1)}, s32[2,4,1,32]{3,1,0,2:T(4,128)S(1)}, u32[]{:S(2)}, u32[]{:S(2)}) collective-permute-start(s32[2,4,1,32]{3,1,0,2:T(4,128)S(1)} %reverse_select_fusion), channel_id=1, source_target_pairs={{0,1},{1,2},{2,3},{3,0},{4,5},{5,6},{6,7},{7,4},{8,9},{9,10},{10,1... | collective-permute-start | bytes 3080 | tf_op jit(solution)/shard_map/ppermute | solution.py:19
  10.1 7.9 %collective-permute-start.13 = (s32[2,4,1,32]{3,1,0,2:T(4,128)S(1)}, s32[2,4,1,32]{3,1,0,2:T(4,128)S(1)}, u32[]{:S(2)}, u32[]{:S(2)}) collective-permute-start(s32[2,4,1,32]{3,1,0,2:T(4,128)S(1)} %reverse_select_fusion), channel_id=1, source_target_pairs={{0,2},{1,3},{2,0},{3,1},{4,6},{5,7},{6,4},{7,5},{8,10},{9,11},{10,... | collective-permute-start | bytes 3080 | tf_op jit(solution)/shard_map/ppermute | solution.py:19
  12.7 5.3 %collective-permute-start.14 = (s32[2,4,1,32]{3,1,0,2:T(4,128)S(1)}, s32[2,4,1,32]{3,1,0,2:T(4,128)S(1)}, u32[]{:S(2)}, u32[]{:S(2)}) collective-permute-start(s32[2,4,1,32]{3,1,0,2:T(4,128)S(1)} %reverse_select_fusion), channel_id=1, source_target_pairs={{0,3},{1,0},{2,1},{3,2},{4,7},{5,4},{6,5},{7,6},{8,11},{9,8},{10,9... | collective-permute-start | bytes 3080 | tf_op jit(solution)/shard_map/ppermute | solution.py:19
  15.0 18.6 %collective-permute-start.2 = (bf16[128,1152]{1,0:T(8,128)(2,1)S(1)}, bf16[128,1152]{1,0:T(8,128)(2,1)S(1)}, u32[]{:S(2)}, u32[]{:S(2)}) collective-permute-start(bf16[128,1152]{1,0:T(8,128)(2,1)S(1)} %get-tuple-element.14), channel_id=1, source_target_pairs={{0,2},{1,3},{2,0},{3,1},{4,6},{5,7},{6,4},{7,5},{8,10},{9,11},{10,... | collective-permute-start | bytes 884744 | tf_op jit(solution)/shard_map/ppermute | solution.py:19
  15.3 18.3 %collective-permute-start = (bf16[128,1152]{1,0:T(8,128)(2,1)S(1)}, bf16[128,1152]{1,0:T(8,128)(2,1)S(1)}, u32[]{:S(2)}, u32[]{:S(2)}) collective-permute-start(bf16[128,1152]{1,0:T(8,128)(2,1)S(1)} %get-tuple-element.12), channel_id=1, source_target_pairs={{0,3},{1,0},{2,1},{3,2},{4,7},{5,4},{6,5},{7,6},{8,11},{9,8},{10,9... | collective-permute-start | bytes 884744 | tf_op jit(solution)/shard_map/ppermute | solution.py:19
  17.9 16.2 %collective-permute-start.6 = (bf16[128,1152]{1,0:T(8,128)(2,1)S(1)}, bf16[128,1152]{1,0:T(8,128)(2,1)S(1)}, u32[]{:S(2)}, u32[]{:S(2)}) collective-permute-start(bf16[128,1152]{1,0:T(8,128)(2,1)S(1)} %get-tuple-element.13), channel_id=1, source_target_pairs={{0,1},{1,2},{2,3},{3,0},{4,5},{5,6},{6,7},{7,4},{8,9},{9,10},{10,1... | collective-permute-start | bytes 884744 | tf_op jit(solution)/shard_map/ppermute | solution.py:19
  24.8 9.6 %collective-permute-start.15 = (bf16[512,1152]{1,0:T(8,128)(2,1)}, bf16[512,1152]{1,0:T(8,128)(2,1)}, u32[]{:S(2)}, u32[]{:S(2)}) collective-permute-start(bf16[512,1152]{1,0:T(8,128)(2,1)} %fusion.5), channel_id=1, source_target_pairs={{0,4},{4,0},{1,5},{5,1},{2,6},{6,2},{3,7},{7,3},{8,12},{12,8},{9,1... | collective-permute-start | bytes 3538952 | tf_op jit(solution)/shard_map/ppermute | solution.py:19
  33.6 11.0 %collective-permute-start.3 = (bf16[128,1152]{1,0:T(8,128)(2,1)S(1)}, bf16[128,1152]{1,0:T(8,128)(2,1)S(1)}, u32[]{:S(2)}, u32[]{:S(2)}) collective-permute-start(bf16[128,1152]{1,0:T(8,128)(2,1)S(1)} %collective-permute-done.2), channel_id=1, source_target_pairs={{0,4},{4,0},{1,5},{5,1},{2,6},{6,2},{3,7},{7,3},{8,12},{12,8},{9,1... | collective-permute-start | bytes 884744 | tf_op jit(solution)/shard_map/ppermute | solution.py:19
  33.6 50.4 %collective-permute-start.1 = (bf16[128,1152]{1,0:T(8,128)(2,1)S(1)}, bf16[128,1152]{1,0:T(8,128)(2,1)}, u32[]{:S(2)}, u32[]{:S(2)}) collective-permute-start(bf16[128,1152]{1,0:T(8,128)(2,1)S(1)} %collective-permute-done), channel_id=1, source_target_pairs={{0,4},{4,0},{1,5},{5,1},{2,6},{6,2},{3,7},{7,3},{8,12},{12,8},{9,1... | collective-permute-start | bytes 884744 | tf_op jit(solution)/shard_map/ppermute | solution.py:19
  34.1 14.2 %collective-permute-start.7 = (bf16[128,1152]{1,0:T(8,128)(2,1)S(1)}, bf16[128,1152]{1,0:T(8,128)(2,1)}, u32[]{:S(2)}, u32[]{:S(2)}) collective-permute-start(bf16[128,1152]{1,0:T(8,128)(2,1)S(1)} %collective-permute-done.6), channel_id=1, source_target_pairs={{0,4},{4,0},{1,5},{5,1},{2,6},{6,2},{3,7},{7,3},{8,12},{12,8},{9,1... | collective-permute-start | bytes 884744 | tf_op jit(solution)/shard_map/ppermute | solution.py:19
  41.0 19.8 %all-to-all-start.1 = ((bf16[4,128,1152]{2,1,0:T(8,128)(2,1)}), bf16[4,128,1152]{2,1,0:T(8,128)(2,1)S(1)}, u32[]{:S(2)}, u32[]{:S(2)}) async-start(bf16[4,128,1152]{2,1,0:T(8,128)(2,1)} %bitcast.4), calls=%async_computation.1 | async-start | bytes 2359296 | tf_op jit(solution)/shard_map/all_to_all | solution.py:23
  48.3 49.9 %collective-permute-start.4 = (bf16[256,1024]{1,0:T(8,128)(2,1)}, bf16[256,1024]{1,0:T(8,128)(2,1)}, u32[]{:S(2)}, u32[]{:S(2)}) collective-permute-start(bf16[256,1024]{1,0:T(8,128)(2,1)} %fusion.28), channel_id=1, source_target_pairs={{0,1},{1,2},{2,3},{3,0},{4,5},{5,6},{6,7},{7,4},{8,9},{9,10},{10,1... | collective-permute-start | bytes 1572872 | tf_op jit(solution)/shard_map/ppermute | solution.py:19
  61.8 9.9 %all-to-all-start.2 = ((bf16[4,32,1152]{2,1,0:T(8,128)(2,1)}), bf16[4,32,1152]{2,1,0:T(8,128)(2,1)}, u32[]{:S(2)}, u32[]{:S(2)}) async-start(bf16[4,32,1152]{2,1,0:T(8,128)(2,1)} %bitcast.5), calls=%async_computation.2 | async-start | bytes 589824 | tf_op jit(solution)/shard_map/all_to_all | solution.py:23
  71.7 17.6 %all-to-all-start.3 = ((bf16[8,16,1152]{2,1,0:T(8,128)(2,1)}), bf16[8,16,1152]{2,1,0:T(8,128)(2,1)S(1)}, u32[]{:S(2)}, u32[]{:S(2)}) async-start(bf16[8,16,1152]{2,1,0:T(8,128)(2,1)} %bitcast.6), calls=%async_computation.3 | async-start | bytes 589824 | tf_op jit(solution)/shard_map/all_to_all | solution.py:23
  83.0 27.2 %collective-permute-start.8 = (bf16[256,1024]{1,0:T(8,128)(2,1)}, bf16[256,1024]{1,0:T(8,128)(2,1)S(1)}, u32[]{:S(2)}, u32[]{:S(2)}) collective-permute-start(bf16[256,1024]{1,0:T(8,128)(2,1)} %fusion.31), channel_id=1, source_target_pairs={{0,3},{1,0},{2,1},{3,2},{4,7},{5,4},{6,5},{7,6},{8,11},{9,8},{10,9... | collective-permute-start | bytes 1572872 | tf_op jit(solution)/shard_map/ppermute | solution.py:19
  84.0 20.9 %collective-permute-start.10 = (bf16[256,1024]{1,0:T(8,128)(2,1)}, bf16[256,1024]{1,0:T(8,128)(2,1)}, u32[]{:S(2)}, u32[]{:S(2)}) collective-permute-start(bf16[256,1024]{1,0:T(8,128)(2,1)} %fusion.37), channel_id=1, source_target_pairs={{0,3},{1,0},{2,1},{3,2},{4,7},{5,4},{6,5},{7,6},{8,11},{9,8},{10,9... | collective-permute-start | bytes 1572872 | tf_op jit(solution)/shard_map/ppermute | solution.py:19
  90.1 13.1 %all-to-all-start.4 = ((bf16[8,16,1152]{2,1,0:T(8,128)(2,1)}), bf16[8,16,1152]{2,1,0:T(8,128)(2,1)S(1)}, u32[]{:S(2)}, u32[]{:S(2)}) async-start(bf16[8,16,1152]{2,1,0:T(8,128)(2,1)} %broadcast_in_dim.114), calls=%async_computation.4 | async-start | bytes 589824 | tf_op jit(solution)/shard_map/all_to_all | solution.py:23
  93.6 44.0 %all-gather.2.cloned.1.call-start = ((), (), s32[]{:S(2)}) async-start(), calls=%async_computation.5 | async-start | bytes 1474560 | tf_op jit(solution)/shard_map/all_gather | solution.py:59
  97.1 23.3 %collective-permute-start.9 = (bf16[256,1024]{1,0:T(8,128)(2,1)}, bf16[256,1024]{1,0:T(8,128)(2,1)S(1)}, u32[]{:S(2)}, u32[]{:S(2)}) collective-permute-start(bf16[256,1024]{1,0:T(8,128)(2,1)} %fusion.34), channel_id=1, source_target_pairs={{0,1},{1,2},{2,3},{3,0},{4,5},{5,6},{6,7},{7,4},{8,9},{9,10},{10,1... | collective-permute-start | bytes 1572872 | tf_op jit(solution)/shard_map/ppermute | solution.py:19
  101.6 17.6 %collective-permute-start.5 = (bf16[256,1024]{1,0:T(8,128)(2,1)}, bf16[256,1024]{1,0:T(8,128)(2,1)}, u32[]{:S(2)}, u32[]{:S(2)}) collective-permute-start(bf16[256,1024]{1,0:T(8,128)(2,1)} %add_convert_fusion.1), channel_id=1, source_target_pairs={{0,1},{1,2},{2,3},{3,0},{4,5},{5,6},{6,7},{7,4},{8,9},{9,10},{10,1... | collective-permute-start | bytes 1572872 | tf_op jit(solution)/shard_map/ppermute | solution.py:19
  107.5 13.0 %collective-permute-start.11 = (bf16[256,1024]{1,0:T(8,128)(2,1)S(1)}, bf16[256,1024]{1,0:T(8,128)(2,1)S(1)}, u32[]{:S(2)}, u32[]{:S(2)}) collective-permute-start(bf16[256,1024]{1,0:T(8,128)(2,1)S(1)} %add_convert_fusion), channel_id=1, source_target_pairs={{0,3},{1,0},{2,1},{3,2},{4,7},{5,4},{6,5},{7,6},{8,11},{9,8},{10,9... | collective-permute-start | bytes 1572872 | tf_op jit(solution)/shard_map/ppermute | solution.py:19
  124.5 23.4 %all-to-all-start = ((f32[64,1,512]{2,1,0:T(1,128)}), f32[64,1,512]{2,1,0:T(1,128)S(1)}, u32[]{:S(2)}, u32[]{:S(2)}) async-start(f32[64,1,512]{2,1,0:T(1,128)} %broadcast_in_dim.100), calls=%async_computation | async-start | bytes 262144 | tf_op jit(solution)/shard_map/all_to_all | solution.py:23
  137.6 14.5 %collective-permute-start.16 = (bf16[4,4,32,1152]{3,2,1,0:T(8,128)(2,1)}, bf16[4,4,32,1152]{3,2,1,0:T(8,128)(2,1)S(1)}, u32[]{:S(2)}, u32[]{:S(2)}) collective-permute-start(bf16[4,4,32,1152]{3,2,1,0:T(8,128)(2,1)} %all-gather.2.cloned.1.call-done), channel_id=1, source_target_pairs={{0,4},{4,0},{1,5},{5,1},{2,6},{6,2},{3,7},{7,3},{8,12},{12,8},{9,1... | collective-permute-start | bytes 3538952 | tf_op jit(solution)/shard_map/ppermute | solution.py:19
  (13 other events, 102.4 us)
Sparse Core Ops, SparseCore 0:
  104.1 27.9 all-gather.1

commit v2 on v0

v2 whole, which is shorter than its diff:
```python
import math

import jax
import jax.numpy as jnp
from jax import lax
from jax.experimental import pallas as pl
from jax.experimental.pallas import tpu as pltpu
from jax.sharding import Mesh, PartitionSpec as P

BEAMS = 8

soft_cap = 30.0
length_power = 0.6
norm_eps = 1e-06

VOC = ("x", "z", "c")
NX, NZ, NC, NY = 4, 8, 2, 4
BLOCK = 256
CHUNK = 512
LANES = 128
VMEM = 36 * 1024 * 1024


def shift(value, axis, size, step):
    return lax.ppermute(value, axis, [(i, (i + step) % size) for i in range(size)])


def exchange(value, axes):
    return lax.all_to_all(value, axes, 0, 0, tiled=True)


def dot_nt(left, right):
    return lax.dot_general(left, right, (((1,), (1,)), ((), ())), preferred_element_type=jnp.float32)


def call(body, outs, args, after=(), smem=0, far_args=0, scratch=()):
    def whole(*refs):
        count = len(args) + len(after)
        tick = refs[count + len(outs)]
        tick[...] = jnp.zeros(tick.shape, tick.dtype)
        body(*refs[: len(args)], *refs[count : count + len(outs)], *refs[count + len(outs) + 1 :])

    spaces = [pltpu.SMEM] * smem + [pltpu.HBM] * far_args
    spaces += [pltpu.VMEM] * (len(args) - len(spaces)) + [pl.ANY] * len(after)
    args = [
        pltpu.with_memory_space_constraint(arg, pltpu.HBM) if space is pltpu.HBM else arg
        for arg, space in zip(args, spaces)
    ]
    out_specs = []
    for out in outs:
        inside = isinstance(out, jax.ShapeDtypeStruct)
        out_specs.append(pl.BlockSpec(memory_space=pltpu.VMEM if inside else pltpu.HBM))
    return pl.pallas_call(
        whole,
        out_shape=list(outs) + [jax.ShapeDtypeStruct((8, LANES), jnp.float32)],
        in_specs=[pl.BlockSpec(memory_space=space) for space in spaces],
        out_specs=out_specs + [pl.BlockSpec(memory_space=pltpu.VMEM)],
        scratch_shapes=list(scratch),
        cost_estimate=pl.CostEstimate(flops=0, bytes_accessed=0, transcendentals=0),
        compiler_params=pltpu.CompilerParams(vmem_limit_bytes=VMEM),
    )(*args, *after)


def like(shape, dtype=jnp.bfloat16):
    return jax.ShapeDtypeStruct(shape, dtype)


def start_all(copies):
    for copy in copies:
        copy.start()
    return copies


def piece_of(hidden_ref, half, quarter):
    rows, width = hidden_ref.shape
    count, depth = rows // NC, width // NY
    return hidden_ref.at[
        pl.ds(pl.multiple_of(half * count, count), count),
        pl.ds(pl.multiple_of(quarter * depth, LANES), depth),
    ]


def gained(features, gain_ref, quarter):
    depth = features.shape[1]
    gain = gain_ref[:, pl.ds(pl.multiple_of(quarter * depth, LANES), depth)]
    return (features.astype(jnp.float32) * gain.astype(jnp.float32)).astype(features.dtype)


def cut_pieces(place, hidden, gain, after):
    rows, width = hidden.shape
    shape = (NY, rows // NC, width // NY)

    def body(place_ref, hidden_ref, gain_ref, out, held, sems):
        copies = start_all(
            [
                pltpu.make_async_copy(piece_of(hidden_ref, place_ref[0], n), held.at[n], sems.at[n])
                for n in range(NY)
            ]
        )
        for n in range(NY):
            copies[n].wait()
            out[n] = gained(held[n], gain_ref, n)

    return call(
        body, [like(shape)], [place, hidden, gain], after, smem=1, far_args=1,
        scratch=[pltpu.VMEM(shape, hidden.dtype), pltpu.SemaphoreType.DMA((NY,))],
    )


def pick_rows(cols, table, scale, after):
    voc_rows, depth = table.shape
    steps = voc_rows // CHUNK
    count = cols.shape[0] // NC
    blocks = 1
    block = count // blocks

    def body(table_ref, col_ref, sent, kept, held, found, sems):
        load = start_all(
            [
                pltpu.make_async_copy(
                    table_ref.at[n * CHUNK : (n + 1) * CHUNK], held.at[n * CHUNK : (n + 1) * CHUNK], sems.at[n]
                )
                for n in range(steps)
            ]
        )
        put = []
        for n in range(NC * blocks):
            ids = lax.broadcasted_iota(jnp.int32, (block, voc_rows), 1)
            at = (n + blocks) % (NC * blocks) * block
            hot = jnp.where(ids == col_ref[at : at + block], 1.0, 0.0).astype(held.dtype)
            if n == 0:
                for copy in load:
                    copy.wait()
            picked = jnp.dot(hot, held[...], preferred_element_type=jnp.float32)
            found[n] = (picked * scale).astype(found.dtype)
            out = (sent, kept)[n // blocks].at[n % blocks * block : (n % blocks + 1) * block]
            put.append(pltpu.make_async_copy(found.at[n], out, sems.at[steps + n]))
            put[-1].start()
        for copy in put:
            copy.wait()

    return call(
        body, [pltpu.HBM((count, depth), table.dtype)] * 2, [table, cols], after, far_args=1,
        scratch=[
            pltpu.VMEM((voc_rows, depth), table.dtype),
            pltpu.VMEM((NC * blocks, block, depth), table.dtype),
            pltpu.SemaphoreType.DMA((steps + NC * blocks,)),
        ],
    )


def products(place, mine, other, table, after):
    half, depth = mine.shape[1:]
    voc_rows = table.shape[0]
    steps = voc_rows // CHUNK
    rows = NC * half
    distances = (2, 1, 3, 0)

    def body(place_ref, mine_ref, other_ref, table_ref, *refs):
        outs = refs[: NY + 1]
        feats, held, results, sems = refs[NY + 1 :]
        get = []
        for n, distance in enumerate(distances):
            plane = lax.rem(place_ref[1] + distance, NY)
            for k, ref in enumerate((mine_ref, other_ref)):
                start = n * rows + k * half
                get.append(
                    pltpu.make_async_copy(ref.at[plane], feats.at[start : start + half], sems.at[0, NC * n + k])
                )
        load = [
            pltpu.make_async_copy(table_ref.at[n * CHUNK : (n + 1) * CHUNK], held.at[n], sems.at[1, n])
            for n in range(steps)
        ]
        start_all(get + load)
        put = []
        for step in range(steps):
            load[step].wait()
            if step == 0:
                for copy in get:
                    copy.wait()
            found = jnp.dot(feats[...], held[step].T, preferred_element_type=jnp.float32)
            results[step] = found.astype(results.dtype)
            for n in range(NY):
                if n == 0:
                    at = step % (steps // 2) * CHUNK
                    out = outs[step // (steps // 2)].at[:, at : at + CHUNK]
                else:
                    out = outs[n + 1].at[:, step * CHUNK : (step + 1) * CHUNK]
                piece = results.at[step, n * rows : (n + 1) * rows]
                put.append(pltpu.make_async_copy(piece, out, sems.at[2 + n, step]))
                put[-1].start()
        for copy in put:
            copy.wait()

    kind = table.dtype
    return call(
        body,
        [pltpu.HBM((rows, voc_rows // 2), kind)] * 2 + [pltpu.HBM((rows, voc_rows), kind)] * 3,
        [place, mine, other, table], after, smem=1, far_args=3,
        scratch=[
            pltpu.VMEM((NY * rows, depth), kind),
            pltpu.VMEM((steps, CHUNK, depth), kind),
            pltpu.VMEM((steps, NY * rows, CHUNK), kind),
            pltpu.SemaphoreType.DMA((2 + NY, 2 * NY)),
        ],
    )


def add_halves(ahead, behind, far_a, far_b, after):
    rows, voc_rows = ahead.shape
    wide = voc_rows // 2
    part = rows // NC

    def body(ahead_ref, behind_ref, a_ref, b_ref, left, right, held, sems):
        sides = ((ahead_ref, a_ref, left, 0), (behind_ref, b_ref, right, wide))
        load, put = [], []
        for n, (near, far, out, start) in enumerate(sides):
            for k in range(NC):
                at = slice(k * part, (k + 1) * part)
                load.append(
                    [
                        pltpu.make_async_copy(near.at[at], held.at[n, at], sems.at[n, k]),
                        pltpu.make_async_copy(far.at[at], held.at[2, at, start : start + wide], sems.at[2 + n, k]),
                    ]
                )
                put.append(pltpu.make_async_copy(held.at[n, at], out.at[at], sems.at[4 + n, k]))
        for pair in load:
            start_all(pair)
        for m, pair in enumerate(load):
            n, k = divmod(m, NC)
            for copy in pair:
                copy.wait()
            at, cols = slice(k * part, (k + 1) * part), slice(n * wide, (n + 1) * wide)
            total = held[n, at, cols].astype(jnp.float32) + held[2, at, cols].astype(jnp.float32)
            held[n, at, cols] = total.astype(held.dtype)
            put[m].start()
        for copy in put:
            copy.wait()

    return call(
        body, [pltpu.HBM(ahead.shape, ahead.dtype)] * 2, [ahead, behind, far_a, far_b], after, far_args=4,
        scratch=[pltpu.VMEM((3, rows, voc_rows), ahead.dtype), pltpu.SemaphoreType.DMA((6, NC))],
    )


def cap_and_sum(place, own, left, right, row_scale, cols, parents, after):
    rows, voc_rows = own.shape
    half = rows // NC
    peers = NX * NZ * NC
    wide = voc_rows // 2

    def body(
        place_ref, own_ref, left_ref, right_ref, scale_ref, col_ref, par_ref, capped_ref, stats_ref,
        held, sems,
    ):
        load = [
            [
                [
                    pltpu.make_async_copy(
                        ref.at[turn * half : (turn + 1) * half, side * wide : (side + 1) * wide],
                        held.at[turn, side, n],
                        sems.at[turn, side, n],
                    )
                    for n, ref in enumerate((own_ref, left_ref, right_ref))
                ]
                for side in range(2)
            ]
            for turn in range(NC)
        ]
        for turn in range(NC):
            for side in range(2):
                start_all(load[turn][side])
        lane = lax.broadcasted_iota(jnp.int32, (half, LANES), 1)
        for turn in range(NC):
            natural = place_ref[0] if turn == 0 else 1 - place_ref[0]
            here = pl.ds(pl.multiple_of(natural * half, half), half)
            scale, col, pick = (
                jnp.broadcast_to(ref[:, here].astype(jnp.float32), (LANES, half)).T
                for ref in (scale_ref, col_ref, par_ref)
            )
            col, pick = col.astype(jnp.int32), pick.astype(jnp.int32)
            total = jnp.zeros((half, LANES), jnp.float32)
            chosen = jnp.zeros((half, LANES), jnp.float32)
            for start in range(0, voc_rows, LANES):
                side = start // wide
                if start % wide == 0:
                    for copy in load[turn][side]:
                        copy.wait()
                at = slice(start % wide, start % wide + LANES)
                logit = sum(held[turn, side, n, :, at].astype(jnp.float32) for n in range(3))
                capped = soft_cap * jnp.tanh(logit * scale / soft_cap)
                capped_ref[here, start : start + LANES] = capped
                total += jnp.exp(capped)
                moved = jnp.concatenate(
                    [
                        jnp.take_along_axis(capped[g : g + BEAMS], pick[g : g + BEAMS], axis=0)
                        for g in range(0, half, BEAMS)
                    ],
                    axis=0,
                )
                chosen += jnp.where(lane + start == col, moved, 0.0)
            for n, part in enumerate((total, chosen)):
                row = jnp.sum(part.T, axis=0, keepdims=True)
                at = pl.ds(pl.multiple_of(n * rows + natural * half, LANES), half)
                stats_ref[:, at] = jnp.broadcast_to(row, (peers, half))

    return call(
        body, [like((rows, voc_rows), jnp.float32), like((peers, 2 * rows), jnp.float32)],
        [place, own, left, right, row_scale, cols, parents], after, smem=1, far_args=3,
        scratch=[pltpu.VMEM((NC, 2, 3, half, wide), own.dtype), pltpu.SemaphoreType.DMA((NC, 2, 3))],
    )


def score(stats, parents, prev_scores, penalty, filler):
    rows = parents.shape[1]

    def body(stats_ref, par_ref, prev_ref, pen_ref, column, chosen_ref, norm_ref, fill):
        fill[...] = jnp.zeros(fill.shape, fill.dtype)
        sums = jnp.sum(stats_ref[...], axis=0, keepdims=True)
        lse = jnp.log(sums[:, :rows])
        sub = lax.broadcasted_iota(jnp.int32, (LANES, LANES), 0)
        lane = lax.broadcasted_iota(jnp.int32, (1, LANES), 1)
        for h in range(rows // LANES):
            at = slice(h * LANES, (h + 1) * LANES)

            def down(row):
                return jnp.broadcast_to(row, (LANES, LANES)).T

            lse_col = down(lse[:, at])
            column[at] = lse_col
            hit = sub == lane // BEAMS * BEAMS + par_ref[:, at]
            lse_par = jnp.sum(jnp.where(hit, lse_col, 0.0), axis=0, keepdims=True)
            prev_par = jnp.sum(jnp.where(hit, down(prev_ref[:, at]), 0.0), axis=0, keepdims=True)
            chosen = sums[:, rows + h * LANES : rows + (h + 1) * LANES] - lse_par
            chosen_ref[:, at] = chosen
            norm_ref[:, at] = (prev_par + chosen) / pen_ref[:, at]

    row = like((1, rows), jnp.float32)
    return call(
        body, [like((rows, LANES), jnp.float32), row, row, like(filler)],
        [stats, parents, prev_scores, penalty],
    )


def subtract(capped, column):
    rows, voc_rows = capped.shape
    steps = 4

    def body(capped_ref, column_ref, log_ref):
        for start in range(0, voc_rows, LANES):
            at = slice(start, start + LANES)
            log_ref[:, at] = capped_ref[:, at] - column_ref[...]

    block = pl.BlockSpec((rows // steps, voc_rows), lambda i: (i, 0))
    return pl.pallas_call(
        body,
        out_shape=like((rows, voc_rows), jnp.float32),
        grid=(steps,),
        in_specs=[block, pl.BlockSpec((rows // steps, LANES), lambda i: (i, 0))],
        out_specs=block,
        cost_estimate=pl.CostEstimate(flops=0, bytes_accessed=0, transcendentals=0),
        compiler_params=pltpu.CompilerParams(vmem_limit_bytes=VMEM),
    )(capped, column)


def add(one, two, after):
    count, depth = one.shape
    cuts = [slice(start, start + LANES) for start in range(0, count, LANES)]

    def body(one_ref, two_ref, out, held, total, sems):
        load = [
            [
                pltpu.make_async_copy(ref.at[at], held.at[k, at], sems.at[k, n])
                for k, ref in enumerate((one_ref, two_ref))
            ]
            for n, at in enumerate(cuts)
        ]
        put = [pltpu.make_async_copy(total.at[at], out.at[at], sems.at[2, n]) for n, at in enumerate(cuts)]
        for pair in load:
            start_all(pair)
        for n, at in enumerate(cuts):
            for copy in load[n]:
                copy.wait()
            total[at] = held[0, at] + held[1, at]
            put[n].start()
        for copy in put:
            copy.wait()

    return call(
        body, [pltpu.HBM(one.shape, one.dtype)], [one, two], after, far_args=2,
        scratch=[
            pltpu.VMEM((2, *one.shape), one.dtype),
            pltpu.VMEM(one.shape, one.dtype),
            pltpu.SemaphoreType.DMA((3, len(cuts))),
        ],
    )


def sum_rows(stacked, copies, after=()):
    terms, rows, depth = stacked.shape

    def body(in_ref, out):
        found = in_ref[0].astype(jnp.float32)
        for n in range(1, terms):
            found = found + in_ref[n].astype(jnp.float32)
        for n in range(copies):
            out[n] = found.astype(stacked.dtype)

    return call(body, [like((copies, rows, depth))], [stacked], after)


def assemble(place, mine, other, after):
    parts = len(mine)
    quarters, part, depth = mine[0].shape

    def body(place_ref, *refs):
        *pieces, out, sems = refs
        copies = []
        for n, ref in enumerate(pieces):
            core = place_ref[0] if n < parts else 1 - place_ref[0]
            x = lax.rem(place_ref[2] + parts - n % parts, parts)
            at = pl.ds(pl.multiple_of((core * parts + x) * part, part), part)
            for q in range(quarters):
                copies.append(
                    pltpu.make_async_copy(
                        ref.at[q], out.at[at, q * depth : (q + 1) * depth], sems.at[n, q]
                    )
                )
        start_all(copies)
        for copy in copies:
            copy.wait()

    return call(
        body, [pltpu.HBM((NC * parts * part, quarters * depth), mine[0].dtype)],
        [place, *mine, *other], after, smem=1,
        scratch=[pltpu.SemaphoreType.DMA((NC * parts, quarters))],
    )


def local(hidden, norm_gain, embed_table, tokens, parents, prev_scores, lengths):
    shard = lax.axis_index(VOC)
    core = lax.axis_index("c")
    y = lax.axis_index("y")
    voc_rows, depth = embed_table.shape
    row_count, width = hidden.shape
    scale = math.sqrt(width)
    place = jnp.stack([core, y, lax.axis_index("x")]).astype(jnp.int32)
    gain = norm_gain.reshape(1, width)
    part = row_count // (NC * NX)

    arrived = jnp.stack([tokens] + [shift(tokens, "y", NY, step) for step in (1, 2, 3)])
    pieces, t_cut = cut_pieces(place, hidden, gain, [arrived])
    mine = exchange(pieces, "y")
    other = shift(mine, "c", NC, 1)
    order = (y - jnp.arange(NY)) % NY
    planes = sum(jnp.where((order == s)[:, None], arrived[s : s + 1], 0) for s in range(NY))
    planes = (planes - shard * voc_rows).reshape(NY, NC, NX, part).transpose(1, 2, 0, 3)
    planes = jnp.where(core == 0, planes, planes[::-1]).reshape(NC * NX * NY * part, 1)

    sent, kept, t_pick = pick_rows(planes, embed_table, scale, [t_cut])
    got = shift(sent, "c", NC, 1)
    found, t_found = add(kept, got, [t_pick])
    found = exchange(found.reshape(NX * NY, part, depth), ("x", "y"))
    far_a, far_b, ahead, behind, own, t_far = products(place, mine, other, embed_table, [t_found])
    far_a = shift(far_a, "y", NY, 1)
    far_b = shift(far_b, "y", NY, 3)
    found, _ = sum_rows(found.reshape(NX, NY * part, depth), 1)
    left, right, t_near = add_halves(ahead, behind, far_a, far_b, [])
    left = shift(left, "y", NY, 1)
    right = shift(right, "y", NY, 3)

    found = exchange(found.reshape(NZ, NY * part // NZ, depth), "z")
    spread, t_z = sum_rows(found, NZ)
    spread = exchange(spread, "z").reshape(NY, part, depth)

    states = hidden.astype(jnp.float32)
    meansq = jnp.mean(states * states, axis=-1)
    row_scale = lax.rsqrt(meansq + norm_eps)
    local_col = tokens - shard * voc_rows
    capped, stats, t_cap = cap_and_sum(
        place, own, left, right, row_scale[None], local_col[None], parents[None], [spread]
    )
    stats = exchange(stats, VOC)
    penalty = jnp.power((5.0 + lengths.astype(jnp.float32)) / 6.0, length_power)
    column, chosen_lp, normalized, filler, _ = score(
        stats, parents[None], prev_scores[None], penalty[None], (row_count, voc_rows // 4)
    )
    log_probs = subtract(capped, column)
    late = [shift(array, "c", NC, 1) for array in (left, right)]
    late.append(shift(filler, "c", NC, 1))
    parts = [spread] + [shift(spread, "x", NX, step) for step in (1, 2, 3)]
    next_embed, _ = assemble(place, parts, [shift(piece, "c", NC, 1) for piece in parts], late)
    return (log_probs, chosen_lp[0], normalized[0], next_embed)


def solution(mesh):
    split = Mesh(mesh.devices.reshape(NX, NZ, NC, NY), VOC + ("y",))
    placed = (P("y", None), P(), P(VOC, "y"), P("y"), P("y"), P("y"), P("y"))
    return jax.shard_map(
        local,
        mesh=split,
        in_specs=placed,
        out_specs=(P("y", VOC), P("y"), P("y"), P("y", None)),
        check_vma=False,
    )
```

time: 443 us -> 143 us (0.32)
  waiting for transfers between devices: 212 us -> 21.1 us
  blocking collectives: 156 us -> 18.6 us
  starting transfers between devices: 9.32 us -> 50.8 us
  Pallas kernels: 0 us -> 39.7 us
  local copies, waits for them, and re-layouts: 22.5 us -> 7.68 us
  between operations: 15.6 us -> 1.07 us
  other arithmetic: 16.7 us -> 3.11 us
  matrix products: 9.56 us -> 0 us
    psum x1 -> x0, waiting for transfers between devices: 187 us -> none  [spread(): total = lax.psum(terms, 'vocab')]
    psum x1 -> x0, blocking collectives: 127 us -> none  [local(): total_exp, chosen_logit = lax.psum((sum_exp, chosen_local), 'vocab')]
    pallas_call x0 -> x11, Pallas kernels: none -> 39.7 us  [the longest x10 37.8 us: call(): pl.pallas_call(whole, out_shape=list(outs) + [jax.ShapeDtypeStruct((8, LA...]
    all_gather x1 -> x0, blocking collectives: 29 us -> none  [local(): all_tokens = lax.all_gather(tokens, 'rows', axis=0, tiled=True)]
    ppermute x0 -> x19, starting transfers between devices: none -> 24.5 us  [shift(): lax.ppermute(value, axis, [(i, (i + step) % size) for i in range(size)])]
    all_to_all x0 -> x1, blocking collectives: none -> 18.6 us  [exchange(): return lax.all_to_all(value, axes, 0, 0, tiled=True)]
    all_to_all x2 -> x4, starting transfers between devices: 9.28 us -> 26.4 us  [exchange(): return lax.all_to_all(value, axes, 0, 0, tiled=True)]
    gather x4 -> x0, local copies, waits for them, and re-layouts: 15.6 us -> none  [the longest x1 9.31 us: local(): picked = jnp.take(embed_table, jnp.clip(all_col, 0, voc_rows - 1), axis=0)]
  transfers between devices with their start and end apart: 4 -> 23, of which waited for: 2 -> 8; matrix products, arithmetic and copies ran while one was open for 7% -> 4% of each run, Pallas kernels for 0% -> 23%
where the time goes in v2:
time: 143 us; the launch traced here: 142 us
  starting transfers between devices  50.8 us (36%)
  Pallas kernels  39.7 us (28%)
  waiting for transfers between devices  21.1 us (15%)
  blocking collectives  18.6 us (13%)
  local copies, waits for them, and re-layouts  7.68 us (5%)
  other arithmetic  3.11 us (2%)
    pallas_call x10, Pallas kernels, call(): pl.pallas_call(whole, out_shape=list(outs) + [jax.ShapeDtypeStruct((8, LA...  37.8 us
    all_to_all x4, starting transfers between devices, exchange(): return lax.all_to_all(value, axes, 0, 0, tiled=True)  26.4 us
    ppermute x19, starting transfers between devices, shift(): lax.ppermute(value, axis, [(i, (i + step) % size) for i in range(size)])  24.5 us
    all_to_all x1, blocking collectives, exchange(): return lax.all_to_all(value, axes, 0, 0, tiled=True)  18.6 us
    all_to_all x4, waiting for transfers between devices, exchange(): return lax.all_to_all(value, axes, 0, 0, tiled=True)  13.7 us
    ppermute x19, waiting for transfers between devices, shift(): lax.ppermute(value, axis, [(i, (i + step) % size) for i in range(size)])  7.37 us
    unnamed x23, local copies, waits for them, and re-layouts  4.63 us
  transfers between devices with their start and end apart: 23, of which 8 were waited for; matrix products, arithmetic and copies ran while one was open for 4% of the time, Pallas kernels for 23%

profile of v2, /device:TPU:1, one launch (start us, length us, event | category | flops | bytes accessed | tf_op | source)
XLA Modules:
  0.0 142.0 jit_solution(10165704285334569114)
XLA Ops:
  0.6 3.6 %collective-permute-start.2 = (s32[256]{0:T(256)}, s32[256]{0:T(256)S(1)}, u32[]{:S(2)}, u32[]{:S(2)}) collective-permute-start(s32[256]{0:T(256)} %param.10), channel_id=1, source_target_pairs={{0,3},{1,0},{2,1},{3,2},{4,7},{5,4},{6,5},{7,6},{8,11},{9,8},{10,9... | collective-permute-start | bytes 3080 | tf_op jit(solution)/shard_map/ppermute | solution.py:25
  9.2 2.9 %shard_map.102 = (bf16[4,128,1152]{2,1,0:T(8,128)(2,1)}, f32[8,128]{1,0:T(8,128)S(1)}) custom-call(s32[3]{0:T(128)S(1)} %pad_add_fusion.1.refs_0_, bf16[256,4608]{1,0:T(8,128)(2,1)} %refs_1_.1, bf16[1,4608]{1,0:T(2,128)(2,1)S(1)} %reshape.116.refs_2_, s32[4,256]{1,0:T(4,128)S(1)} %pad_add_fusion.refs_3_), custom_call_target="tpu_custom_call" | custom-call | tf_op jit(solution)/shard_map/pallas_call | solution.py:53
  12.0 3.5 %all-to-all-start = ((bf16[4,128,1152]{2,1,0:T(8,128)(2,1)}), bf16[4,128,1152]{2,1,0:T(8,128)(2,1)S(1)}, u32[]{:S(2)}, u32[]{:S(2)}) async-start(bf16[4,128,1152]{2,1,0:T(8,128)(2,1)} %get-tuple-element.27), calls=%async_computation | async-start | bytes 2359296 | tf_op jit(solution)/shard_map/all_to_all | solution.py:29
  16.5 9.0 %shard_map.103 = (bf16[512,1152]{1,0:T(8,128)(2,1)}, bf16[512,1152]{1,0:T(8,128)(2,1)}, f32[8,128]{1,0:T(8,128)S(1)}) custom-call(bf16[2048,1152]{1,0:T(8,128)(2,1)} %refs_3_.1, s32[1024,1]{1,0:T(8,128)S(1)} %reshape.122.refs_1_, f32[8,128]{1,0:T(8,128)S(1)} %get-tuple-element.28.refs_2_), custom_call_target="tpu_custom_call" | custom-call | tf_op jit(solution)/shard_map/pallas_call | solution.py:53
  25.5 2.5 %collective-permute-start.4 = (bf16[512,1152]{1,0:T(8,128)(2,1)}, bf16[512,1152]{1,0:T(8,128)(2,1)S(1)}, u32[]{:S(2)}, u32[]{:S(2)}) collective-permute-start(bf16[512,1152]{1,0:T(8,128)(2,1)} %get-tuple-element.30), channel_id=1, source_target_pairs={{0,4},{4,0},{1,5},{5,1},{2,6},{6,2},{3,7},{7,3},{8,12},{12,8},{9,1... | collective-permute-start | bytes 3538952 | tf_op jit(solution)/shard_map/ppermute | solution.py:25
  28.0 1.7 %all-to-all-done.refs_1_ = bf16[4,128,1152]{2,1,0:T(8,128)(2,1)S(1)} async-done(((bf16[4,128,1152]{2,1,0:T(8,128)(2,1)}), bf16[4,128,1152]{2,1,0:T(8,128)(2,1)S(1)}, u32[]{:S(2)}, u32[]{:S(2)}) %all-to-all-start) | async-done | bytes 1179680 | tf_op jit(solution)/shard_map/all_to_all | solution.py:29
  29.7 3.3 %collective-permute-start.3 = (bf16[4,128,1152]{2,1,0:T(8,128)(2,1)S(1)}, bf16[4,128,1152]{2,1,0:T(8,128)(2,1)S(1)}, u32[]{:S(2)}, u32[]{:S(2)}) collective-permute-start(bf16[4,128,1152]{2,1,0:T(8,128)(2,1)S(1)} %all-to-all-done.refs_1_), channel_id=1, source_target_pairs={{0,4},{4,0},{1,5},{5,1},{2,6},{6,2},{3,7},{7,3},{8,12},{12,8},{9,1... | collective-permute-start | bytes 3538952 | tf_op jit(solution)/shard_map/ppermute | solution.py:25
  34.0 2.5 %shard_map.104 = (bf16[512,1152]{1,0:T(8,128)(2,1)}, f32[8,128]{1,0:T(8,128)S(1)}) custom-call(bf16[512,1152]{1,0:T(8,128)(2,1)} %get-tuple-element.29.refs_0_, bf16[512,1152]{1,0:T(8,128)(2,1)} %copy-done.6, f32[8,128]{1,0:T(8,128)S(1)} %get-tuple-element.31.refs_2_), custom_call_target="tpu_custom_call" | custom-call | tf_op jit(solution)/shard_map/pallas_call | solution.py:53
  36.5 4.7 %all-to-all-start.1 = ((bf16[16,32,1152]{2,1,0:T(8,128)(2,1)}), bf16[16,32,1152]{2,1,0:T(8,128)(2,1)S(1)}, u32[]{:S(2)}, u32[]{:S(2)}) async-start(bf16[16,32,1152]{2,1,0:T(8,128)(2,1)} %bitcast.37), calls=%async_computation.1 | async-start | bytes 2359296 | tf_op jit(solution)/shard_map/all_to_all | solution.py:29
  42.3 10.8 %shard_map.105 = (bf16[256,1024]{1,0:T(8,128)(2,1)}, bf16[256,1024]{1,0:T(8,128)(2,1)}, bf16[256,2048]{1,0:T(8,128)(2,1)}, bf16[256,2048]{1,0:T(8,128)(2,1)}, bf...) custom-call(s32[3]{0:T(128)S(1)} %pad_add_fusion.1.refs_0_, bf16[4,128,1152]{2,1,0:T(8,128)(2,1)} %copy-done.4, ...), custom_call_target="tpu_custom_call" | custom-call | tf_op jit(solution)/shard_map/pallas_call | solution.py:53
  55.9 2.4 %all-to-all-done.1 = bf16[16,32,1152]{2,1,0:T(8,128)(2,1)S(1)} async-done(((bf16[16,32,1152]{2,1,0:T(8,128)(2,1)}), bf16[16,32,1152]{2,1,0:T(8,128)(2,1)S(1)}, u32[]{:S(2)}, u32[]{:S(2)}) %all-to-all-start.1) | async-done | bytes 1179680 | tf_op jit(solution)/shard_map/all_to_all | solution.py:29
  59.2 8.2 %all-to-all-start.2 = ((bf16[8,16,1152]{2,1,0:T(8,128)(2,1)}), bf16[8,16,1152]{2,1,0:T(8,128)(2,1)S(1)}, u32[]{:S(2)}, u32[]{:S(2)}) async-start(bf16[8,16,1152]{2,1,0:T(8,128)(2,1)} %bitcast.12), calls=%async_computation.2 | async-start | bytes 589824 | tf_op jit(solution)/shard_map/all_to_all | solution.py:29
  67.4 3.3 %collective-permute-done.5.refs_2_ = bf16[256,1024]{1,0:T(8,128)(2,1)S(1)} collective-permute-done((bf16[256,1024]{1,0:T(8,128)(2,1)}, bf16[256,1024]{1,0:T(8,128)(2,1)S(1)}, u32[]{:S(2)}, u32[]{:S(2)}) %collective-permute-start.5) | collective-permute-done | bytes 524320 | tf_op jit(solution)/shard_map/ppermute | solution.py:25
  71.6 3.4 %shard_map.106 = (bf16[256,2048]{1,0:T(8,128)(2,1)}, bf16[256,2048]{1,0:T(8,128)(2,1)}, f32[8,128]{1,0:T(8,128)}) custom-call(bf16[256,2048]{1,0:T(8,128)(2,1)} %get-tuple-element.34.refs_0_, bf16[256,2048]{1,0:T(8,128)(2,1)} %get-tuple-element.35.refs_1_, bf16[256,1024]{1,0:T(8,128)(2,1)} %copy-done.7, bf16[256,1024]{1,0:T(8,128)(2,1)} %copy-done.8), custom_call_target="tpu_custom_call" | custom-call | tf_op jit(solution)/shard_map/pallas_call | solution.py:53
  75.1 2.7 %collective-permute-start.8 = (bf16[256,2048]{1,0:T(8,128)(2,1)}, bf16[256,2048]{1,0:T(8,128)(2,1)}, u32[]{:S(2)}, u32[]{:S(2)}) collective-permute-start(bf16[256,2048]{1,0:T(8,128)(2,1)} %get-tuple-element.39), channel_id=1, source_target_pairs={{0,3},{1,0},{2,1},{3,2},{4,7},{5,4},{6,5},{7,6},{8,11},{9,8},{10,9... | collective-permute-start | bytes 3145736 | tf_op jit(solution)/shard_map/ppermute | solution.py:25
  78.3 18.6 %all_to_all.31 = bf16[8,16,1152]{2,1,0:T(8,128)(2,1)S(1)} all-to-all(bf16[8,16,1152]{2,1,0:T(8,128)(2,1)S(1)} %get-tuple-element.42), channel_id=1, replica_groups=mesh['x'=4,'z'=8,'c'=2,'y'=4] {'z'}, dimensions={0} | all-to-all | bytes 589824 | tf_op jit(solution)/shard_map/all_to_all | solution.py:29
  96.9 2.9 %collective-permute-start.12 = (bf16[4,32,1152]{2,1,0:T(8,128)(2,1)S(1)}, bf16[4,32,1152]{2,1,0:T(8,128)(2,1)S(1)}, u32[]{:S(2)}, u32[]{:S(2)}) collective-permute-start(bf16[4,32,1152]{2,1,0:T(8,128)(2,1)S(1)} %bitcast.23), channel_id=1, source_target_pairs={{0,4},{4,0},{1,5},{5,1},{2,6},{6,2},{3,7},{7,3},{8,12},{12,8},{9,1... | collective-permute-start | bytes 884744 | tf_op jit(solution)/shard_map/ppermute | solution.py:25
  102.2 2.2 %multiply_reduce_fusion = f32[256]{0:T(256)S(1)} fusion(bf16[256,4608]{1,0:T(8,128)(2,1)} %refs_1_.1), kind=kLoop, calls=%fused_computation | loop fusion | flops 3538688 | bytes 2360320 | tf_op jit(solution)/shard_map/reduce_sum | solution.py:477
  106.6 2.0 %collective-permute-done.11.refs_4_ = bf16[4,32,1152]{2,1,0:T(8,128)(2,1)} collective-permute-done((bf16[4,32,1152]{2,1,0:T(8,128)(2,1)S(1)}, bf16[4,32,1152]{2,1,0:T(8,128)(2,1)}, u32[]{:S(2)}, u32[]{:S(2)}) %collective-permute-start.11) | collective-permute-done | bytes 294944 | tf_op jit(solution)/shard_map/ppermute | solution.py:25
  109.8 3.4 %shard_map.109 = (f32[256,2048]{1,0:T(8,128)S(1)}, f32[64,512]{1,0:T(8,128)S(1)}, f32[8,128]{1,0:T(8,128)}) custom-call(s32[3]{0:T(128)S(1)} %pad_add_fusion.1.refs_0_, bf16[256,2048]{1,0:T(8,128)(2,1)} %get-tuple-element.33.refs_1_, bf16[256,2048]{1,0:T(8,128)(2,1)} %collective-permute-done.7.refs_2_, bf16[256,2048]{1,0:T(8,128)(2,1)} %collective-permute-done.8.refs_3_, ...), custom_call_target="tpu_custom_call" | custom-call | tf_op jit(solution)/shard_map/pallas_call | solution.py:53
  113.9 9.9 %all-to-all-start.4 = ((f32[64,1,512]{2,1,0:T(1,128)}), f32[64,1,512]{2,1,0:T(1,128)}, u32[]{:S(2)}, u32[]{:S(2)}) async-start(f32[64,1,512]{2,1,0:T(1,128)} %copy.13), calls=%async_computation.4 | async-start | bytes 262144 | tf_op jit(solution)/shard_map/all_to_all | solution.py:29
  124.6 9.5 %all-to-all-done.4 = f32[64,1,512]{2,1,0:T(1,128)} async-done(((f32[64,1,512]{2,1,0:T(1,128)}), f32[64,1,512]{2,1,0:T(1,128)}, u32[]{:S(2)}, u32[]{:S(2)}) %all-to-all-start.4) | async-done | bytes 131104 | tf_op jit(solution)/shard_map/all_to_all | solution.py:29
  136.2 1.8 %shard_map.111 = f32[256,2048]{1,0:T(8,128)} custom-call(f32[256,2048]{1,0:T(8,128)S(1)} %get-tuple-element.43.capped_ref, f32[256,128]{1,0:T(8,128)S(1)} %get-tuple-element.45.column_ref), custom_call_target="tpu_custom_call" | custom-call | tf_op jit(solution)/shard_map/pallas_call | solution.py:355
  138.1 3.7 %shard_map.112 = (bf16[256,4608]{1,0:T(8,128)(2,1)}, f32[8,128]{1,0:T(8,128)}) custom-call(s32[3]{0:T(128)S(1)} %pad_add_fusion.1.refs_0_, bf16[4,32,1152]{2,1,0:T(8,128)(2,1)S(1)} %bitcast.28, bf16[4,32,1152]{2,1,0:T(8,128)(2,1)} %collective-permute-done.9.refs_2_, bf16[4,32,1152]{2,1,0:T(8,128)(2,1)} %collective-permute-done.10.refs_3_, ...), custom_call_target="tpu_custom_call" | custom-call | tf_op jit(solution)/shard_map/pallas_call | solution.py:53
  (74 shorter events, 22.3 us)
Async XLA Ops:
  0.6 6.3 %collective-permute-start.2 = (s32[256]{0:T(256)}, s32[256]{0:T(256)S(1)}, u32[]{:S(2)}, u32[]{:S(2)}) collective-permute-start(s32[256]{0:T(256)} %param.10), channel_id=1, source_target_pairs={{0,3},{1,0},{2,1},{3,2},{4,7},{5,4},{6,5},{7,6},{8,11},{9,8},{10,9... | collective-permute-start | bytes 3080 | tf_op jit(solution)/shard_map/ppermute | solution.py:25
  4.3 4.1 %collective-permute-start.1 = (s32[256]{0:T(256)}, s32[256]{0:T(256)S(1)}, u32[]{:S(2)}, u32[]{:S(2)}) collective-permute-start(s32[256]{0:T(256)} %param.10), channel_id=1, source_target_pairs={{0,2},{1,3},{2,0},{3,1},{4,6},{5,7},{6,4},{7,5},{8,10},{9,11},{10,... | collective-permute-start | bytes 3080 | tf_op jit(solution)/shard_map/ppermute | solution.py:25
  4.6 3.8 %collective-permute-start = (s32[256]{0:T(256)}, s32[256]{0:T(256)S(1)}, u32[]{:S(2)}, u32[]{:S(2)}) collective-permute-start(s32[256]{0:T(256)} %param.10), channel_id=1, source_target_pairs={{0,1},{1,2},{2,3},{3,0},{4,5},{5,6},{6,7},{7,4},{8,9},{9,10},{10,1... | collective-permute-start | bytes 3080 | tf_op jit(solution)/shard_map/ppermute | solution.py:25
  12.0 17.7 %all-to-all-start = ((bf16[4,128,1152]{2,1,0:T(8,128)(2,1)}), bf16[4,128,1152]{2,1,0:T(8,128)(2,1)S(1)}, u32[]{:S(2)}, u32[]{:S(2)}) async-start(bf16[4,128,1152]{2,1,0:T(8,128)(2,1)} %get-tuple-element.27), calls=%async_computation | async-start | bytes 2359296 | tf_op jit(solution)/shard_map/all_to_all | solution.py:29
  25.5 7.5 %collective-permute-start.4 = (bf16[512,1152]{1,0:T(8,128)(2,1)}, bf16[512,1152]{1,0:T(8,128)(2,1)S(1)}, u32[]{:S(2)}, u32[]{:S(2)}) collective-permute-start(bf16[512,1152]{1,0:T(8,128)(2,1)} %get-tuple-element.30), channel_id=1, source_target_pairs={{0,4},{4,0},{1,5},{5,1},{2,6},{6,2},{3,7},{7,3},{8,12},{12,8},{9,1... | collective-permute-start | bytes 3538952 | tf_op jit(solution)/shard_map/ppermute | solution.py:25
  29.7 11.6 %collective-permute-start.3 = (bf16[4,128,1152]{2,1,0:T(8,128)(2,1)S(1)}, bf16[4,128,1152]{2,1,0:T(8,128)(2,1)S(1)}, u32[]{:S(2)}, u32[]{:S(2)}) collective-permute-start(bf16[4,128,1152]{2,1,0:T(8,128)(2,1)S(1)} %all-to-all-done.refs_1_), channel_id=1, source_target_pairs={{0,4},{4,0},{1,5},{5,1},{2,6},{6,2},{3,7},{7,3},{8,12},{12,8},{9,1... | collective-permute-start | bytes 3538952 | tf_op jit(solution)/shard_map/ppermute | solution.py:25
  36.5 21.8 %all-to-all-start.1 = ((bf16[16,32,1152]{2,1,0:T(8,128)(2,1)}), bf16[16,32,1152]{2,1,0:T(8,128)(2,1)S(1)}, u32[]{:S(2)}, u32[]{:S(2)}) async-start(bf16[16,32,1152]{2,1,0:T(8,128)(2,1)} %bitcast.37), calls=%async_computation.1 | async-start | bytes 2359296 | tf_op jit(solution)/shard_map/all_to_all | solution.py:29
  53.1 17.5 %collective-permute-start.5 = (bf16[256,1024]{1,0:T(8,128)(2,1)}, bf16[256,1024]{1,0:T(8,128)(2,1)S(1)}, u32[]{:S(2)}, u32[]{:S(2)}) collective-permute-start(bf16[256,1024]{1,0:T(8,128)(2,1)} %get-tuple-element.36), channel_id=1, source_target_pairs={{0,1},{1,2},{2,3},{3,0},{4,5},{5,6},{6,7},{7,4},{8,9},{9,10},{10,1... | collective-permute-start | bytes 1572872 | tf_op jit(solution)/shard_map/ppermute | solution.py:25
  54.5 16.1 %collective-permute-start.6 = (bf16[256,1024]{1,0:T(8,128)(2,1)}, bf16[256,1024]{1,0:T(8,128)(2,1)S(1)}, u32[]{:S(2)}, u32[]{:S(2)}) collective-permute-start(bf16[256,1024]{1,0:T(8,128)(2,1)} %get-tuple-element.37), channel_id=1, source_target_pairs={{0,3},{1,0},{2,1},{3,2},{4,7},{5,4},{6,5},{7,6},{8,11},{9,8},{10,9... | collective-permute-start | bytes 1572872 | tf_op jit(solution)/shard_map/ppermute | solution.py:25
  59.2 18.6 %all-to-all-start.2 = ((bf16[8,16,1152]{2,1,0:T(8,128)(2,1)}), bf16[8,16,1152]{2,1,0:T(8,128)(2,1)S(1)}, u32[]{:S(2)}, u32[]{:S(2)}) async-start(bf16[8,16,1152]{2,1,0:T(8,128)(2,1)} %bitcast.12), calls=%async_computation.2 | async-start | bytes 589824 | tf_op jit(solution)/shard_map/all_to_all | solution.py:29
  75.0 34.8 %copy-start.2 = (s32[256]{0:T(256)S(1)}, s32[256]{0:T(256)}, u32[]{:S(2)}) copy-start(s32[256]{0:T(256)} %param.11) | copy-start | bytes 3076
  75.0 25.9 %collective-permute-start.7 = (bf16[256,2048]{1,0:T(8,128)(2,1)}, bf16[256,2048]{1,0:T(8,128)(2,1)}, u32[]{:S(2)}, u32[]{:S(2)}) collective-permute-start(bf16[256,2048]{1,0:T(8,128)(2,1)} %get-tuple-element.38), channel_id=1, source_target_pairs={{0,1},{1,2},{2,3},{3,0},{4,5},{5,6},{6,7},{7,4},{8,9},{9,10},{10,1... | collective-permute-start | bytes 3145736 | tf_op jit(solution)/shard_map/ppermute | solution.py:25
  75.1 27.1 %collective-permute-start.8 = (bf16[256,2048]{1,0:T(8,128)(2,1)}, bf16[256,2048]{1,0:T(8,128)(2,1)}, u32[]{:S(2)}, u32[]{:S(2)}) collective-permute-start(bf16[256,2048]{1,0:T(8,128)(2,1)} %get-tuple-element.39), channel_id=1, source_target_pairs={{0,3},{1,0},{2,1},{3,2},{4,7},{5,4},{6,5},{7,6},{8,11},{9,8},{10,9... | collective-permute-start | bytes 3145736 | tf_op jit(solution)/shard_map/ppermute | solution.py:25
  96.9 9.0 %collective-permute-start.12 = (bf16[4,32,1152]{2,1,0:T(8,128)(2,1)S(1)}, bf16[4,32,1152]{2,1,0:T(8,128)(2,1)S(1)}, u32[]{:S(2)}, u32[]{:S(2)}) collective-permute-start(bf16[4,32,1152]{2,1,0:T(8,128)(2,1)S(1)} %bitcast.23), channel_id=1, source_target_pairs={{0,4},{4,0},{1,5},{5,1},{2,6},{6,2},{3,7},{7,3},{8,12},{12,8},{9,1... | collective-permute-start | bytes 884744 | tf_op jit(solution)/shard_map/ppermute | solution.py:25
  99.8 8.7 %collective-permute-start.11 = (bf16[4,32,1152]{2,1,0:T(8,128)(2,1)S(1)}, bf16[4,32,1152]{2,1,0:T(8,128)(2,1)}, u32[]{:S(2)}, u32[]{:S(2)}) collective-permute-start(bf16[4,32,1152]{2,1,0:T(8,128)(2,1)S(1)} %bitcast.24), channel_id=1, source_target_pairs={{0,192},{64,0},{128,64},{192,128},{1,193},{65,1},{129,65},{193,129... | collective-permute-start | bytes 884744 | tf_op jit(solution)/shard_map/ppermute | solution.py:25
  100.9 37.2 %collective-permute-start.16 = (bf16[256,2048]{1,0:T(8,128)(2,1)}, bf16[256,2048]{1,0:T(8,128)(2,1)S(1)}, u32[]{:S(2)}, u32[]{:S(2)}) collective-permute-start(bf16[256,2048]{1,0:T(8,128)(2,1)} %collective-permute-done.7.refs_2_), channel_id=1, source_target_pairs={{0,4},{4,0},{1,5},{5,1},{2,6},{6,2},{3,7},{7,3},{8,12},{12,8},{9,1... | collective-permute-start | bytes 3145736 | tf_op jit(solution)/shard_map/ppermute | solution.py:25
  102.2 36.0 %collective-permute-start.17 = (bf16[256,2048]{1,0:T(8,128)(2,1)}, bf16[256,2048]{1,0:T(8,128)(2,1)}, u32[]{:S(2)}, u32[]{:S(2)}) collective-permute-start(bf16[256,2048]{1,0:T(8,128)(2,1)} %collective-permute-done.8.refs_3_), channel_id=1, source_target_pairs={{0,4},{4,0},{1,5},{5,1},{2,6},{6,2},{3,7},{7,3},{8,12},{12,8},{9,1... | collective-permute-start | bytes 3145736 | tf_op jit(solution)/shard_map/ppermute | solution.py:25
  104.4 19.5 %collective-permute-start.10 = (bf16[4,32,1152]{2,1,0:T(8,128)(2,1)S(1)}, bf16[4,32,1152]{2,1,0:T(8,128)(2,1)}, u32[]{:S(2)}, u32[]{:S(2)}) collective-permute-start(bf16[4,32,1152]{2,1,0:T(8,128)(2,1)S(1)} %bitcast.25), channel_id=1, source_target_pairs={{0,128},{64,192},{128,0},{192,64},{1,129},{65,193},{129,1},{193,65... | collective-permute-start | bytes 884744 | tf_op jit(solution)/shard_map/ppermute | solution.py:25
  106.6 17.9 %collective-permute-start.9 = (bf16[4,32,1152]{2,1,0:T(8,128)(2,1)S(1)}, bf16[4,32,1152]{2,1,0:T(8,128)(2,1)}, u32[]{:S(2)}, u32[]{:S(2)}) collective-permute-start(bf16[4,32,1152]{2,1,0:T(8,128)(2,1)S(1)} %bitcast.26), channel_id=1, source_target_pairs={{0,64},{64,128},{128,192},{192,0},{1,65},{65,129},{129,193},{193,1... | collective-permute-start | bytes 884744 | tf_op jit(solution)/shard_map/ppermute | solution.py:25
  108.6 27.3 %collective-permute-start.15 = (bf16[4,32,1152]{2,1,0:T(8,128)(2,1)}, bf16[4,32,1152]{2,1,0:T(8,128)(2,1)}, u32[]{:S(2)}, u32[]{:S(2)}) collective-permute-start(bf16[4,32,1152]{2,1,0:T(8,128)(2,1)} %collective-permute-done.11.refs_4_), channel_id=1, source_target_pairs={{0,4},{4,0},{1,5},{5,1},{2,6},{6,2},{3,7},{7,3},{8,12},{12,8},{9,1... | collective-permute-start | bytes 884744 | tf_op jit(solution)/shard_map/ppermute | solution.py:25
  113.9 20.2 %all-to-all-start.4 = ((f32[64,1,512]{2,1,0:T(1,128)}), f32[64,1,512]{2,1,0:T(1,128)}, u32[]{:S(2)}, u32[]{:S(2)}) async-start(f32[64,1,512]{2,1,0:T(1,128)} %copy.13), calls=%async_computation.4 | async-start | bytes 262144 | tf_op jit(solution)/shard_map/all_to_all | solution.py:29
  123.9 14.2 %collective-permute-start.14 = (bf16[4,32,1152]{2,1,0:T(8,128)(2,1)}, bf16[4,32,1152]{2,1,0:T(8,128)(2,1)}, u32[]{:S(2)}, u32[]{:S(2)}) collective-permute-start(bf16[4,32,1152]{2,1,0:T(8,128)(2,1)} %collective-permute-done.10.refs_3_), channel_id=1, source_target_pairs={{0,4},{4,0},{1,5},{5,1},{2,6},{6,2},{3,7},{7,3},{8,12},{12,8},{9,1... | collective-permute-start | bytes 884744 | tf_op jit(solution)/shard_map/ppermute | solution.py:25
  124.5 13.6 %collective-permute-start.13 = (bf16[4,32,1152]{2,1,0:T(8,128)(2,1)}, bf16[4,32,1152]{2,1,0:T(8,128)(2,1)}, u32[]{:S(2)}, u32[]{:S(2)}) collective-permute-start(bf16[4,32,1152]{2,1,0:T(8,128)(2,1)} %collective-permute-done.9.refs_2_), channel_id=1, source_target_pairs={{0,4},{4,0},{1,5},{5,1},{2,6},{6,2},{3,7},{7,3},{8,12},{12,8},{9,1... | collective-permute-start | bytes 884744 | tf_op jit(solution)/shard_map/ppermute | solution.py:25
  135.8 2.3 %collective-permute-start.18 = (bf16[256,512]{1,0:T(8,128)(2,1)S(1)}, bf16[256,512]{1,0:T(8,128)(2,1)S(1)}, u32[]{:S(2)}, u32[]{:S(2)}) collective-permute-start(bf16[256,512]{1,0:T(8,128)(2,1)S(1)} %get-tuple-element.48), channel_id=1, source_target_pairs={{0,4},{4,0},{1,5},{5,1},{2,6},{6,2},{3,7},{7,3},{8,12},{12,8},{9,1... | collective-permute-start | bytes 786440 | tf_op jit(solution)/shard_map/ppermute | solution.py:25
  (10 other events, 90.3 us)

commit v3 on v2

--- a/solution.py
+++ b/solution.py
@@ -17,6 +17,7 @@
 NX, NZ, NC, NY = 4, 8, 2, 4
 BLOCK = 256
 CHUNK = 512
+SWAP = 512
 LANES = 128
 VMEM = 36 * 1024 * 1024
 
@@ -33,14 +34,14 @@
     return lax.dot_general(left, right, (((1,), (1,)), ((), ())), preferred_element_type=jnp.float32)
 
 
-def call(body, outs, args, after=(), smem=0, far_args=0, scratch=()):
+def call(body, outs, args, after=(), smem=0, far_args=0, any_args=0, scratch=()):
     def whole(*refs):
         count = len(args) + len(after)
         tick = refs[count + len(outs)]
         tick[...] = jnp.zeros(tick.shape, tick.dtype)
         body(*refs[: len(args)], *refs[count : count + len(outs)], *refs[count + len(outs) + 1 :])
 
-    spaces = [pltpu.SMEM] * smem + [pltpu.HBM] * far_args
+    spaces = [pltpu.SMEM] * smem + [pltpu.HBM] * far_args + [pl.ANY] * any_args
     spaces += [pltpu.VMEM] * (len(args) - len(spaces)) + [pl.ANY] * len(after)
     args = [
         pltpu.with_memory_space_constraint(arg, pltpu.HBM) if space is pltpu.HBM else arg
@@ -149,16 +150,20 @@
     )
 
 
-def products(place, mine, other, table, after):
+def products(place, table, mine, other, distances, splits, after):
     half, depth = mine.shape[1:]
     voc_rows = table.shape[0]
     steps = voc_rows // CHUNK
     rows = NC * half
-    distances = (2, 1, 3, 0)
-
-    def body(place_ref, mine_ref, other_ref, table_ref, *refs):
-        outs = refs[: NY + 1]
-        feats, held, results, sems = refs[NY + 1 :]
+    count = len(distances)
+
+    def body(place_ref, table_ref, mine_ref, other_ref, *refs):
+        outs = refs[: sum(splits)]
+        feats, held, results, sems = refs[sum(splits) :]
+        load = [
+            pltpu.make_async_copy(table_ref.at[n * CHUNK : (n + 1) * CHUNK], held.at[n], sems.at[1, n])
+            for n in range(steps)
+        ]
         get = []
         for n, distance in enumerate(distances):
             plane = lax.rem(place_ref[1] + distance, NY)
@@ -167,42 +172,64 @@
                 get.append(
                     pltpu.make_async_copy(ref.at[plane], feats.at[start : start + half], sems.at[0, NC * n + k])
                 )
-        load = [
-            pltpu.make_async_copy(table_ref.at[n * CHUNK : (n + 1) * CHUNK], held.at[n], sems.at[1, n])
-            for n in range(steps)
-        ]
-        start_all(get + load)
+        start_all(load[:1] + get + load[1:])
         put = []
         for step in range(steps):
             load[step].wait()
+            block = held[step].T
             if step == 0:
                 for copy in get:
                     copy.wait()
-            found = jnp.dot(feats[...], held[step].T, preferred_element_type=jnp.float32)
+            found = jnp.dot(feats[...], block, preferred_element_type=jnp.float32)
             results[step] = found.astype(results.dtype)
-            for n in range(NY):
-                if n == 0:
-                    at = step % (steps // 2) * CHUNK
-                    out = outs[step // (steps // 2)].at[:, at : at + CHUNK]
-                else:
-                    out = outs[n + 1].at[:, step * CHUNK : (step + 1) * CHUNK]
+            first = 0
+            for n in range(count):
+                share = steps // splits[n]
+                at = step % share * CHUNK
+                out = outs[first + step // share].at[:, at : at + CHUNK]
                 piece = results.at[step, n * rows : (n + 1) * rows]
                 put.append(pltpu.make_async_copy(piece, out, sems.at[2 + n, step]))
                 put[-1].start()
+                first += splits[n]
         for copy in put:
             copy.wait()
 
     kind = table.dtype
-    return call(
-        body,
-        [pltpu.HBM((rows, voc_rows // 2), kind)] * 2 + [pltpu.HBM((rows, voc_rows), kind)] * 3,
-        [place, mine, other, table], after, smem=1, far_args=3,
+    outs = [pltpu.HBM((rows, voc_rows // split), kind) for split in splits for _ in range(split)]
+    return call(
+        body, outs, [place, table, mine, other], after, smem=1, far_args=1, any_args=2,
         scratch=[
-            pltpu.VMEM((NY * rows, depth), kind),
+            pltpu.VMEM((count * rows, depth), kind),
             pltpu.VMEM((steps, CHUNK, depth), kind),
-            pltpu.VMEM((steps, NY * rows, CHUNK), kind),
-            pltpu.SemaphoreType.DMA((2 + NY, 2 * NY)),
+            pltpu.VMEM((steps, count * rows, CHUNK), kind),
+            pltpu.SemaphoreType.DMA((2 + count, 2 * NY)),
         ],
+    )
+
+
+def scales(hidden, after):
+    rows, width = hidden.shape
+    steps = rows // LANES
+
+    def body(hidden_ref, out, held, sems):
+        load = start_all(
+            [
+                pltpu.make_async_copy(hidden_ref.at[n * LANES : (n + 1) * LANES], held.at[n], sems.at[n])
+                for n in range(steps)
+            ]
+        )
+        for n in range(steps):
+            load[n].wait()
+            total = jnp.zeros((LANES, LANES), jnp.float32)
+            for start in range(0, width, LANES):
+                piece = held[n, :, start : start + LANES].astype(jnp.float32)
+                total += piece * piece
+            mean = jnp.sum(total.T, axis=0, keepdims=True) / width
+            out[:, n * LANES : (n + 1) * LANES] = lax.rsqrt(mean + norm_eps)
+
+    return call(
+        body, [like((1, rows), jnp.float32)], [hidden], after, far_args=1,
+        scratch=[pltpu.VMEM((steps, LANES, width), hidden.dtype), pltpu.SemaphoreType.DMA((steps,))],
     )
 
 
@@ -238,7 +265,7 @@
             copy.wait()
 
     return call(
-        body, [pltpu.HBM(ahead.shape, ahead.dtype)] * 2, [ahead, behind, far_a, far_b], after, far_args=4,
+        body, [pltpu.HBM(ahead.shape, ahead.dtype)] * 2, [ahead, behind, far_a, far_b], after, far_args=2, any_args=2,
         scratch=[pltpu.VMEM((3, rows, voc_rows), ahead.dtype), pltpu.SemaphoreType.DMA((6, NC))],
     )
 
@@ -246,7 +273,6 @@
 def cap_and_sum(place, own, left, right, row_scale, cols, parents, after):
     rows, voc_rows = own.shape
     half = rows // NC
-    peers = NX * NZ * NC
     wide = voc_rows // 2
 
     def body(
@@ -301,23 +327,32 @@
                 chosen += jnp.where(lane + start == col, moved, 0.0)
             for n, part in enumerate((total, chosen)):
                 row = jnp.sum(part.T, axis=0, keepdims=True)
-                at = pl.ds(pl.multiple_of(n * rows + natural * half, LANES), half)
-                stats_ref[:, at] = jnp.broadcast_to(row, (peers, half))
-
-    return call(
-        body, [like((rows, voc_rows), jnp.float32), like((peers, 2 * rows), jnp.float32)],
+                stats_ref[pl.ds(n * NC + natural, 1)] = row
+        stats_ref[2 * NC :] = jnp.zeros((SWAP - 2 * NC, half), jnp.float32)
+
+    return call(
+        body, [like((rows, voc_rows), jnp.float32), like((SWAP, half), jnp.float32)],
         [place, own, left, right, row_scale, cols, parents], after, smem=1, far_args=3,
         scratch=[pltpu.VMEM((NC, 2, 3, half, wide), own.dtype), pltpu.SemaphoreType.DMA((NC, 2, 3))],
     )
 
 
-def score(stats, parents, prev_scores, penalty, filler):
+def spread_sum(one, two):
+    peers = NX * NZ
+
+    def body(one_ref, two_ref, out):
+        total = one_ref[: 2 * NC] + two_ref[: 2 * NC]
+        out[...] = jnp.broadcast_to(total[None], out.shape)
+
+    return call(body, [like((peers, 2 * NC, one.shape[1]), one.dtype)], [one, two])
+
+
+def score(stats, parents, prev_scores, penalty, after):
     rows = parents.shape[1]
 
-    def body(stats_ref, par_ref, prev_ref, pen_ref, column, chosen_ref, norm_ref, fill):
-        fill[...] = jnp.zeros(fill.shape, fill.dtype)
-        sums = jnp.sum(stats_ref[...], axis=0, keepdims=True)
-        lse = jnp.log(sums[:, :rows])
+    def body(stats_ref, par_ref, prev_ref, pen_ref, column, chosen_ref, norm_ref):
+        sums = jnp.sum(stats_ref[...], axis=0)
+        lse = jnp.log(sums)
         sub = lax.broadcasted_iota(jnp.int32, (LANES, LANES), 0)
         lane = lax.broadcasted_iota(jnp.int32, (1, LANES), 1)
         for h in range(rows // LANES):
@@ -326,19 +361,18 @@
             def down(row):
                 return jnp.broadcast_to(row, (LANES, LANES)).T
 
-            lse_col = down(lse[:, at])
+            lse_col = down(lse[h : h + 1])
             column[at] = lse_col
             hit = sub == lane // BEAMS * BEAMS + par_ref[:, at]
             lse_par = jnp.sum(jnp.where(hit, lse_col, 0.0), axis=0, keepdims=True)
             prev_par = jnp.sum(jnp.where(hit, down(prev_ref[:, at]), 0.0), axis=0, keepdims=True)
-            chosen = sums[:, rows + h * LANES : rows + (h + 1) * LANES] - lse_par
+            chosen = sums[NC + h : NC + h + 1] - lse_par
             chosen_ref[:, at] = chosen
             norm_ref[:, at] = (prev_par + chosen) / pen_ref[:, at]
 
     row = like((1, rows), jnp.float32)
     return call(
-        body, [like((rows, LANES), jnp.float32), row, row, like(filler)],
-        [stats, parents, prev_scores, penalty],
+        body, [like((rows, LANES), jnp.float32), row, row], [stats, parents, prev_scores, penalty], after
     )
 
 
@@ -387,7 +421,7 @@
             copy.wait()
 
     return call(
-        body, [pltpu.HBM(one.shape, one.dtype)], [one, two], after, far_args=2,
+        body, [pltpu.HBM(one.shape, one.dtype)], [one, two], after, far_args=1, any_args=1,
         scratch=[
             pltpu.VMEM((2, *one.shape), one.dtype),
             pltpu.VMEM(one.shape, one.dtype),
@@ -409,7 +443,7 @@
     return call(body, [like((copies, rows, depth))], [stacked], after)
 
 
-def assemble(place, mine, other, after):
+def assemble(place, mine, other):
     parts = len(mine)
     quarters, part, depth = mine[0].shape
 
@@ -432,7 +466,7 @@
 
     return call(
         body, [pltpu.HBM((NC * parts * part, quarters * depth), mine[0].dtype)],
-        [place, *mine, *other], after, smem=1,
+        [place, *mine, *other], smem=1,
         scratch=[pltpu.SemaphoreType.DMA((NC * parts, quarters))],
     )
 
@@ -448,8 +482,9 @@
     gain = norm_gain.reshape(1, width)
     part = row_count // (NC * NX)
 
-    arrived = jnp.stack([tokens] + [shift(tokens, "y", NY, step) for step in (1, 2, 3)])
-    pieces, t_cut = cut_pieces(place, hidden, gain, [arrived])
+    arrived = [tokens] + [shift(tokens, "y", NY, step) for step in (1, 2, 3)]
+    pieces, t_cut = cut_pieces(place, hidden, gain, arrived[1:])
+    arrived = jnp.stack(arrived)
     mine = exchange(pieces, "y")
     other = shift(mine, "c", NC, 1)
     order = (y - jnp.arange(NY)) % NY
@@ -461,11 +496,15 @@
     got = shift(sent, "c", NC, 1)
     found, t_found = add(kept, got, [t_pick])
     found = exchange(found.reshape(NX * NY, part, depth), ("x", "y"))
-    far_a, far_b, ahead, behind, own, t_far = products(place, mine, other, embed_table, [t_found])
+    far_a, far_b, t_far = products(place, embed_table, mine, other, (2,), (2,), [t_found])
     far_a = shift(far_a, "y", NY, 1)
     far_b = shift(far_b, "y", NY, 3)
-    found, _ = sum_rows(found.reshape(NX, NY * part, depth), 1)
-    left, right, t_near = add_halves(ahead, behind, far_a, far_b, [])
+    ahead, behind, own, t_all = products(
+        place, embed_table, mine, other, (1, 3, 0), (1, 1, 1), [t_far]
+    )
+    row_scale, t_scale = scales(hidden, [t_all])
+    found, t_sum = sum_rows(found.reshape(NX, NY * part, depth), 1, [t_scale])
+    left, right, t_near = add_halves(ahead, behind, far_a, far_b, [t_sum])
     left = shift(left, "y", NY, 1)
     right = shift(right, "y", NY, 3)
 
@@ -473,23 +512,19 @@
     spread, t_z = sum_rows(found, NZ)
     spread = exchange(spread, "z").reshape(NY, part, depth)
 
-    states = hidden.astype(jnp.float32)
-    meansq = jnp.mean(states * states, axis=-1)
-    row_scale = lax.rsqrt(meansq + norm_eps)
     local_col = tokens - shard * voc_rows
     capped, stats, t_cap = cap_and_sum(
-        place, own, left, right, row_scale[None], local_col[None], parents[None], [spread]
-    )
-    stats = exchange(stats, VOC)
+        place, own, left, right, row_scale, local_col[None], parents[None], [spread]
+    )
+    stats, _ = spread_sum(stats, shift(stats, "c", NC, 1))
+    stats = exchange(stats, ("x", "z"))
     penalty = jnp.power((5.0 + lengths.astype(jnp.float32)) / 6.0, length_power)
-    column, chosen_lp, normalized, filler, _ = score(
-        stats, parents[None], prev_scores[None], penalty[None], (row_count, voc_rows // 4)
+    parts = [spread] + [shift(spread, "x", NX, step) for step in (1, 2, 3)]
+    next_embed, t_whole = assemble(place, parts, [shift(piece, "c", NC, 1) for piece in parts])
+    column, chosen_lp, normalized, _ = score(
+        stats, parents[None], prev_scores[None], penalty[None], [t_whole]
     )
     log_probs = subtract(capped, column)
-    late = [shift(array, "c", NC, 1) for array in (left, right)]
-    late.append(shift(filler, "c", NC, 1))
-    parts = [spread] + [shift(spread, "x", NX, step) for step in (1, 2, 3)]
-    next_embed, _ = assemble(place, parts, [shift(piece, "c", NC, 1) for piece in parts], late)
     return (log_probs, chosen_lp[0], normalized[0], next_embed)
 
 

time: 143 us -> 128 us (0.90)
  waiting for transfers between devices: 21.1 us -> 11.5 us
  local copies, waits for them, and re-layouts: 7.68 us -> 3.57 us
  Pallas kernels: 39.7 us -> 43.4 us
  other arithmetic: 3.11 us -> 0.21 us
  blocking collectives: 18.6 us -> 15.8 us
  starting transfers between devices: 50.8 us -> 52.3 us
    ppermute x19 -> x17, waiting for transfers between devices: 7.37 us -> 1.23 us  [shift(): lax.ppermute(value, axis, [(i, (i + step) % size) for i in range(size)])]
    ppermute x19 -> x17, starting transfers between devices: 24.5 us -> 30.2 us  [shift(): lax.ppermute(value, axis, [(i, (i + step) % size) for i in range(size)])]
    all_to_all x4, starting transfers between devices: 26.4 us -> 22 us  [exchange(): return lax.all_to_all(value, axes, 0, 0, tiled=True)]
    pallas_call x10 -> x13, Pallas kernels: 37.8 us -> 41.6 us  [call(): pl.pallas_call(whole, out_shape=list(outs) + [jax.ShapeDtypeStruct((8, LA...]
    all_to_all x4, waiting for transfers between devices: 13.7 us -> 10.3 us  [exchange(): return lax.all_to_all(value, axes, 0, 0, tiled=True)]
    unnamed x23 -> x12, local copies, waits for them, and re-layouts: 4.63 us -> 1.31 us
    all_to_all x1, blocking collectives: 18.6 us -> 15.8 us  [exchange(): return lax.all_to_all(value, axes, 0, 0, tiled=True)]
    reduce_sum x1 -> x0, other arithmetic: 2.21 us -> none  [local(): meansq = jnp.mean(states * states, axis=-1)]
  transfers between devices with their start and end apart: 23 -> 21, of which waited for: 8 -> 5; matrix products, arithmetic and copies ran while one was open for 4% -> 2% of each run, Pallas kernels for 23% -> 30%
where the time goes in v3:
time: 128 us
  starting transfers between devices  52.3 us (41%)
  Pallas kernels  43.4 us (34%)
  blocking collectives  15.8 us (12%)
  waiting for transfers between devices  11.5 us (9%)
  local copies, waits for them, and re-layouts  3.57 us (3%)
    pallas_call x13, Pallas kernels, call(): pl.pallas_call(whole, out_shape=list(outs) + [jax.ShapeDtypeStruct((8, LA...  41.6 us
    ppermute x17, starting transfers between devices, shift(): lax.ppermute(value, axis, [(i, (i + step) % size) for i in range(size)])  30.2 us
    all_to_all x4, starting transfers between devices, exchange(): return lax.all_to_all(value, axes, 0, 0, tiled=True)  22 us
    all_to_all x1, blocking collectives, exchange(): return lax.all_to_all(value, axes, 0, 0, tiled=True)  15.8 us
    all_to_all x4, waiting for transfers between devices, exchange(): return lax.all_to_all(value, axes, 0, 0, tiled=True)  10.3 us
  transfers between devices with their start and end apart: 21, of which 5 were waited for; matrix products, arithmetic and copies ran while one was open for 2% of the time, Pallas kernels for 30%

profile of v3, /device:TPU:1, one launch (start us, length us, event | category | flops | bytes accessed | tf_op | source)
XLA Modules:
  0.0 127.7 jit_solution(5901419108799135957)
XLA Ops:
  0.6 2.2 %collective-permute-start = (s32[256]{0:T(256)}, s32[256]{0:T(256)S(1)}, u32[]{:S(2)}, u32[]{:S(2)}) collective-permute-start(s32[256]{0:T(256)} %param.10), channel_id=1, source_target_pairs={{0,1},{1,2},{2,3},{3,0},{4,5},{5,6},{6,7},{7,4},{8,9},{9,10},{10,1... | collective-permute-start | bytes 3080 | tf_op jit(solution)/shard_map/ppermute | solution.py:26
  2.8 2.6 %collective-permute-start.1 = (s32[256]{0:T(256)}, s32[256]{0:T(256)S(1)}, u32[]{:S(2)}, u32[]{:S(2)}) collective-permute-start(s32[256]{0:T(256)} %param.10), channel_id=1, source_target_pairs={{0,2},{1,3},{2,0},{3,1},{4,6},{5,7},{6,4},{7,5},{8,10},{9,11},{10,... | collective-permute-start | bytes 3080 | tf_op jit(solution)/shard_map/ppermute | solution.py:26
  8.4 2.9 %shard_map.102 = (bf16[4,128,1152]{2,1,0:T(8,128)(2,1)}, f32[8,128]{1,0:T(8,128)S(1)}) custom-call(s32[3]{0:T(128)S(1)} %pad_add_fusion.refs_0_, bf16[256,4608]{1,0:T(8,128)(2,1)} %refs_0_.3, bf16[1,4608]{1,0:T(2,128)(2,1)S(1)} %reshape.96.refs_2_, s32[256]{0:T(256)S(1)} %collective-permute-done.refs_3_, s32[256]{0:T(256)S(1)} %collective-permute-done.1.refs_4_, ...), custom_call_target="tpu_custom_call" | custom-call | tf_op jit(solution)/shard_map/pallas_call | solution.py:54
  11.3 3.5 %all-to-all-start = ((bf16[4,128,1152]{2,1,0:T(8,128)(2,1)}), bf16[4,128,1152]{2,1,0:T(8,128)(2,1)S(1)}, u32[]{:S(2)}, u32[]{:S(2)}) async-start(bf16[4,128,1152]{2,1,0:T(8,128)(2,1)} %get-tuple-element.33), calls=%async_computation | async-start | bytes 2359296 | tf_op jit(solution)/shard_map/all_to_all | solution.py:30
  15.7 9.0 %shard_map.103 = (bf16[512,1152]{1,0:T(8,128)(2,1)}, bf16[512,1152]{1,0:T(8,128)(2,1)}, f32[8,128]{1,0:T(8,128)S(1)}) custom-call(bf16[2048,1152]{1,0:T(8,128)(2,1)} %refs_1_.5, s32[1024,1]{1,0:T(8,128)S(1)} %reshape.102.refs_1_, f32[8,128]{1,0:T(8,128)S(1)} %get-tuple-element.34.refs_2_), custom_call_target="tpu_custom_call" | custom-call | tf_op jit(solution)/shard_map/pallas_call | solution.py:54
  24.7 2.5 %collective-permute-start.4 = (bf16[512,1152]{1,0:T(8,128)(2,1)}, bf16[512,1152]{1,0:T(8,128)(2,1)S(1)}, u32[]{:S(2)}, u32[]{:S(2)}) collective-permute-start(bf16[512,1152]{1,0:T(8,128)(2,1)} %get-tuple-element.36), channel_id=1, source_target_pairs={{0,4},{4,0},{1,5},{5,1},{2,6},{6,2},{3,7},{7,3},{8,12},{12,8},{9,1... | collective-permute-start | bytes 3538952 | tf_op jit(solution)/shard_map/ppermute | solution.py:26
  28.9 3.3 %collective-permute-start.3 = (bf16[4,128,1152]{2,1,0:T(8,128)(2,1)S(1)}, bf16[4,128,1152]{2,1,0:T(8,128)(2,1)S(1)}, u32[]{:S(2)}, u32[]{:S(2)}) collective-permute-start(bf16[4,128,1152]{2,1,0:T(8,128)(2,1)S(1)} %all-to-all-done.refs_2_), channel_id=1, source_target_pairs={{0,4},{4,0},{1,5},{5,1},{2,6},{6,2},{3,7},{7,3},{8,12},{12,8},{9,1... | collective-permute-start | bytes 3538952 | tf_op jit(solution)/shard_map/ppermute | solution.py:26
  32.2 2.1 %shard_map.104 = (bf16[512,1152]{1,0:T(8,128)(2,1)}, f32[8,128]{1,0:T(8,128)S(1)}) custom-call(bf16[512,1152]{1,0:T(8,128)(2,1)} %get-tuple-element.35.refs_0_, bf16[512,1152]{1,0:T(8,128)(2,1)S(1)} %collective-permute-done.4.refs_1_, f32[8,128]{1,0:T(8,128)S(1)} %get-tuple-element.37.refs_2_), custom_call_target="tpu_custom_call" | custom-call | tf_op jit(solution)/shard_map/pallas_call | solution.py:54
  34.4 4.8 %all-to-all-start.1 = ((bf16[16,32,1152]{2,1,0:T(8,128)(2,1)}), bf16[16,32,1152]{2,1,0:T(8,128)(2,1)S(1)}, u32[]{:S(2)}, u32[]{:S(2)}) async-start(bf16[16,32,1152]{2,1,0:T(8,128)(2,1)} %bitcast.25), calls=%async_computation.1 | async-start | bytes 2359296 | tf_op jit(solution)/shard_map/all_to_all | solution.py:30
  39.1 5.0 %shard_map.105 = (bf16[256,1024]{1,0:T(8,128)(2,1)}, bf16[256,1024]{1,0:T(8,128)(2,1)}, f32[8,128]{1,0:T(8,128)S(1)}) custom-call(s32[3]{0:T(128)S(1)} %pad_add_fusion.refs_0_, bf16[2048,1152]{1,0:T(8,128)(2,1)} %refs_1_.5, bf16[4,128,1152]{2,1,0:T(8,128)(2,1)S(1)} %all-to-all-done.refs_2_, bf16[4,128,1152]{2,1,0:T(8,128)(2,1)S(1)} %collective-permute-done.3.refs_3_, ...), custom_call_target="tpu_custom_call" | custom-call | tf_op jit(solution)/shard_map/pallas_call | solution.py:54
  47.1 8.0 %shard_map.106 = (bf16[256,2048]{1,0:T(8,128)(2,1)}, bf16[256,2048]{1,0:T(8,128)(2,1)}, bf16[256,2048]{1,0:T(8,128)(2,1)}, f32[8,128]{1,0:T(8,128)S(1)}) custom-call(s32[3]{0:T(128)S(1)} %pad_add_fusion.refs_0_, bf16[2048,1152]{1,0:T(8,128)(2,1)} %refs_1_.5, bf16[4,128,1152]{2,1,0:T(8,128)(2,1)S(1)} %all-to-all-done.refs_2_, ...), custom_call_target="tpu_custom_call" | custom-call | tf_op jit(solution)/shard_map/pallas_call | solution.py:54
  55.1 2.0 %shard_map.107 = (f32[1,256]{1,0:T(1,128)S(1)}, f32[8,128]{1,0:T(8,128)S(1)}) custom-call(bf16[256,4608]{1,0:T(8,128)(2,1)} %refs_0_.3, f32[8,128]{1,0:T(8,128)S(1)} %get-tuple-element.46.refs_1_), custom_call_target="tpu_custom_call" | custom-call | tf_op jit(solution)/shard_map/pallas_call | solution.py:54
  58.0 8.2 %all-to-all-start.2 = ((bf16[8,16,1152]{2,1,0:T(8,128)(2,1)}), bf16[8,16,1152]{2,1,0:T(8,128)(2,1)S(1)}, u32[]{:S(2)}, u32[]{:S(2)}) async-start(bf16[8,16,1152]{2,1,0:T(8,128)(2,1)} %bitcast.7), calls=%async_computation.2 | async-start | bytes 589824 | tf_op jit(solution)/shard_map/all_to_all | solution.py:30
  67.1 3.4 %shard_map.109 = (bf16[256,2048]{1,0:T(8,128)(2,1)}, bf16[256,2048]{1,0:T(8,128)(2,1)}, f32[8,128]{1,0:T(8,128)}) custom-call(bf16[256,2048]{1,0:T(8,128)(2,1)} %get-tuple-element.41.refs_0_, bf16[256,2048]{1,0:T(8,128)(2,1)} %get-tuple-element.42.refs_1_, bf16[256,1024]{1,0:T(8,128)(2,1)} %collective-permute-done.5.refs_2_, ...), custom_call_target="tpu_custom_call" | custom-call | tf_op jit(solution)/shard_map/pallas_call | solution.py:54
  70.6 2.7 %collective-permute-start.8 = (bf16[256,2048]{1,0:T(8,128)(2,1)}, bf16[256,2048]{1,0:T(8,128)(2,1)S(1)}, u32[]{:S(2)}, u32[]{:S(2)}) collective-permute-start(bf16[256,2048]{1,0:T(8,128)(2,1)} %get-tuple-element.50), channel_id=1, source_target_pairs={{0,3},{1,0},{2,1},{3,2},{4,7},{5,4},{6,5},{7,6},{8,11},{9,8},{10,9... | collective-permute-start | bytes 3145736 | tf_op jit(solution)/shard_map/ppermute | solution.py:26
  73.3 2.7 %all-to-all-done.2.refs_0_ = bf16[8,16,1152]{2,1,0:T(8,128)(2,1)S(1)} async-done(((bf16[8,16,1152]{2,1,0:T(8,128)(2,1)}), bf16[8,16,1152]{2,1,0:T(8,128)(2,1)S(1)}, u32[]{:S(2)}, u32[]{:S(2)}) %all-to-all-start.2) | async-done | bytes 294944 | tf_op jit(solution)/shard_map/all_to_all | solution.py:30
  76.6 15.8 %all_to_all.25 = bf16[8,16,1152]{2,1,0:T(8,128)(2,1)S(1)} all-to-all(bf16[8,16,1152]{2,1,0:T(8,128)(2,1)S(1)} %get-tuple-element.53), channel_id=1, replica_groups=mesh['x'=4,'z'=8,'c'=2,'y'=4] {'z'}, dimensions={0} | all-to-all | bytes 589824 | tf_op jit(solution)/shard_map/all_to_all | solution.py:30
  93.1 2.4 %collective-permute-start.11 = (bf16[4,32,1152]{2,1,0:T(8,128)(2,1)S(1)}, bf16[4,32,1152]{2,1,0:T(8,128)(2,1)S(1)}, u32[]{:S(2)}, u32[]{:S(2)}) collective-permute-start(bf16[4,32,1152]{2,1,0:T(8,128)(2,1)S(1)} %bitcast.15), channel_id=1, source_target_pairs={{0,128},{64,192},{128,0},{192,64},{1,129},{65,193},{129,1},{193,65... | collective-permute-start | bytes 884744 | tf_op jit(solution)/shard_map/ppermute | solution.py:26
  98.0 3.4 %shard_map.111 = (f32[256,2048]{1,0:T(8,128)S(1)}, f32[512,128]{1,0:T(8,128)S(1)}, f32[8,128]{1,0:T(8,128)}) custom-call(s32[3]{0:T(128)S(1)} %pad_add_fusion.refs_0_, bf16[256,2048]{1,0:T(8,128)(2,1)} %get-tuple-element.40.refs_1_, bf16[256,2048]{1,0:T(8,128)(2,1)} %copy-done.2, bf16[256,2048]{1,0:T(8,128)(2,1)} %copy-done.3, ...), custom_call_target="tpu_custom_call" | custom-call | tf_op jit(solution)/shard_map/pallas_call | solution.py:54
  101.4 4.1 %collective-permute-start.9 = (f32[512,128]{1,0:T(8,128)S(1)}, f32[512,128]{1,0:T(8,128)S(1)}, u32[]{:S(2)}, u32[]{:S(2)}) collective-permute-start(f32[512,128]{1,0:T(8,128)S(1)} %get-tuple-element.55.refs_0_), channel_id=1, source_target_pairs={{0,4},{4,0},{1,5},{5,1},{2,6},{6,2},{3,7},{7,3},{8,12},{12,8},{9,1... | collective-permute-start | bytes 786440 | tf_op jit(solution)/shard_map/ppermute | solution.py:26
  106.5 3.3 %collective-permute-start.15 = (bf16[4,32,1152]{2,1,0:T(8,128)(2,1)S(1)}, bf16[4,32,1152]{2,1,0:T(8,128)(2,1)}, u32[]{:S(2)}, u32[]{:S(2)}) collective-permute-start(bf16[4,32,1152]{2,1,0:T(8,128)(2,1)S(1)} %collective-permute-done.11.refs_3_), channel_id=1, source_target_pairs={{0,4},{4,0},{1,5},{5,1},{2,6},{6,2},{3,7},{7,3},{8,12},{12,8},{9,1... | collective-permute-start | bytes 884744 | tf_op jit(solution)/shard_map/ppermute | solution.py:26
  110.6 5.6 %all-to-all-start.4 = ((f32[32,4,128]{2,1,0:T(4,128)}), f32[32,4,128]{2,1,0:T(4,128)S(1)}, u32[]{:S(2)}, u32[]{:S(2)}) async-start(f32[32,4,128]{2,1,0:T(4,128)} %get-tuple-element.56), calls=%async_computation.4 | async-start | bytes 131072 | tf_op jit(solution)/shard_map/all_to_all | solution.py:30
  116.3 2.9 %shard_map.113 = (bf16[256,4608]{1,0:T(8,128)(2,1)}, f32[8,128]{1,0:T(8,128)S(1)}) custom-call(s32[3]{0:T(128)S(1)} %pad_add_fusion.refs_0_, bf16[4,32,1152]{2,1,0:T(8,128)(2,1)S(1)} %bitcast.19, bf16[4,32,1152]{2,1,0:T(8,128)(2,1)S(1)} %collective-permute-done.10.refs_2_, bf16[4,32,1152]{2,1,0:T(8,128)(2,1)S(1)} %collective-permute-done.11.refs_3_, ...), custom_call_target="tpu_custom_call" | custom-call | tf_op jit(solution)/shard_map/pallas_call | solution.py:54
  119.2 5.9 %all-to-all-done.4.refs_0_ = f32[32,4,128]{2,1,0:T(4,128)S(1)} async-done(((f32[32,4,128]{2,1,0:T(4,128)}), f32[32,4,128]{2,1,0:T(4,128)S(1)}, u32[]{:S(2)}, u32[]{:S(2)}) %all-to-all-start.4) | async-done | bytes 65568 | tf_op jit(solution)/shard_map/all_to_all | solution.py:30
  (58 shorter events, 18.6 us)
Async XLA Ops:
  0.6 7.5 %collective-permute-start = (s32[256]{0:T(256)}, s32[256]{0:T(256)S(1)}, u32[]{:S(2)}, u32[]{:S(2)}) collective-permute-start(s32[256]{0:T(256)} %param.10), channel_id=1, source_target_pairs={{0,1},{1,2},{2,3},{3,0},{4,5},{5,6},{6,7},{7,4},{8,9},{9,10},{10,1... | collective-permute-start | bytes 3080 | tf_op jit(solution)/shard_map/ppermute | solution.py:26
  2.8 5.3 %collective-permute-start.1 = (s32[256]{0:T(256)}, s32[256]{0:T(256)S(1)}, u32[]{:S(2)}, u32[]{:S(2)}) collective-permute-start(s32[256]{0:T(256)} %param.10), channel_id=1, source_target_pairs={{0,2},{1,3},{2,0},{3,1},{4,6},{5,7},{6,4},{7,5},{8,10},{9,11},{10,... | collective-permute-start | bytes 3080 | tf_op jit(solution)/shard_map/ppermute | solution.py:26
  5.5 2.9 %collective-permute-start.2 = (s32[256]{0:T(256)}, s32[256]{0:T(256)S(1)}, u32[]{:S(2)}, u32[]{:S(2)}) collective-permute-start(s32[256]{0:T(256)} %param.10), channel_id=1, source_target_pairs={{0,3},{1,0},{2,1},{3,2},{4,7},{5,4},{6,5},{7,6},{8,11},{9,8},{10,9... | collective-permute-start | bytes 3080 | tf_op jit(solution)/shard_map/ppermute | solution.py:26
  11.3 17.6 %all-to-all-start = ((bf16[4,128,1152]{2,1,0:T(8,128)(2,1)}), bf16[4,128,1152]{2,1,0:T(8,128)(2,1)S(1)}, u32[]{:S(2)}, u32[]{:S(2)}) async-start(bf16[4,128,1152]{2,1,0:T(8,128)(2,1)} %get-tuple-element.33), calls=%async_computation | async-start | bytes 2359296 | tf_op jit(solution)/shard_map/all_to_all | solution.py:30
  24.7 7.5 %collective-permute-start.4 = (bf16[512,1152]{1,0:T(8,128)(2,1)}, bf16[512,1152]{1,0:T(8,128)(2,1)S(1)}, u32[]{:S(2)}, u32[]{:S(2)}) collective-permute-start(bf16[512,1152]{1,0:T(8,128)(2,1)} %get-tuple-element.36), channel_id=1, source_target_pairs={{0,4},{4,0},{1,5},{5,1},{2,6},{6,2},{3,7},{7,3},{8,12},{12,8},{9,1... | collective-permute-start | bytes 3538952 | tf_op jit(solution)/shard_map/ppermute | solution.py:26
  28.9 10.2 %collective-permute-start.3 = (bf16[4,128,1152]{2,1,0:T(8,128)(2,1)S(1)}, bf16[4,128,1152]{2,1,0:T(8,128)(2,1)S(1)}, u32[]{:S(2)}, u32[]{:S(2)}) collective-permute-start(bf16[4,128,1152]{2,1,0:T(8,128)(2,1)S(1)} %all-to-all-done.refs_2_), channel_id=1, source_target_pairs={{0,4},{4,0},{1,5},{5,1},{2,6},{6,2},{3,7},{7,3},{8,12},{12,8},{9,1... | collective-permute-start | bytes 3538952 | tf_op jit(solution)/shard_map/ppermute | solution.py:26
  34.4 22.7 %all-to-all-start.1 = ((bf16[16,32,1152]{2,1,0:T(8,128)(2,1)}), bf16[16,32,1152]{2,1,0:T(8,128)(2,1)S(1)}, u32[]{:S(2)}, u32[]{:S(2)}) async-start(bf16[16,32,1152]{2,1,0:T(8,128)(2,1)} %bitcast.25), calls=%async_computation.1 | async-start | bytes 2359296 | tf_op jit(solution)/shard_map/all_to_all | solution.py:30
  44.1 23.0 %collective-permute-start.5 = (bf16[256,1024]{1,0:T(8,128)(2,1)}, bf16[256,1024]{1,0:T(8,128)(2,1)}, u32[]{:S(2)}, u32[]{:S(2)}) collective-permute-start(bf16[256,1024]{1,0:T(8,128)(2,1)} %get-tuple-element.43), channel_id=1, source_target_pairs={{0,1},{1,2},{2,3},{3,0},{4,5},{5,6},{6,7},{7,4},{8,9},{9,10},{10,1... | collective-permute-start | bytes 1572872 | tf_op jit(solution)/shard_map/ppermute | solution.py:26
  45.6 21.5 %collective-permute-start.6 = (bf16[256,1024]{1,0:T(8,128)(2,1)}, bf16[256,1024]{1,0:T(8,128)(2,1)}, u32[]{:S(2)}, u32[]{:S(2)}) collective-permute-start(bf16[256,1024]{1,0:T(8,128)(2,1)} %get-tuple-element.44), channel_id=1, source_target_pairs={{0,3},{1,0},{2,1},{3,2},{4,7},{5,4},{6,5},{7,6},{8,11},{9,8},{10,9... | collective-permute-start | bytes 1572872 | tf_op jit(solution)/shard_map/ppermute | solution.py:26
  58.0 18.0 %all-to-all-start.2 = ((bf16[8,16,1152]{2,1,0:T(8,128)(2,1)}), bf16[8,16,1152]{2,1,0:T(8,128)(2,1)S(1)}, u32[]{:S(2)}, u32[]{:S(2)}) async-start(bf16[8,16,1152]{2,1,0:T(8,128)(2,1)} %bitcast.7), calls=%async_computation.2 | async-start | bytes 589824 | tf_op jit(solution)/shard_map/all_to_all | solution.py:30
  67.1 29.5 %copy-start.4 = (s32[256]{0:T(256)S(1)}, s32[256]{0:T(256)}, u32[]{:S(2)}) copy-start(s32[256]{0:T(256)} %param.10) | copy-start | bytes 3076
  67.1 30.9 %copy-start = (s32[256]{0:T(256)S(1)}, s32[256]{0:T(256)}, u32[]{:S(2)}) copy-start(s32[256]{0:T(256)} %param.11) | copy-start | bytes 3076
  70.5 26.1 %collective-permute-start.7 = (bf16[256,2048]{1,0:T(8,128)(2,1)}, bf16[256,2048]{1,0:T(8,128)(2,1)S(1)}, u32[]{:S(2)}, u32[]{:S(2)}) collective-permute-start(bf16[256,2048]{1,0:T(8,128)(2,1)} %get-tuple-element.49), channel_id=1, source_target_pairs={{0,1},{1,2},{2,3},{3,0},{4,5},{5,6},{6,7},{7,4},{8,9},{9,10},{10,1... | collective-permute-start | bytes 3145736 | tf_op jit(solution)/shard_map/ppermute | solution.py:26
  70.6 26.1 %collective-permute-start.8 = (bf16[256,2048]{1,0:T(8,128)(2,1)}, bf16[256,2048]{1,0:T(8,128)(2,1)S(1)}, u32[]{:S(2)}, u32[]{:S(2)}) collective-permute-start(bf16[256,2048]{1,0:T(8,128)(2,1)} %get-tuple-element.50), channel_id=1, source_target_pairs={{0,3},{1,0},{2,1},{3,2},{4,7},{5,4},{6,5},{7,6},{8,11},{9,8},{10,9... | collective-permute-start | bytes 3145736 | tf_op jit(solution)/shard_map/ppermute | solution.py:26
  92.4 13.1 %collective-permute-start.10 = (bf16[4,32,1152]{2,1,0:T(8,128)(2,1)S(1)}, bf16[4,32,1152]{2,1,0:T(8,128)(2,1)S(1)}, u32[]{:S(2)}, u32[]{:S(2)}) collective-permute-start(bf16[4,32,1152]{2,1,0:T(8,128)(2,1)S(1)} %bitcast.14), channel_id=1, source_target_pairs={{0,64},{64,128},{128,192},{192,0},{1,65},{65,129},{129,193},{193,1... | collective-permute-start | bytes 884744 | tf_op jit(solution)/shard_map/ppermute | solution.py:26
  93.1 13.4 %collective-permute-start.11 = (bf16[4,32,1152]{2,1,0:T(8,128)(2,1)S(1)}, bf16[4,32,1152]{2,1,0:T(8,128)(2,1)S(1)}, u32[]{:S(2)}, u32[]{:S(2)}) collective-permute-start(bf16[4,32,1152]{2,1,0:T(8,128)(2,1)S(1)} %bitcast.15), channel_id=1, source_target_pairs={{0,128},{64,192},{128,0},{192,64},{1,129},{65,193},{129,1},{193,65... | collective-permute-start | bytes 884744 | tf_op jit(solution)/shard_map/ppermute | solution.py:26
  95.5 14.3 %collective-permute-start.12 = (bf16[4,32,1152]{2,1,0:T(8,128)(2,1)S(1)}, bf16[4,32,1152]{2,1,0:T(8,128)(2,1)S(1)}, u32[]{:S(2)}, u32[]{:S(2)}) collective-permute-start(bf16[4,32,1152]{2,1,0:T(8,128)(2,1)S(1)} %bitcast.16), channel_id=1, source_target_pairs={{0,192},{64,0},{128,64},{192,128},{1,193},{65,1},{129,65},{193,129... | collective-permute-start | bytes 884744 | tf_op jit(solution)/shard_map/ppermute | solution.py:26
  98.0 18.2 %copy-start.5 = (s32[256]{0:T(256)S(1)}, s32[256]{0:T(256)}, u32[]{:S(2)}) copy-start(s32[256]{0:T(256)} %param.13) | copy-start | bytes 3076
  101.4 8.6 %collective-permute-start.9 = (f32[512,128]{1,0:T(8,128)S(1)}, f32[512,128]{1,0:T(8,128)S(1)}, u32[]{:S(2)}, u32[]{:S(2)}) collective-permute-start(f32[512,128]{1,0:T(8,128)S(1)} %get-tuple-element.55.refs_0_), channel_id=1, source_target_pairs={{0,4},{4,0},{1,5},{5,1},{2,6},{6,2},{3,7},{7,3},{8,12},{12,8},{9,1... | collective-permute-start | bytes 786440 | tf_op jit(solution)/shard_map/ppermute | solution.py:26
  105.4 10.8 %collective-permute-start.13 = (bf16[4,32,1152]{2,1,0:T(8,128)(2,1)S(1)}, bf16[4,32,1152]{2,1,0:T(8,128)(2,1)}, u32[]{:S(2)}, u32[]{:S(2)}) collective-permute-start(bf16[4,32,1152]{2,1,0:T(8,128)(2,1)S(1)} %bitcast.18), channel_id=1, source_target_pairs={{0,4},{4,0},{1,5},{5,1},{2,6},{6,2},{3,7},{7,3},{8,12},{12,8},{9,1... | collective-permute-start | bytes 884744 | tf_op jit(solution)/shard_map/ppermute | solution.py:26
  105.5 10.7 %collective-permute-start.14 = (bf16[4,32,1152]{2,1,0:T(8,128)(2,1)S(1)}, bf16[4,32,1152]{2,1,0:T(8,128)(2,1)}, u32[]{:S(2)}, u32[]{:S(2)}) collective-permute-start(bf16[4,32,1152]{2,1,0:T(8,128)(2,1)S(1)} %collective-permute-done.10.refs_2_), channel_id=1, source_target_pairs={{0,4},{4,0},{1,5},{5,1},{2,6},{6,2},{3,7},{7,3},{8,12},{12,8},{9,1... | collective-permute-start | bytes 884744 | tf_op jit(solution)/shard_map/ppermute | solution.py:26
  106.5 9.8 %collective-permute-start.15 = (bf16[4,32,1152]{2,1,0:T(8,128)(2,1)S(1)}, bf16[4,32,1152]{2,1,0:T(8,128)(2,1)}, u32[]{:S(2)}, u32[]{:S(2)}) collective-permute-start(bf16[4,32,1152]{2,1,0:T(8,128)(2,1)S(1)} %collective-permute-done.11.refs_3_), channel_id=1, source_target_pairs={{0,4},{4,0},{1,5},{5,1},{2,6},{6,2},{3,7},{7,3},{8,12},{12,8},{9,1... | collective-permute-start | bytes 884744 | tf_op jit(solution)/shard_map/ppermute | solution.py:26
  109.8 6.5 %collective-permute-start.16 = (bf16[4,32,1152]{2,1,0:T(8,128)(2,1)S(1)}, bf16[4,32,1152]{2,1,0:T(8,128)(2,1)}, u32[]{:S(2)}, u32[]{:S(2)}) collective-permute-start(bf16[4,32,1152]{2,1,0:T(8,128)(2,1)S(1)} %collective-permute-done.12.refs_4_), channel_id=1, source_target_pairs={{0,4},{4,0},{1,5},{5,1},{2,6},{6,2},{3,7},{7,3},{8,12},{12,8},{9,1... | collective-permute-start | bytes 884744 | tf_op jit(solution)/shard_map/ppermute | solution.py:26
  110.6 14.4 %all-to-all-start.4 = ((f32[32,4,128]{2,1,0:T(4,128)}), f32[32,4,128]{2,1,0:T(4,128)S(1)}, u32[]{:S(2)}, u32[]{:S(2)}) async-start(f32[32,4,128]{2,1,0:T(4,128)} %get-tuple-element.56), calls=%async_computation.4 | async-start | bytes 131072 | tf_op jit(solution)/shard_map/all_to_all | solution.py:30
  (3 other events, 11.1 us)

commit v4 on v3

--- a/solution.py
+++ b/solution.py
@@ -347,54 +347,57 @@
     return call(body, [like((peers, 2 * NC, one.shape[1]), one.dtype)], [one, two])
 
 
-def score(stats, parents, prev_scores, penalty, after):
-    rows = parents.shape[1]
-
-    def body(stats_ref, par_ref, prev_ref, pen_ref, column, chosen_ref, norm_ref):
-        sums = jnp.sum(stats_ref[...], axis=0)
-        lse = jnp.log(sums)
-        sub = lax.broadcasted_iota(jnp.int32, (LANES, LANES), 0)
-        lane = lax.broadcasted_iota(jnp.int32, (1, LANES), 1)
-        for h in range(rows // LANES):
-            at = slice(h * LANES, (h + 1) * LANES)
-
-            def down(row):
-                return jnp.broadcast_to(row, (LANES, LANES)).T
-
-            lse_col = down(lse[h : h + 1])
-            column[at] = lse_col
-            hit = sub == lane // BEAMS * BEAMS + par_ref[:, at]
-            lse_par = jnp.sum(jnp.where(hit, lse_col, 0.0), axis=0, keepdims=True)
-            prev_par = jnp.sum(jnp.where(hit, down(prev_ref[:, at]), 0.0), axis=0, keepdims=True)
-            chosen = sums[NC + h : NC + h + 1] - lse_par
-            chosen_ref[:, at] = chosen
-            norm_ref[:, at] = (prev_par + chosen) / pen_ref[:, at]
-
-    row = like((1, rows), jnp.float32)
-    return call(
-        body, [like((rows, LANES), jnp.float32), row, row], [stats, parents, prev_scores, penalty], after
-    )
-
-
-def subtract(capped, column):
+def finish(capped, stats, parents, prev_scores, penalty, after):
     rows, voc_rows = capped.shape
     steps = 4
-
-    def body(capped_ref, column_ref, log_ref):
+    part = rows // steps
+
+    def body(capped_ref, stats_ref, par_ref, prev_ref, pen_ref, after_ref, log_ref, chosen_ref, norm_ref, column):
+        step = pl.program_id(0)
+
+        @pl.when(step == 0)
+        def _():
+            sums = jnp.sum(stats_ref[...], axis=0)
+            lse = jnp.log(sums)
+            sub = lax.broadcasted_iota(jnp.int32, (LANES, LANES), 0)
+            lane = lax.broadcasted_iota(jnp.int32, (1, LANES), 1)
+            for h in range(rows // LANES):
+                at = slice(h * LANES, (h + 1) * LANES)
+
+                def down(row):
+                    return jnp.broadcast_to(row, (LANES, LANES)).T
+
+                lse_col = down(lse[h : h + 1])
+                column[at] = lse_col
+                hit = sub == lane // BEAMS * BEAMS + par_ref[:, at]
+                lse_par = jnp.sum(jnp.where(hit, lse_col, 0.0), axis=0, keepdims=True)
+                prev_par = jnp.sum(jnp.where(hit, down(prev_ref[:, at]), 0.0), axis=0, keepdims=True)
+                chosen = sums[NC + h : NC + h + 1] - lse_par
+                chosen_ref[:, at] = chosen
+                norm_ref[:, at] = (prev_par + chosen) / pen_ref[:, at]
+
+        lse_here = column[pl.ds(pl.multiple_of(step * part, part), part)]
         for start in range(0, voc_rows, LANES):
             at = slice(start, start + LANES)
-            log_ref[:, at] = capped_ref[:, at] - column_ref[...]
-
-    block = pl.BlockSpec((rows // steps, voc_rows), lambda i: (i, 0))
+            log_ref[:, at] = capped_ref[:, at] - lse_here
+
+    block = pl.BlockSpec((part, voc_rows), lambda i: (i, 0))
+    row = pl.BlockSpec((1, rows), lambda i: (0, 0))
     return pl.pallas_call(
         body,
-        out_shape=like((rows, voc_rows), jnp.float32),
+        out_shape=[
+            like((rows, voc_rows), jnp.float32), like((1, rows), jnp.float32), like((1, rows), jnp.float32)
+        ],
         grid=(steps,),
-        in_specs=[block, pl.BlockSpec((rows // steps, LANES), lambda i: (i, 0))],
-        out_specs=block,
+        in_specs=[
+            block, pl.BlockSpec(stats.shape, lambda i: (0, 0, 0)), row, row, row,
+            pl.BlockSpec(memory_space=pl.ANY),
+        ],
+        out_specs=[block, row, row],
+        scratch_shapes=[pltpu.VMEM((rows, LANES), jnp.float32)],
         cost_estimate=pl.CostEstimate(flops=0, bytes_accessed=0, transcendentals=0),
         compiler_params=pltpu.CompilerParams(vmem_limit_bytes=VMEM),
-    )(capped, column)
+    )(capped, stats, parents, prev_scores, penalty, after)
 
 
 def add(one, two, after):
@@ -521,10 +524,9 @@
     penalty = jnp.power((5.0 + lengths.astype(jnp.float32)) / 6.0, length_power)
     parts = [spread] + [shift(spread, "x", NX, step) for step in (1, 2, 3)]
     next_embed, t_whole = assemble(place, parts, [shift(piece, "c", NC, 1) for piece in parts])
-    column, chosen_lp, normalized, _ = score(
-        stats, parents[None], prev_scores[None], penalty[None], [t_whole]
-    )
-    log_probs = subtract(capped, column)
+    log_probs, chosen_lp, normalized = finish(
+        capped, stats, parents[None], prev_scores[None], penalty[None], t_whole
+    )
     return (log_probs, chosen_lp[0], normalized[0], next_embed)
 
 

time: 128 us -> 128 us (level)
    pallas_call x13 -> x12, Pallas kernels: 41.6 us -> 40.8 us  [call(): pl.pallas_call(whole, out_shape=list(outs) + [jax.ShapeDtypeStruct((8, LA...]
where the time goes in v4:
time: 128 us; the launch traced here: 127 us
  starting transfers between devices  52.3 us (41%)
  Pallas kernels  42.9 us (34%)
  blocking collectives  15.8 us (12%)
  waiting for transfers between devices  11.5 us (9%)
  local copies, waits for them, and re-layouts  3.57 us (3%)
    pallas_call x12, Pallas kernels, call(): pl.pallas_call(whole, out_shape=list(outs) + [jax.ShapeDtypeStruct((8, LA...  40.8 us
    ppermute x17, starting transfers between devices, shift(): lax.ppermute(value, axis, [(i, (i + step) % size) for i in range(size)])  30.2 us
    all_to_all x4, starting transfers between devices, exchange(): return lax.all_to_all(value, axes, 0, 0, tiled=True)  22 us
    all_to_all x1, blocking collectives, exchange(): return lax.all_to_all(value, axes, 0, 0, tiled=True)  15.8 us
    all_to_all x4, waiting for transfers between devices, exchange(): return lax.all_to_all(value, axes, 0, 0, tiled=True)  10.3 us
  transfers between devices with their start and end apart: 21, of which 5 were waited for; matrix products, arithmetic and copies ran while one was open for 2% of the time, Pallas kernels for 30%

profile of v4, /device:TPU:1, one launch (start us, length us, event | category | flops | bytes accessed | tf_op | source)
XLA Modules:
  0.0 127.1 jit_solution(13356632618549487575)
XLA Ops:
  0.6 2.2 %collective-permute-start = (s32[256]{0:T(256)}, s32[256]{0:T(256)S(1)}, u32[]{:S(2)}, u32[]{:S(2)}) collective-permute-start(s32[256]{0:T(256)} %param.10), channel_id=1, source_target_pairs={{0,1},{1,2},{2,3},{3,0},{4,5},{5,6},{6,7},{7,4},{8,9},{9,10},{10,1... | collective-permute-start | bytes 3080 | tf_op jit(solution)/shard_map/ppermute | solution.py:26
  2.8 2.6 %collective-permute-start.1 = (s32[256]{0:T(256)}, s32[256]{0:T(256)S(1)}, u32[]{:S(2)}, u32[]{:S(2)}) collective-permute-start(s32[256]{0:T(256)} %param.10), channel_id=1, source_target_pairs={{0,2},{1,3},{2,0},{3,1},{4,6},{5,7},{6,4},{7,5},{8,10},{9,11},{10,... | collective-permute-start | bytes 3080 | tf_op jit(solution)/shard_map/ppermute | solution.py:26
  8.4 2.9 %shard_map.102 = (bf16[4,128,1152]{2,1,0:T(8,128)(2,1)}, f32[8,128]{1,0:T(8,128)S(1)}) custom-call(s32[3]{0:T(128)S(1)} %pad_add_fusion.refs_0_, bf16[256,4608]{1,0:T(8,128)(2,1)} %refs_0_.3, bf16[1,4608]{1,0:T(2,128)(2,1)S(1)} %reshape.96.refs_2_, s32[256]{0:T(256)S(1)} %collective-permute-done.refs_3_, s32[256]{0:T(256)S(1)} %collective-permute-done.1.refs_4_, ...), custom_call_target="tpu_custom_call" | custom-call | tf_op jit(solution)/shard_map/pallas_call | solution.py:54
  11.3 3.5 %all-to-all-start = ((bf16[4,128,1152]{2,1,0:T(8,128)(2,1)}), bf16[4,128,1152]{2,1,0:T(8,128)(2,1)S(1)}, u32[]{:S(2)}, u32[]{:S(2)}) async-start(bf16[4,128,1152]{2,1,0:T(8,128)(2,1)} %get-tuple-element.33), calls=%async_computation | async-start | bytes 2359296 | tf_op jit(solution)/shard_map/all_to_all | solution.py:30
  15.7 9.0 %shard_map.103 = (bf16[512,1152]{1,0:T(8,128)(2,1)}, bf16[512,1152]{1,0:T(8,128)(2,1)}, f32[8,128]{1,0:T(8,128)S(1)}) custom-call(bf16[2048,1152]{1,0:T(8,128)(2,1)} %refs_1_.5, s32[1024,1]{1,0:T(8,128)S(1)} %reshape.102.refs_1_, f32[8,128]{1,0:T(8,128)S(1)} %get-tuple-element.34.refs_2_), custom_call_target="tpu_custom_call" | custom-call | tf_op jit(solution)/shard_map/pallas_call | solution.py:54
  24.7 2.5 %collective-permute-start.4 = (bf16[512,1152]{1,0:T(8,128)(2,1)}, bf16[512,1152]{1,0:T(8,128)(2,1)S(1)}, u32[]{:S(2)}, u32[]{:S(2)}) collective-permute-start(bf16[512,1152]{1,0:T(8,128)(2,1)} %get-tuple-element.36), channel_id=1, source_target_pairs={{0,4},{4,0},{1,5},{5,1},{2,6},{6,2},{3,7},{7,3},{8,12},{12,8},{9,1... | collective-permute-start | bytes 3538952 | tf_op jit(solution)/shard_map/ppermute | solution.py:26
  28.9 3.3 %collective-permute-start.3 = (bf16[4,128,1152]{2,1,0:T(8,128)(2,1)S(1)}, bf16[4,128,1152]{2,1,0:T(8,128)(2,1)S(1)}, u32[]{:S(2)}, u32[]{:S(2)}) collective-permute-start(bf16[4,128,1152]{2,1,0:T(8,128)(2,1)S(1)} %all-to-all-done.refs_2_), channel_id=1, source_target_pairs={{0,4},{4,0},{1,5},{5,1},{2,6},{6,2},{3,7},{7,3},{8,12},{12,8},{9,1... | collective-permute-start | bytes 3538952 | tf_op jit(solution)/shard_map/ppermute | solution.py:26
  32.2 2.1 %shard_map.104 = (bf16[512,1152]{1,0:T(8,128)(2,1)}, f32[8,128]{1,0:T(8,128)S(1)}) custom-call(bf16[512,1152]{1,0:T(8,128)(2,1)} %get-tuple-element.35.refs_0_, bf16[512,1152]{1,0:T(8,128)(2,1)S(1)} %collective-permute-done.4.refs_1_, f32[8,128]{1,0:T(8,128)S(1)} %get-tuple-element.37.refs_2_), custom_call_target="tpu_custom_call" | custom-call | tf_op jit(solution)/shard_map/pallas_call | solution.py:54
  34.4 4.8 %all-to-all-start.1 = ((bf16[16,32,1152]{2,1,0:T(8,128)(2,1)}), bf16[16,32,1152]{2,1,0:T(8,128)(2,1)S(1)}, u32[]{:S(2)}, u32[]{:S(2)}) async-start(bf16[16,32,1152]{2,1,0:T(8,128)(2,1)} %bitcast.25), calls=%async_computation.1 | async-start | bytes 2359296 | tf_op jit(solution)/shard_map/all_to_all | solution.py:30
  39.1 5.0 %shard_map.105 = (bf16[256,1024]{1,0:T(8,128)(2,1)}, bf16[256,1024]{1,0:T(8,128)(2,1)}, f32[8,128]{1,0:T(8,128)S(1)}) custom-call(s32[3]{0:T(128)S(1)} %pad_add_fusion.refs_0_, bf16[2048,1152]{1,0:T(8,128)(2,1)} %refs_1_.5, bf16[4,128,1152]{2,1,0:T(8,128)(2,1)S(1)} %all-to-all-done.refs_2_, bf16[4,128,1152]{2,1,0:T(8,128)(2,1)S(1)} %collective-permute-done.3.refs_3_, ...), custom_call_target="tpu_custom_call" | custom-call | tf_op jit(solution)/shard_map/pallas_call | solution.py:54
  47.1 8.0 %shard_map.106 = (bf16[256,2048]{1,0:T(8,128)(2,1)}, bf16[256,2048]{1,0:T(8,128)(2,1)}, bf16[256,2048]{1,0:T(8,128)(2,1)}, f32[8,128]{1,0:T(8,128)S(1)}) custom-call(s32[3]{0:T(128)S(1)} %pad_add_fusion.refs_0_, bf16[2048,1152]{1,0:T(8,128)(2,1)} %refs_1_.5, bf16[4,128,1152]{2,1,0:T(8,128)(2,1)S(1)} %all-to-all-done.refs_2_, ...), custom_call_target="tpu_custom_call" | custom-call | tf_op jit(solution)/shard_map/pallas_call | solution.py:54
  58.0 8.2 %all-to-all-start.2 = ((bf16[8,16,1152]{2,1,0:T(8,128)(2,1)}), bf16[8,16,1152]{2,1,0:T(8,128)(2,1)S(1)}, u32[]{:S(2)}, u32[]{:S(2)}) async-start(bf16[8,16,1152]{2,1,0:T(8,128)(2,1)} %bitcast.7), calls=%async_computation.2 | async-start | bytes 589824 | tf_op jit(solution)/shard_map/all_to_all | solution.py:30
  67.1 3.4 %shard_map.109 = (bf16[256,2048]{1,0:T(8,128)(2,1)}, bf16[256,2048]{1,0:T(8,128)(2,1)}, f32[8,128]{1,0:T(8,128)}) custom-call(bf16[256,2048]{1,0:T(8,128)(2,1)} %get-tuple-element.41.refs_0_, bf16[256,2048]{1,0:T(8,128)(2,1)} %get-tuple-element.42.refs_1_, bf16[256,1024]{1,0:T(8,128)(2,1)} %collective-permute-done.5.refs_2_, ...), custom_call_target="tpu_custom_call" | custom-call | tf_op jit(solution)/shard_map/pallas_call | solution.py:54
  70.6 2.7 %collective-permute-start.8 = (bf16[256,2048]{1,0:T(8,128)(2,1)}, bf16[256,2048]{1,0:T(8,128)(2,1)S(1)}, u32[]{:S(2)}, u32[]{:S(2)}) collective-permute-start(bf16[256,2048]{1,0:T(8,128)(2,1)} %get-tuple-element.50), channel_id=1, source_target_pairs={{0,3},{1,0},{2,1},{3,2},{4,7},{5,4},{6,5},{7,6},{8,11},{9,8},{10,9... | collective-permute-start | bytes 3145736 | tf_op jit(solution)/shard_map/ppermute | solution.py:26
  73.3 2.7 %all-to-all-done.2.refs_0_ = bf16[8,16,1152]{2,1,0:T(8,128)(2,1)S(1)} async-done(((bf16[8,16,1152]{2,1,0:T(8,128)(2,1)}), bf16[8,16,1152]{2,1,0:T(8,128)(2,1)S(1)}, u32[]{:S(2)}, u32[]{:S(2)}) %all-to-all-start.2) | async-done | bytes 294944 | tf_op jit(solution)/shard_map/all_to_all | solution.py:30
  76.6 15.8 %all_to_all.25 = bf16[8,16,1152]{2,1,0:T(8,128)(2,1)S(1)} all-to-all(bf16[8,16,1152]{2,1,0:T(8,128)(2,1)S(1)} %get-tuple-element.53), channel_id=1, replica_groups=mesh['x'=4,'z'=8,'c'=2,'y'=4] {'z'}, dimensions={0} | all-to-all | bytes 589824 | tf_op jit(solution)/shard_map/all_to_all | solution.py:30
  93.1 2.4 %collective-permute-start.11 = (bf16[4,32,1152]{2,1,0:T(8,128)(2,1)S(1)}, bf16[4,32,1152]{2,1,0:T(8,128)(2,1)S(1)}, u32[]{:S(2)}, u32[]{:S(2)}) collective-permute-start(bf16[4,32,1152]{2,1,0:T(8,128)(2,1)S(1)} %bitcast.15), channel_id=1, source_target_pairs={{0,128},{64,192},{128,0},{192,64},{1,129},{65,193},{129,1},{193,65... | collective-permute-start | bytes 884744 | tf_op jit(solution)/shard_map/ppermute | solution.py:26
  98.0 3.4 %shard_map.111 = (f32[256,2048]{1,0:T(8,128)S(1)}, f32[512,128]{1,0:T(8,128)S(1)}, f32[8,128]{1,0:T(8,128)}) custom-call(s32[3]{0:T(128)S(1)} %pad_add_fusion.refs_0_, bf16[256,2048]{1,0:T(8,128)(2,1)} %get-tuple-element.40.refs_1_, bf16[256,2048]{1,0:T(8,128)(2,1)} %copy-done.2, bf16[256,2048]{1,0:T(8,128)(2,1)} %copy-done.3, ...), custom_call_target="tpu_custom_call" | custom-call | tf_op jit(solution)/shard_map/pallas_call | solution.py:54
  101.4 4.1 %collective-permute-start.9 = (f32[512,128]{1,0:T(8,128)S(1)}, f32[512,128]{1,0:T(8,128)S(1)}, u32[]{:S(2)}, u32[]{:S(2)}) collective-permute-start(f32[512,128]{1,0:T(8,128)S(1)} %get-tuple-element.55.refs_0_), channel_id=1, source_target_pairs={{0,4},{4,0},{1,5},{5,1},{2,6},{6,2},{3,7},{7,3},{8,12},{12,8},{9,1... | collective-permute-start | bytes 786440 | tf_op jit(solution)/shard_map/ppermute | solution.py:26
  106.5 3.3 %collective-permute-start.15 = (bf16[4,32,1152]{2,1,0:T(8,128)(2,1)S(1)}, bf16[4,32,1152]{2,1,0:T(8,128)(2,1)}, u32[]{:S(2)}, u32[]{:S(2)}) collective-permute-start(bf16[4,32,1152]{2,1,0:T(8,128)(2,1)S(1)} %collective-permute-done.11.refs_3_), channel_id=1, source_target_pairs={{0,4},{4,0},{1,5},{5,1},{2,6},{6,2},{3,7},{7,3},{8,12},{12,8},{9,1... | collective-permute-start | bytes 884744 | tf_op jit(solution)/shard_map/ppermute | solution.py:26
  110.6 5.6 %all-to-all-start.4 = ((f32[32,4,128]{2,1,0:T(4,128)}), f32[32,4,128]{2,1,0:T(4,128)S(1)}, u32[]{:S(2)}, u32[]{:S(2)}) async-start(f32[32,4,128]{2,1,0:T(4,128)} %get-tuple-element.56), calls=%async_computation.4 | async-start | bytes 131072 | tf_op jit(solution)/shard_map/all_to_all | solution.py:30
  116.3 2.9 %shard_map.113 = (bf16[256,4608]{1,0:T(8,128)(2,1)}, f32[8,128]{1,0:T(8,128)S(1)}) custom-call(s32[3]{0:T(128)S(1)} %pad_add_fusion.refs_0_, bf16[4,32,1152]{2,1,0:T(8,128)(2,1)S(1)} %bitcast.19, bf16[4,32,1152]{2,1,0:T(8,128)(2,1)S(1)} %collective-permute-done.10.refs_2_, bf16[4,32,1152]{2,1,0:T(8,128)(2,1)S(1)} %collective-permute-done.11.refs_3_, ...), custom_call_target="tpu_custom_call" | custom-call | tf_op jit(solution)/shard_map/pallas_call | solution.py:54
  119.2 5.9 %all-to-all-done.4.stats_ref = f32[32,4,128]{2,1,0:T(4,128)S(1)} async-done(((f32[32,4,128]{2,1,0:T(4,128)}), f32[32,4,128]{2,1,0:T(4,128)S(1)}, u32[]{:S(2)}, u32[]{:S(2)}) %all-to-all-start.4) | async-done | bytes 65568 | tf_op jit(solution)/shard_map/all_to_all | solution.py:30
  125.1 2.1 %shard_map.114 = (f32[256,2048]{1,0:T(8,128)}, f32[1,256]{1,0:T(1,128)}, f32[1,256]{1,0:T(1,128)}) custom-call(f32[256,2048]{1,0:T(8,128)S(1)} %get-tuple-element.54.capped_ref, f32[32,4,128]{2,1,0:T(4,128)S(1)} %all-to-all-done.4.stats_ref, s32[1,256]{1,0:T(1,128)S(1)} %bitcast.21, f32[1,256]{1,0:T(1,128)S(1)} %bitcast.24, f32[1,256]{1,0:T(1,128)S(1)} %bitcast.22, ...), custom_call_target="tpu_custom_call" | custom-call | tf_op jit(solution)/shard_map/pallas_call | solution.py:386
  (57 shorter events, 18.0 us)
Async XLA Ops:
  0.6 7.5 %collective-permute-start = (s32[256]{0:T(256)}, s32[256]{0:T(256)S(1)}, u32[]{:S(2)}, u32[]{:S(2)}) collective-permute-start(s32[256]{0:T(256)} %param.10), channel_id=1, source_target_pairs={{0,1},{1,2},{2,3},{3,0},{4,5},{5,6},{6,7},{7,4},{8,9},{9,10},{10,1... | collective-permute-start | bytes 3080 | tf_op jit(solution)/shard_map/ppermute | solution.py:26
  2.8 5.3 %collective-permute-start.1 = (s32[256]{0:T(256)}, s32[256]{0:T(256)S(1)}, u32[]{:S(2)}, u32[]{:S(2)}) collective-permute-start(s32[256]{0:T(256)} %param.10), channel_id=1, source_target_pairs={{0,2},{1,3},{2,0},{3,1},{4,6},{5,7},{6,4},{7,5},{8,10},{9,11},{10,... | collective-permute-start | bytes 3080 | tf_op jit(solution)/shard_map/ppermute | solution.py:26
  5.5 2.9 %collective-permute-start.2 = (s32[256]{0:T(256)}, s32[256]{0:T(256)S(1)}, u32[]{:S(2)}, u32[]{:S(2)}) collective-permute-start(s32[256]{0:T(256)} %param.10), channel_id=1, source_target_pairs={{0,3},{1,0},{2,1},{3,2},{4,7},{5,4},{6,5},{7,6},{8,11},{9,8},{10,9... | collective-permute-start | bytes 3080 | tf_op jit(solution)/shard_map/ppermute | solution.py:26
  11.3 17.6 %all-to-all-start = ((bf16[4,128,1152]{2,1,0:T(8,128)(2,1)}), bf16[4,128,1152]{2,1,0:T(8,128)(2,1)S(1)}, u32[]{:S(2)}, u32[]{:S(2)}) async-start(bf16[4,128,1152]{2,1,0:T(8,128)(2,1)} %get-tuple-element.33), calls=%async_computation | async-start | bytes 2359296 | tf_op jit(solution)/shard_map/all_to_all | solution.py:30
  24.7 7.5 %collective-permute-start.4 = (bf16[512,1152]{1,0:T(8,128)(2,1)}, bf16[512,1152]{1,0:T(8,128)(2,1)S(1)}, u32[]{:S(2)}, u32[]{:S(2)}) collective-permute-start(bf16[512,1152]{1,0:T(8,128)(2,1)} %get-tuple-element.36), channel_id=1, source_target_pairs={{0,4},{4,0},{1,5},{5,1},{2,6},{6,2},{3,7},{7,3},{8,12},{12,8},{9,1... | collective-permute-start | bytes 3538952 | tf_op jit(solution)/shard_map/ppermute | solution.py:26
  28.9 10.2 %collective-permute-start.3 = (bf16[4,128,1152]{2,1,0:T(8,128)(2,1)S(1)}, bf16[4,128,1152]{2,1,0:T(8,128)(2,1)S(1)}, u32[]{:S(2)}, u32[]{:S(2)}) collective-permute-start(bf16[4,128,1152]{2,1,0:T(8,128)(2,1)S(1)} %all-to-all-done.refs_2_), channel_id=1, source_target_pairs={{0,4},{4,0},{1,5},{5,1},{2,6},{6,2},{3,7},{7,3},{8,12},{12,8},{9,1... | collective-permute-start | bytes 3538952 | tf_op jit(solution)/shard_map/ppermute | solution.py:26
  34.4 22.7 %all-to-all-start.1 = ((bf16[16,32,1152]{2,1,0:T(8,128)(2,1)}), bf16[16,32,1152]{2,1,0:T(8,128)(2,1)S(1)}, u32[]{:S(2)}, u32[]{:S(2)}) async-start(bf16[16,32,1152]{2,1,0:T(8,128)(2,1)} %bitcast.25), calls=%async_computation.1 | async-start | bytes 2359296 | tf_op jit(solution)/shard_map/all_to_all | solution.py:30
  44.1 23.0 %collective-permute-start.5 = (bf16[256,1024]{1,0:T(8,128)(2,1)}, bf16[256,1024]{1,0:T(8,128)(2,1)}, u32[]{:S(2)}, u32[]{:S(2)}) collective-permute-start(bf16[256,1024]{1,0:T(8,128)(2,1)} %get-tuple-element.43), channel_id=1, source_target_pairs={{0,1},{1,2},{2,3},{3,0},{4,5},{5,6},{6,7},{7,4},{8,9},{9,10},{10,1... | collective-permute-start | bytes 1572872 | tf_op jit(solution)/shard_map/ppermute | solution.py:26
  45.6 21.5 %collective-permute-start.6 = (bf16[256,1024]{1,0:T(8,128)(2,1)}, bf16[256,1024]{1,0:T(8,128)(2,1)}, u32[]{:S(2)}, u32[]{:S(2)}) collective-permute-start(bf16[256,1024]{1,0:T(8,128)(2,1)} %get-tuple-element.44), channel_id=1, source_target_pairs={{0,3},{1,0},{2,1},{3,2},{4,7},{5,4},{6,5},{7,6},{8,11},{9,8},{10,9... | collective-permute-start | bytes 1572872 | tf_op jit(solution)/shard_map/ppermute | solution.py:26
  58.0 18.0 %all-to-all-start.2 = ((bf16[8,16,1152]{2,1,0:T(8,128)(2,1)}), bf16[8,16,1152]{2,1,0:T(8,128)(2,1)S(1)}, u32[]{:S(2)}, u32[]{:S(2)}) async-start(bf16[8,16,1152]{2,1,0:T(8,128)(2,1)} %bitcast.7), calls=%async_computation.2 | async-start | bytes 589824 | tf_op jit(solution)/shard_map/all_to_all | solution.py:30
  67.1 29.5 %copy-start.4 = (s32[256]{0:T(256)S(1)}, s32[256]{0:T(256)}, u32[]{:S(2)}) copy-start(s32[256]{0:T(256)} %param.10) | copy-start | bytes 3076
  67.1 30.9 %copy-start = (s32[256]{0:T(256)S(1)}, s32[256]{0:T(256)}, u32[]{:S(2)}) copy-start(s32[256]{0:T(256)} %param.11) | copy-start | bytes 3076
  70.5 26.1 %collective-permute-start.7 = (bf16[256,2048]{1,0:T(8,128)(2,1)}, bf16[256,2048]{1,0:T(8,128)(2,1)S(1)}, u32[]{:S(2)}, u32[]{:S(2)}) collective-permute-start(bf16[256,2048]{1,0:T(8,128)(2,1)} %get-tuple-element.49), channel_id=1, source_target_pairs={{0,1},{1,2},{2,3},{3,0},{4,5},{5,6},{6,7},{7,4},{8,9},{9,10},{10,1... | collective-permute-start | bytes 3145736 | tf_op jit(solution)/shard_map/ppermute | solution.py:26
  70.6 26.1 %collective-permute-start.8 = (bf16[256,2048]{1,0:T(8,128)(2,1)}, bf16[256,2048]{1,0:T(8,128)(2,1)S(1)}, u32[]{:S(2)}, u32[]{:S(2)}) collective-permute-start(bf16[256,2048]{1,0:T(8,128)(2,1)} %get-tuple-element.50), channel_id=1, source_target_pairs={{0,3},{1,0},{2,1},{3,2},{4,7},{5,4},{6,5},{7,6},{8,11},{9,8},{10,9... | collective-permute-start | bytes 3145736 | tf_op jit(solution)/shard_map/ppermute | solution.py:26
  92.4 13.1 %collective-permute-start.10 = (bf16[4,32,1152]{2,1,0:T(8,128)(2,1)S(1)}, bf16[4,32,1152]{2,1,0:T(8,128)(2,1)S(1)}, u32[]{:S(2)}, u32[]{:S(2)}) collective-permute-start(bf16[4,32,1152]{2,1,0:T(8,128)(2,1)S(1)} %bitcast.14), channel_id=1, source_target_pairs={{0,64},{64,128},{128,192},{192,0},{1,65},{65,129},{129,193},{193,1... | collective-permute-start | bytes 884744 | tf_op jit(solution)/shard_map/ppermute | solution.py:26
  93.1 13.4 %collective-permute-start.11 = (bf16[4,32,1152]{2,1,0:T(8,128)(2,1)S(1)}, bf16[4,32,1152]{2,1,0:T(8,128)(2,1)S(1)}, u32[]{:S(2)}, u32[]{:S(2)}) collective-permute-start(bf16[4,32,1152]{2,1,0:T(8,128)(2,1)S(1)} %bitcast.15), channel_id=1, source_target_pairs={{0,128},{64,192},{128,0},{192,64},{1,129},{65,193},{129,1},{193,65... | collective-permute-start | bytes 884744 | tf_op jit(solution)/shard_map/ppermute | solution.py:26
  95.5 14.3 %collective-permute-start.12 = (bf16[4,32,1152]{2,1,0:T(8,128)(2,1)S(1)}, bf16[4,32,1152]{2,1,0:T(8,128)(2,1)S(1)}, u32[]{:S(2)}, u32[]{:S(2)}) collective-permute-start(bf16[4,32,1152]{2,1,0:T(8,128)(2,1)S(1)} %bitcast.16), channel_id=1, source_target_pairs={{0,192},{64,0},{128,64},{192,128},{1,193},{65,1},{129,65},{193,129... | collective-permute-start | bytes 884744 | tf_op jit(solution)/shard_map/ppermute | solution.py:26
  98.0 18.2 %copy-start.5 = (s32[256]{0:T(256)S(1)}, s32[256]{0:T(256)}, u32[]{:S(2)}) copy-start(s32[256]{0:T(256)} %param.13) | copy-start | bytes 3076
  101.4 8.6 %collective-permute-start.9 = (f32[512,128]{1,0:T(8,128)S(1)}, f32[512,128]{1,0:T(8,128)S(1)}, u32[]{:S(2)}, u32[]{:S(2)}) collective-permute-start(f32[512,128]{1,0:T(8,128)S(1)} %get-tuple-element.55.refs_0_), channel_id=1, source_target_pairs={{0,4},{4,0},{1,5},{5,1},{2,6},{6,2},{3,7},{7,3},{8,12},{12,8},{9,1... | collective-permute-start | bytes 786440 | tf_op jit(solution)/shard_map/ppermute | solution.py:26
  105.4 10.8 %collective-permute-start.13 = (bf16[4,32,1152]{2,1,0:T(8,128)(2,1)S(1)}, bf16[4,32,1152]{2,1,0:T(8,128)(2,1)}, u32[]{:S(2)}, u32[]{:S(2)}) collective-permute-start(bf16[4,32,1152]{2,1,0:T(8,128)(2,1)S(1)} %bitcast.18), channel_id=1, source_target_pairs={{0,4},{4,0},{1,5},{5,1},{2,6},{6,2},{3,7},{7,3},{8,12},{12,8},{9,1... | collective-permute-start | bytes 884744 | tf_op jit(solution)/shard_map/ppermute | solution.py:26
  105.5 10.7 %collective-permute-start.14 = (bf16[4,32,1152]{2,1,0:T(8,128)(2,1)S(1)}, bf16[4,32,1152]{2,1,0:T(8,128)(2,1)}, u32[]{:S(2)}, u32[]{:S(2)}) collective-permute-start(bf16[4,32,1152]{2,1,0:T(8,128)(2,1)S(1)} %collective-permute-done.10.refs_2_), channel_id=1, source_target_pairs={{0,4},{4,0},{1,5},{5,1},{2,6},{6,2},{3,7},{7,3},{8,12},{12,8},{9,1... | collective-permute-start | bytes 884744 | tf_op jit(solution)/shard_map/ppermute | solution.py:26
  106.5 9.8 %collective-permute-start.15 = (bf16[4,32,1152]{2,1,0:T(8,128)(2,1)S(1)}, bf16[4,32,1152]{2,1,0:T(8,128)(2,1)}, u32[]{:S(2)}, u32[]{:S(2)}) collective-permute-start(bf16[4,32,1152]{2,1,0:T(8,128)(2,1)S(1)} %collective-permute-done.11.refs_3_), channel_id=1, source_target_pairs={{0,4},{4,0},{1,5},{5,1},{2,6},{6,2},{3,7},{7,3},{8,12},{12,8},{9,1... | collective-permute-start | bytes 884744 | tf_op jit(solution)/shard_map/ppermute | solution.py:26
  109.8 6.5 %collective-permute-start.16 = (bf16[4,32,1152]{2,1,0:T(8,128)(2,1)S(1)}, bf16[4,32,1152]{2,1,0:T(8,128)(2,1)}, u32[]{:S(2)}, u32[]{:S(2)}) collective-permute-start(bf16[4,32,1152]{2,1,0:T(8,128)(2,1)S(1)} %collective-permute-done.12.refs_4_), channel_id=1, source_target_pairs={{0,4},{4,0},{1,5},{5,1},{2,6},{6,2},{3,7},{7,3},{8,12},{12,8},{9,1... | collective-permute-start | bytes 884744 | tf_op jit(solution)/shard_map/ppermute | solution.py:26
  110.6 14.4 %all-to-all-start.4 = ((f32[32,4,128]{2,1,0:T(4,128)}), f32[32,4,128]{2,1,0:T(4,128)S(1)}, u32[]{:S(2)}, u32[]{:S(2)}) async-start(f32[32,4,128]{2,1,0:T(4,128)} %get-tuple-element.56), calls=%async_computation.4 | async-start | bytes 131072 | tf_op jit(solution)/shard_map/all_to_all | solution.py:30
  (3 other events, 11.1 us)

commit v5 on v4

--- a/solution.py
+++ b/solution.py
@@ -108,6 +108,22 @@
     )
 
 
+def take_planes(place, mine, groups):
+    def body(place_ref, mine_ref, *refs):
+        copies = []
+        for out, distances in zip(refs, groups):
+            for n, distance in enumerate(distances):
+                plane = lax.rem(place_ref[1] + distance, NY)
+                copies.append(pltpu.make_async_copy(mine_ref.at[plane], out.at[n], refs[-1].at[len(copies)]))
+        for copy in start_all(copies):
+            copy.wait()
+
+    outs = [like((len(distances), *mine.shape[1:])) for distances in groups]
+    return call(
+        body, outs, [place, mine], smem=1, any_args=1, scratch=[pltpu.SemaphoreType.DMA((NY,))]
+    )
+
+
 def pick_rows(cols, table, scale, after):
     voc_rows, depth = table.shape
     steps = voc_rows // CHUNK
@@ -115,7 +131,7 @@
     blocks = 1
     block = count // blocks
 
-    def body(table_ref, col_ref, sent, kept, held, found, sems):
+    def body(table_ref, col_ref, sent_a, sent_b, kept, held, found, sems):
         load = start_all(
             [
                 pltpu.make_async_copy(
@@ -134,32 +150,36 @@
                     copy.wait()
             picked = jnp.dot(hot, held[...], preferred_element_type=jnp.float32)
             found[n] = (picked * scale).astype(found.dtype)
-            out = (sent, kept)[n // blocks].at[n % blocks * block : (n % blocks + 1) * block]
-            put.append(pltpu.make_async_copy(found.at[n], out, sems.at[steps + n]))
-            put[-1].start()
+            if n == 0:
+                parts = ((found.at[0, : block // 2], sent_a), (found.at[0, block // 2 :], sent_b))
+            else:
+                parts = ((found.at[n], kept),)
+            for part, out in parts:
+                put.append(pltpu.make_async_copy(part, out, sems.at[steps + len(put)]))
+                put[-1].start()
         for copy in put:
             copy.wait()
 
     return call(
-        body, [pltpu.HBM((count, depth), table.dtype)] * 2, [table, cols], after, far_args=1,
+        body, [pltpu.HBM((rows, depth), table.dtype) for rows in (count // 2, count // 2, count)], [table, cols], after, far_args=1,
         scratch=[
             pltpu.VMEM((voc_rows, depth), table.dtype),
             pltpu.VMEM((NC * blocks, block, depth), table.dtype),
-            pltpu.SemaphoreType.DMA((steps + NC * blocks,)),
+            pltpu.SemaphoreType.DMA((steps + 3,)),
         ],
     )
 
 
-def products(place, table, mine, other, distances, splits, after):
+def products(place, table, mine, others, distances, splits, after):
     half, depth = mine.shape[1:]
     voc_rows = table.shape[0]
     steps = voc_rows // CHUNK
     rows = NC * half
     count = len(distances)
 
-    def body(place_ref, table_ref, mine_ref, other_ref, *refs):
-        outs = refs[: sum(splits)]
-        feats, held, results, sems = refs[sum(splits) :]
+    def body(place_ref, table_ref, mine_ref, *refs):
+        outs = refs[len(others) : -4]
+        feats, held, results, sems = refs[-4:]
         load = [
             pltpu.make_async_copy(table_ref.at[n * CHUNK : (n + 1) * CHUNK], held.at[n], sems.at[1, n])
             for n in range(steps)
@@ -167,10 +187,10 @@
         get = []
         for n, distance in enumerate(distances):
             plane = lax.rem(place_ref[1] + distance, NY)
-            for k, ref in enumerate((mine_ref, other_ref)):
+            for k, ref in enumerate((mine_ref.at[plane], refs[1 - distance // 2].at[distance % 2])):
                 start = n * rows + k * half
                 get.append(
-                    pltpu.make_async_copy(ref.at[plane], feats.at[start : start + half], sems.at[0, NC * n + k])
+                    pltpu.make_async_copy(ref, feats.at[start : start + half], sems.at[0, NC * n + k])
                 )
         start_all(load[:1] + get + load[1:])
         put = []
@@ -197,7 +217,7 @@
     kind = table.dtype
     outs = [pltpu.HBM((rows, voc_rows // split), kind) for split in splits for _ in range(split)]
     return call(
-        body, outs, [place, table, mine, other], after, smem=1, far_args=1, any_args=2,
+        body, outs, [place, table, mine, *others], after, smem=1, far_args=1, any_args=1 + len(others),
         scratch=[
             pltpu.VMEM((count * rows, depth), kind),
             pltpu.VMEM((steps, CHUNK, depth), kind),
@@ -400,18 +420,20 @@
     )(capped, stats, parents, prev_scores, penalty, after)
 
 
-def add(one, two, after):
+def add(one, halves, after):
     count, depth = one.shape
     cuts = [slice(start, start + LANES) for start in range(0, count, LANES)]
 
-    def body(one_ref, two_ref, out, held, total, sems):
-        load = [
-            [
-                pltpu.make_async_copy(ref.at[at], held.at[k, at], sems.at[k, n])
-                for k, ref in enumerate((one_ref, two_ref))
-            ]
-            for n, at in enumerate(cuts)
-        ]
+    def body(one_ref, low_ref, high_ref, out, held, total, sems):
+        load = []
+        for n, at in enumerate(cuts):
+            ref, start = (low_ref, at.start) if at.start < count // 2 else (high_ref, at.start - count // 2)
+            load.append(
+                [
+                    pltpu.make_async_copy(one_ref.at[at], held.at[0, at], sems.at[0, n]),
+                    pltpu.make_async_copy(ref.at[start : start + LANES], held.at[1, at], sems.at[1, n]),
+                ]
+            )
         put = [pltpu.make_async_copy(total.at[at], out.at[at], sems.at[2, n]) for n, at in enumerate(cuts)]
         for pair in load:
             start_all(pair)
@@ -424,7 +446,7 @@
             copy.wait()
 
     return call(
-        body, [pltpu.HBM(one.shape, one.dtype)], [one, two], after, far_args=1, any_args=1,
+        body, [pltpu.HBM(one.shape, one.dtype)], [one, *halves], after, far_args=1, any_args=2,
         scratch=[
             pltpu.VMEM((2, *one.shape), one.dtype),
             pltpu.VMEM(one.shape, one.dtype),
@@ -489,30 +511,30 @@
     pieces, t_cut = cut_pieces(place, hidden, gain, arrived[1:])
     arrived = jnp.stack(arrived)
     mine = exchange(pieces, "y")
-    other = shift(mine, "c", NC, 1)
+    *others, _ = take_planes(place, mine, ((2, 3), (0, 1)))
+    others = [shift(array, "c", NC, 1) for array in others]
     order = (y - jnp.arange(NY)) % NY
     planes = sum(jnp.where((order == s)[:, None], arrived[s : s + 1], 0) for s in range(NY))
     planes = (planes - shard * voc_rows).reshape(NY, NC, NX, part).transpose(1, 2, 0, 3)
     planes = jnp.where(core == 0, planes, planes[::-1]).reshape(NC * NX * NY * part, 1)
 
-    sent, kept, t_pick = pick_rows(planes, embed_table, scale, [t_cut])
-    got = shift(sent, "c", NC, 1)
-    found, t_found = add(kept, got, [t_pick])
+    *sent, kept, t_pick = pick_rows(planes, embed_table, scale, [t_cut])
+    got = [shift(piece, "c", NC, 1) for piece in sent]
+    row_scale, t_scale = scales(hidden, [t_pick])
+    found, t_found = add(kept, got, [t_scale])
     found = exchange(found.reshape(NX * NY, part, depth), ("x", "y"))
-    far_a, far_b, t_far = products(place, embed_table, mine, other, (2,), (2,), [t_found])
+    far_a, far_b, t_far = products(place, embed_table, mine, others[:1], (2,), (2,), [t_found])
     far_a = shift(far_a, "y", NY, 1)
     far_b = shift(far_b, "y", NY, 3)
-    ahead, behind, own, t_all = products(
-        place, embed_table, mine, other, (1, 3, 0), (1, 1, 1), [t_far]
-    )
-    row_scale, t_scale = scales(hidden, [t_all])
-    found, t_sum = sum_rows(found.reshape(NX, NY * part, depth), 1, [t_scale])
+    ahead, behind, t_all = products(place, embed_table, mine, others, (1, 3), (1, 1), [t_far])
+    found, t_sum = sum_rows(found.reshape(NX, NY * part, depth), 1, [t_all])
     left, right, t_near = add_halves(ahead, behind, far_a, far_b, [t_sum])
     left = shift(left, "y", NY, 1)
     right = shift(right, "y", NY, 3)
 
     found = exchange(found.reshape(NZ, NY * part // NZ, depth), "z")
-    spread, t_z = sum_rows(found, NZ)
+    own, t_own = products(place, embed_table, mine, others, (0,), (1,), [t_near])
+    spread, t_z = sum_rows(found, NZ, [t_own])
     spread = exchange(spread, "z").reshape(NY, part, depth)
 
     local_col = tokens - shard * voc_rows

time: 128 us -> 134 us (1.047)
  Pallas kernels: 42.9 us -> 46.3 us
  blocking collectives: 15.8 us -> 18.5 us
  starting transfers between devices: 52.3 us -> 54 us
    all_to_all x4, waiting for transfers between devices: 10.3 us -> 5.88 us  [exchange(): return lax.all_to_all(value, axes, 0, 0, tiled=True)]
    pallas_call x12 -> x14, Pallas kernels: 40.8 us -> 44.3 us  [call(): pl.pallas_call(whole, out_shape=list(outs) + [jax.ShapeDtypeStruct((8, LA...]
    ppermute x17 -> x19, waiting for transfers between devices: 1.23 us -> 4.27 us  [shift(): lax.ppermute(value, axis, [(i, (i + step) % size) for i in range(size)])]
    all_to_all x1, blocking collectives: 15.8 us -> 18.5 us  [exchange(): return lax.all_to_all(value, axes, 0, 0, tiled=True)]
    all_to_all x4, starting transfers between devices: 22 us -> 24.7 us  [exchange(): return lax.all_to_all(value, axes, 0, 0, tiled=True)]
    ppermute x17 -> x19, starting transfers between devices: 30.2 us -> 29.4 us  [shift(): lax.ppermute(value, axis, [(i, (i + step) % size) for i in range(size)])]
  transfers between devices with their start and end apart: 21 -> 23, of which waited for: 5 -> 5; matrix products, arithmetic and copies ran while one was open for 2% -> 2% of each run, Pallas kernels for 30% -> 31%
where the time goes in v5:
time: 134 us; the launch traced here: 133 us
  starting transfers between devices  54 us (40%)
  Pallas kernels  46.3 us (35%)
  blocking collectives  18.5 us (14%)
  waiting for transfers between devices  10.2 us (8%)
  local copies, waits for them, and re-layouts  2.99 us (2%)
    pallas_call x14, Pallas kernels, call(): pl.pallas_call(whole, out_shape=list(outs) + [jax.ShapeDtypeStruct((8, LA...  44.3 us
    ppermute x19, starting transfers between devices, shift(): lax.ppermute(value, axis, [(i, (i + step) % size) for i in range(size)])  29.4 us
    all_to_all x4, starting transfers between devices, exchange(): return lax.all_to_all(value, axes, 0, 0, tiled=True)  24.7 us
    all_to_all x1, blocking collectives, exchange(): return lax.all_to_all(value, axes, 0, 0, tiled=True)  18.5 us
    all_to_all x4, waiting for transfers between devices, exchange(): return lax.all_to_all(value, axes, 0, 0, tiled=True)  5.88 us
    ppermute x19, waiting for transfers between devices, shift(): lax.ppermute(value, axis, [(i, (i + step) % size) for i in range(size)])  4.27 us
  transfers between devices with their start and end apart: 23, of which 5 were waited for; matrix products, arithmetic and copies ran while one was open for 2% of the time, Pallas kernels for 31%

profile of v5, /device:TPU:1, one launch (start us, length us, event | category | flops | bytes accessed | tf_op | source)
XLA Modules:
  0.0 133.2 jit_solution(14842834083067447283)
XLA Ops:
  0.6 2.2 %collective-permute-start = (s32[256]{0:T(256)}, s32[256]{0:T(256)S(1)}, u32[]{:S(2)}, u32[]{:S(2)}) collective-permute-start(s32[256]{0:T(256)} %param.10), channel_id=1, source_target_pairs={{0,1},{1,2},{2,3},{3,0},{4,5},{5,6},{6,7},{7,4},{8,9},{9,10},{10,1... | collective-permute-start | bytes 3080 | tf_op jit(solution)/shard_map/ppermute | solution.py:26
  2.8 2.6 %collective-permute-start.1 = (s32[256]{0:T(256)}, s32[256]{0:T(256)S(1)}, u32[]{:S(2)}, u32[]{:S(2)}) collective-permute-start(s32[256]{0:T(256)} %param.10), channel_id=1, source_target_pairs={{0,2},{1,3},{2,0},{3,1},{4,6},{5,7},{6,4},{7,5},{8,10},{9,11},{10,... | collective-permute-start | bytes 3080 | tf_op jit(solution)/shard_map/ppermute | solution.py:26
  8.4 2.9 %shard_map.102 = (bf16[4,128,1152]{2,1,0:T(8,128)(2,1)}, f32[8,128]{1,0:T(8,128)S(1)}) custom-call(s32[3]{0:T(128)S(1)} %pad_add_fusion.refs_0_, bf16[256,4608]{1,0:T(8,128)(2,1)} %refs_0_.3, bf16[1,4608]{1,0:T(2,128)(2,1)S(1)} %reshape.96.refs_2_, s32[256]{0:T(256)S(1)} %collective-permute-done.refs_3_, s32[256]{0:T(256)S(1)} %collective-permute-done.1.refs_4_, ...), custom_call_target="tpu_custom_call" | custom-call | tf_op jit(solution)/shard_map/pallas_call | solution.py:54
  11.3 3.5 %all-to-all-start = ((bf16[4,128,1152]{2,1,0:T(8,128)(2,1)}), bf16[4,128,1152]{2,1,0:T(8,128)(2,1)S(1)}, u32[]{:S(2)}, u32[]{:S(2)}) async-start(bf16[4,128,1152]{2,1,0:T(8,128)(2,1)} %get-tuple-element.38), calls=%async_computation | async-start | bytes 2359296 | tf_op jit(solution)/shard_map/all_to_all | solution.py:30
  15.7 9.0 %shard_map.104 = (bf16[256,1152]{1,0:T(8,128)(2,1)}, bf16[256,1152]{1,0:T(8,128)(2,1)}, bf16[512,1152]{1,0:T(8,128)(2,1)}, f32[8,128]{1,0:T(8,128)S(1)}) custom-call(bf16[2048,1152]{1,0:T(8,128)(2,1)} %refs_1_.7, s32[1024,1]{1,0:T(8,128)S(1)} %reshape.102.refs_1_, f32[8,128]{1,0:T(8,128)S(1)} %get-tuple-element.41.refs_2_), custom_call_target="tpu_custom_call" | custom-call | tf_op jit(solution)/shard_map/pallas_call | solution.py:54
  24.7 2.5 %collective-permute-start.5 = (bf16[256,1152]{1,0:T(8,128)(2,1)}, bf16[256,1152]{1,0:T(8,128)(2,1)S(1)}, u32[]{:S(2)}, u32[]{:S(2)}) collective-permute-start(bf16[256,1152]{1,0:T(8,128)(2,1)} %get-tuple-element.43), channel_id=1, source_target_pairs={{0,4},{4,0},{1,5},{5,1},{2,6},{6,2},{3,7},{7,3},{8,12},{12,8},{9,1... | collective-permute-start | bytes 1769480 | tf_op jit(solution)/shard_map/ppermute | solution.py:26
  27.3 2.0 %shard_map.105 = (f32[1,256]{1,0:T(1,128)S(1)}, f32[8,128]{1,0:T(8,128)S(1)}) custom-call(bf16[256,4608]{1,0:T(8,128)(2,1)} %refs_0_.3, f32[8,128]{1,0:T(8,128)S(1)} %get-tuple-element.45.refs_1_), custom_call_target="tpu_custom_call" | custom-call | tf_op jit(solution)/shard_map/pallas_call | solution.py:54
  29.9 2.2 %shard_map.106 = (bf16[512,1152]{1,0:T(8,128)(2,1)}, f32[8,128]{1,0:T(8,128)S(1)}) custom-call(bf16[512,1152]{1,0:T(8,128)(2,1)} %get-tuple-element.42.refs_0_, bf16[256,1152]{1,0:T(8,128)(2,1)S(1)} %collective-permute-done.5.refs_1_, bf16[256,1152]{1,0:T(8,128)(2,1)S(1)} %collective-permute-done.6.refs_2_, f32[8,128]{1,0:T(8,128)S(1)} %get-tuple-element.46.refs_3_), custom_call_target="tpu_custom_call" | custom-call | tf_op jit(solution)/shard_map/pallas_call | solution.py:54
  32.0 7.1 %all-to-all-start.1 = ((bf16[16,32,1152]{2,1,0:T(8,128)(2,1)}), bf16[16,32,1152]{2,1,0:T(8,128)(2,1)S(1)}, u32[]{:S(2)}, u32[]{:S(2)}) async-start(bf16[16,32,1152]{2,1,0:T(8,128)(2,1)} %bitcast.26), calls=%async_computation.1 | async-start | bytes 2359296 | tf_op jit(solution)/shard_map/all_to_all | solution.py:30
  42.9 5.0 %shard_map.107 = (bf16[256,1024]{1,0:T(8,128)(2,1)}, bf16[256,1024]{1,0:T(8,128)(2,1)}, f32[8,128]{1,0:T(8,128)S(1)}) custom-call(s32[3]{0:T(128)S(1)} %pad_add_fusion.refs_0_, bf16[2048,1152]{1,0:T(8,128)(2,1)} %refs_1_.7, bf16[4,128,1152]{2,1,0:T(8,128)(2,1)S(1)} %all-to-all-done.refs_1_.refs_2_, bf16[2,128,1152]{2,1,0:T(8,128)(2,1)S(1)} %collective-permute-done.3.refs_3_, ...), custom_call_target="tpu_custom_call" | custom-call | tf_op jit(solution)/shard_map/pallas_call | solution.py:54
  50.9 6.5 %shard_map.108 = (bf16[256,2048]{1,0:T(8,128)(2,1)}, bf16[256,2048]{1,0:T(8,128)(2,1)}, f32[8,128]{1,0:T(8,128)S(1)}) custom-call(s32[3]{0:T(128)S(1)} %pad_add_fusion.refs_0_, bf16[2048,1152]{1,0:T(8,128)(2,1)} %refs_1_.7, bf16[4,128,1152]{2,1,0:T(8,128)(2,1)S(1)} %all-to-all-done.refs_1_.refs_2_, bf16[2,128,1152]{2,1,0:T(8,128)(2,1)S(1)} %collective-permute-done.3.refs_3_, ...), custom_call_target="tpu_custom_call" | custom-call | tf_op jit(solution)/shard_map/pallas_call | solution.py:54
  58.3 8.2 %all-to-all-start.2 = ((bf16[8,16,1152]{2,1,0:T(8,128)(2,1)}), bf16[8,16,1152]{2,1,0:T(8,128)(2,1)S(1)}, u32[]{:S(2)}, u32[]{:S(2)}) async-start(bf16[8,16,1152]{2,1,0:T(8,128)(2,1)} %bitcast.20), calls=%async_computation.2 | async-start | bytes 589824 | tf_op jit(solution)/shard_map/all_to_all | solution.py:30
  66.5 2.0 %collective-permute-done.7.refs_2_ = bf16[256,1024]{1,0:T(8,128)(2,1)} collective-permute-done((bf16[256,1024]{1,0:T(8,128)(2,1)}, bf16[256,1024]{1,0:T(8,128)(2,1)}, u32[]{:S(2)}, u32[]{:S(2)}) %collective-permute-start.7) | collective-permute-done | bytes 524320 | tf_op jit(solution)/shard_map/ppermute | solution.py:26
  68.6 2.8 %shard_map.110 = (bf16[256,2048]{1,0:T(8,128)(2,1)}, bf16[256,2048]{1,0:T(8,128)(2,1)}, f32[8,128]{1,0:T(8,128)S(1)}) custom-call(bf16[256,2048]{1,0:T(8,128)(2,1)} %get-tuple-element.49.refs_0_, bf16[256,2048]{1,0:T(8,128)(2,1)} %get-tuple-element.50.refs_1_, bf16[256,1024]{1,0:T(8,128)(2,1)} %collective-permute-done.7.refs_2_, ...), custom_call_target="tpu_custom_call" | custom-call | tf_op jit(solution)/shard_map/pallas_call | solution.py:54
  71.5 2.6 %collective-permute-start.10 = (bf16[256,2048]{1,0:T(8,128)(2,1)}, bf16[256,2048]{1,0:T(8,128)(2,1)}, u32[]{:S(2)}, u32[]{:S(2)}) collective-permute-start(bf16[256,2048]{1,0:T(8,128)(2,1)} %get-tuple-element.59), channel_id=1, source_target_pairs={{0,3},{1,0},{2,1},{3,2},{4,7},{5,4},{6,5},{7,6},{8,11},{9,8},{10,9... | collective-permute-start | bytes 3145736 | tf_op jit(solution)/shard_map/ppermute | solution.py:26
  74.1 5.0 %shard_map.111 = (bf16[256,2048]{1,0:T(8,128)(2,1)}, f32[8,128]{1,0:T(8,128)S(1)}) custom-call(s32[3]{0:T(128)S(1)} %pad_add_fusion.refs_0_, bf16[2048,1152]{1,0:T(8,128)(2,1)} %refs_1_.7, bf16[4,128,1152]{2,1,0:T(8,128)(2,1)S(1)} %all-to-all-done.refs_1_.refs_2_, bf16[2,128,1152]{2,1,0:T(8,128)(2,1)S(1)} %collective-permute-done.3.refs_3_, ...), custom_call_target="tpu_custom_call" | custom-call | tf_op jit(solution)/shard_map/pallas_call | solution.py:54
  79.7 18.5 %all_to_all.25 = bf16[8,16,1152]{2,1,0:T(8,128)(2,1)S(1)} all-to-all(bf16[8,16,1152]{2,1,0:T(8,128)(2,1)S(1)} %get-tuple-element.63), channel_id=1, replica_groups=mesh['x'=4,'z'=8,'c'=2,'y'=4] {'z'}, dimensions={0} | all-to-all | bytes 589824 | tf_op jit(solution)/shard_map/all_to_all | solution.py:30
  101.7 3.4 %shard_map.113 = (f32[256,2048]{1,0:T(8,128)S(1)}, f32[512,128]{1,0:T(8,128)S(1)}, f32[8,128]{1,0:T(8,128)}) custom-call(s32[3]{0:T(128)S(1)} %pad_add_fusion.refs_0_, bf16[256,2048]{1,0:T(8,128)(2,1)} %get-tuple-element.57.refs_1_, bf16[256,2048]{1,0:T(8,128)(2,1)} %collective-permute-done.9.refs_2_, bf16[256,2048]{1,0:T(8,128)(2,1)} %collective-permute-done.10.refs_3_, ...), custom_call_target="tpu_custom_call" | custom-call | tf_op jit(solution)/shard_map/pallas_call | solution.py:54
  105.1 3.9 %collective-permute-start.11 = (f32[512,128]{1,0:T(8,128)S(1)}, f32[512,128]{1,0:T(8,128)S(1)}, u32[]{:S(2)}, u32[]{:S(2)}) collective-permute-start(f32[512,128]{1,0:T(8,128)S(1)} %get-tuple-element.65.refs_0_), channel_id=1, source_target_pairs={{0,4},{4,0},{1,5},{5,1},{2,6},{6,2},{3,7},{7,3},{8,12},{12,8},{9,1... | collective-permute-start | bytes 786440 | tf_op jit(solution)/shard_map/ppermute | solution.py:26
  109.0 6.2 %collective-permute-start.16 = (bf16[4,32,1152]{2,1,0:T(8,128)(2,1)S(1)}, bf16[4,32,1152]{2,1,0:T(8,128)(2,1)}, u32[]{:S(2)}, u32[]{:S(2)}) collective-permute-start(bf16[4,32,1152]{2,1,0:T(8,128)(2,1)S(1)} %collective-permute-done.12.refs_2_), channel_id=1, source_target_pairs={{0,4},{4,0},{1,5},{5,1},{2,6},{6,2},{3,7},{7,3},{8,12},{12,8},{9,1... | collective-permute-start | bytes 884744 | tf_op jit(solution)/shard_map/ppermute | solution.py:26
  116.5 5.8 %all-to-all-start.4 = ((f32[32,4,128]{2,1,0:T(4,128)}), f32[32,4,128]{2,1,0:T(4,128)S(1)}, u32[]{:S(2)}, u32[]{:S(2)}) async-start(f32[32,4,128]{2,1,0:T(4,128)} %get-tuple-element.66), calls=%async_computation.4 | async-start | bytes 131072 | tf_op jit(solution)/shard_map/all_to_all | solution.py:30
  122.4 2.9 %shard_map.115 = (bf16[256,4608]{1,0:T(8,128)(2,1)}, f32[8,128]{1,0:T(8,128)S(1)}) custom-call(s32[3]{0:T(128)S(1)} %pad_add_fusion.refs_0_, bf16[4,32,1152]{2,1,0:T(8,128)(2,1)S(1)} %bitcast.19, bf16[4,32,1152]{2,1,0:T(8,128)(2,1)S(1)} %collective-permute-done.12.refs_2_, bf16[4,32,1152]{2,1,0:T(8,128)(2,1)S(1)} %collective-permute-done.13.refs_3_, ...), custom_call_target="tpu_custom_call" | custom-call | tf_op jit(solution)/shard_map/pallas_call | solution.py:54
  125.3 5.9 %all-to-all-done.4.stats_ref = f32[32,4,128]{2,1,0:T(4,128)S(1)} async-done(((f32[32,4,128]{2,1,0:T(4,128)}), f32[32,4,128]{2,1,0:T(4,128)S(1)}, u32[]{:S(2)}, u32[]{:S(2)}) %all-to-all-start.4) | async-done | bytes 65568 | tf_op jit(solution)/shard_map/all_to_all | solution.py:30
  131.2 2.1 %shard_map.116 = (f32[256,2048]{1,0:T(8,128)}, f32[1,256]{1,0:T(1,128)}, f32[1,256]{1,0:T(1,128)}) custom-call(f32[256,2048]{1,0:T(8,128)S(1)} %get-tuple-element.64.capped_ref, f32[32,4,128]{2,1,0:T(4,128)S(1)} %all-to-all-done.4.stats_ref, s32[1,256]{1,0:T(1,128)S(1)} %bitcast.22, f32[1,256]{1,0:T(1,128)S(1)} %bitcast.25, f32[1,256]{1,0:T(1,128)S(1)} %bitcast.23, ...), custom_call_target="tpu_custom_call" | custom-call | tf_op jit(solution)/shard_map/pallas_call | solution.py:406
  (61 shorter events, 17.7 us)
Async XLA Ops:
  0.6 7.5 %collective-permute-start = (s32[256]{0:T(256)}, s32[256]{0:T(256)S(1)}, u32[]{:S(2)}, u32[]{:S(2)}) collective-permute-start(s32[256]{0:T(256)} %param.10), channel_id=1, source_target_pairs={{0,1},{1,2},{2,3},{3,0},{4,5},{5,6},{6,7},{7,4},{8,9},{9,10},{10,1... | collective-permute-start | bytes 3080 | tf_op jit(solution)/shard_map/ppermute | solution.py:26
  2.8 5.3 %collective-permute-start.1 = (s32[256]{0:T(256)}, s32[256]{0:T(256)S(1)}, u32[]{:S(2)}, u32[]{:S(2)}) collective-permute-start(s32[256]{0:T(256)} %param.10), channel_id=1, source_target_pairs={{0,2},{1,3},{2,0},{3,1},{4,6},{5,7},{6,4},{7,5},{8,10},{9,11},{10,... | collective-permute-start | bytes 3080 | tf_op jit(solution)/shard_map/ppermute | solution.py:26
  5.5 2.9 %collective-permute-start.2 = (s32[256]{0:T(256)}, s32[256]{0:T(256)S(1)}, u32[]{:S(2)}, u32[]{:S(2)}) collective-permute-start(s32[256]{0:T(256)} %param.10), channel_id=1, source_target_pairs={{0,3},{1,0},{2,1},{3,2},{4,7},{5,4},{6,5},{7,6},{8,11},{9,8},{10,9... | collective-permute-start | bytes 3080 | tf_op jit(solution)/shard_map/ppermute | solution.py:26
  11.3 20.8 %all-to-all-start = ((bf16[4,128,1152]{2,1,0:T(8,128)(2,1)}), bf16[4,128,1152]{2,1,0:T(8,128)(2,1)S(1)}, u32[]{:S(2)}, u32[]{:S(2)}) async-start(bf16[4,128,1152]{2,1,0:T(8,128)(2,1)} %get-tuple-element.38), calls=%async_computation | async-start | bytes 2359296 | tf_op jit(solution)/shard_map/all_to_all | solution.py:30
  24.7 4.5 %collective-permute-start.5 = (bf16[256,1152]{1,0:T(8,128)(2,1)}, bf16[256,1152]{1,0:T(8,128)(2,1)S(1)}, u32[]{:S(2)}, u32[]{:S(2)}) collective-permute-start(bf16[256,1152]{1,0:T(8,128)(2,1)} %get-tuple-element.43), channel_id=1, source_target_pairs={{0,4},{4,0},{1,5},{5,1},{2,6},{6,2},{3,7},{7,3},{8,12},{12,8},{9,1... | collective-permute-start | bytes 1769480 | tf_op jit(solution)/shard_map/ppermute | solution.py:26
  27.2 2.7 %collective-permute-start.6 = (bf16[256,1152]{1,0:T(8,128)(2,1)}, bf16[256,1152]{1,0:T(8,128)(2,1)S(1)}, u32[]{:S(2)}, u32[]{:S(2)}) collective-permute-start(bf16[256,1152]{1,0:T(8,128)(2,1)} %get-tuple-element.44), channel_id=1, source_target_pairs={{0,4},{4,0},{1,5},{5,1},{2,6},{6,2},{3,7},{7,3},{8,12},{12,8},{9,1... | collective-permute-start | bytes 1769480 | tf_op jit(solution)/shard_map/ppermute | solution.py:26
  32.0 25.4 %all-to-all-start.1 = ((bf16[16,32,1152]{2,1,0:T(8,128)(2,1)}), bf16[16,32,1152]{2,1,0:T(8,128)(2,1)S(1)}, u32[]{:S(2)}, u32[]{:S(2)}) async-start(bf16[16,32,1152]{2,1,0:T(8,128)(2,1)} %bitcast.26), calls=%async_computation.1 | async-start | bytes 2359296 | tf_op jit(solution)/shard_map/all_to_all | solution.py:30
  40.6 2.4 %collective-permute-start.3 = (bf16[2,128,1152]{2,1,0:T(8,128)(2,1)S(1)}, bf16[2,128,1152]{2,1,0:T(8,128)(2,1)S(1)}, u32[]{:S(2)}, u32[]{:S(2)}) collective-permute-start(bf16[2,128,1152]{2,1,0:T(8,128)(2,1)S(1)} %get-tuple-element.39), channel_id=1, source_target_pairs={{0,4},{4,0},{1,5},{5,1},{2,6},{6,2},{3,7},{7,3},{8,12},{12,8},{9,1... | collective-permute-start | bytes 1769480 | tf_op jit(solution)/shard_map/ppermute | solution.py:26
  41.3 9.6 %collective-permute-start.4 = (bf16[2,128,1152]{2,1,0:T(8,128)(2,1)S(1)}, bf16[2,128,1152]{2,1,0:T(8,128)(2,1)S(1)}, u32[]{:S(2)}, u32[]{:S(2)}) collective-permute-start(bf16[2,128,1152]{2,1,0:T(8,128)(2,1)S(1)} %get-tuple-element.40), channel_id=1, source_target_pairs={{0,4},{4,0},{1,5},{5,1},{2,6},{6,2},{3,7},{7,3},{8,12},{12,8},{9,1... | collective-permute-start | bytes 1769480 | tf_op jit(solution)/shard_map/ppermute | solution.py:26
  47.9 20.6 %collective-permute-start.7 = (bf16[256,1024]{1,0:T(8,128)(2,1)}, bf16[256,1024]{1,0:T(8,128)(2,1)}, u32[]{:S(2)}, u32[]{:S(2)}) collective-permute-start(bf16[256,1024]{1,0:T(8,128)(2,1)} %get-tuple-element.51), channel_id=1, source_target_pairs={{0,1},{1,2},{2,3},{3,0},{4,5},{5,6},{6,7},{7,4},{8,9},{9,10},{10,1... | collective-permute-start | bytes 1572872 | tf_op jit(solution)/shard_map/ppermute | solution.py:26
  49.6 18.9 %collective-permute-start.8 = (bf16[256,1024]{1,0:T(8,128)(2,1)}, bf16[256,1024]{1,0:T(8,128)(2,1)}, u32[]{:S(2)}, u32[]{:S(2)}) collective-permute-start(bf16[256,1024]{1,0:T(8,128)(2,1)} %get-tuple-element.52), channel_id=1, source_target_pairs={{0,3},{1,0},{2,1},{3,2},{4,7},{5,4},{6,5},{7,6},{8,11},{9,8},{10,9... | collective-permute-start | bytes 1572872 | tf_op jit(solution)/shard_map/ppermute | solution.py:26
  58.3 20.8 %all-to-all-start.2 = ((bf16[8,16,1152]{2,1,0:T(8,128)(2,1)}), bf16[8,16,1152]{2,1,0:T(8,128)(2,1)S(1)}, u32[]{:S(2)}, u32[]{:S(2)}) async-start(bf16[8,16,1152]{2,1,0:T(8,128)(2,1)} %bitcast.20), calls=%async_computation.2 | async-start | bytes 589824 | tf_op jit(solution)/shard_map/all_to_all | solution.py:30
  71.4 30.3 %collective-permute-start.9 = (bf16[256,2048]{1,0:T(8,128)(2,1)}, bf16[256,2048]{1,0:T(8,128)(2,1)}, u32[]{:S(2)}, u32[]{:S(2)}) collective-permute-start(bf16[256,2048]{1,0:T(8,128)(2,1)} %get-tuple-element.58), channel_id=1, source_target_pairs={{0,1},{1,2},{2,3},{3,0},{4,5},{5,6},{6,7},{7,4},{8,9},{9,10},{10,1... | collective-permute-start | bytes 3145736 | tf_op jit(solution)/shard_map/ppermute | solution.py:26
  71.5 30.2 %collective-permute-start.10 = (bf16[256,2048]{1,0:T(8,128)(2,1)}, bf16[256,2048]{1,0:T(8,128)(2,1)}, u32[]{:S(2)}, u32[]{:S(2)}) collective-permute-start(bf16[256,2048]{1,0:T(8,128)(2,1)} %get-tuple-element.59), channel_id=1, source_target_pairs={{0,3},{1,0},{2,1},{3,2},{4,7},{5,4},{6,5},{7,6},{8,11},{9,8},{10,9... | collective-permute-start | bytes 3145736 | tf_op jit(solution)/shard_map/ppermute | solution.py:26
  74.1 27.6 %copy-start.1 = (s32[256]{0:T(256)S(1)}, s32[256]{0:T(256)}, u32[]{:S(2)}) copy-start(s32[256]{0:T(256)} %param.11) | copy-start | bytes 3076
  98.3 10.8 %collective-permute-start.12 = (bf16[4,32,1152]{2,1,0:T(8,128)(2,1)S(1)}, bf16[4,32,1152]{2,1,0:T(8,128)(2,1)S(1)}, u32[]{:S(2)}, u32[]{:S(2)}) collective-permute-start(bf16[4,32,1152]{2,1,0:T(8,128)(2,1)S(1)} %bitcast.14), channel_id=1, source_target_pairs={{0,64},{64,128},{128,192},{192,0},{1,65},{65,129},{129,193},{193,1... | collective-permute-start | bytes 884744 | tf_op jit(solution)/shard_map/ppermute | solution.py:26
  98.3 17.0 %collective-permute-start.13 = (bf16[4,32,1152]{2,1,0:T(8,128)(2,1)S(1)}, bf16[4,32,1152]{2,1,0:T(8,128)(2,1)S(1)}, u32[]{:S(2)}, u32[]{:S(2)}) collective-permute-start(bf16[4,32,1152]{2,1,0:T(8,128)(2,1)S(1)} %bitcast.15), channel_id=1, source_target_pairs={{0,128},{64,192},{128,0},{192,64},{1,129},{65,193},{129,1},{193,65... | collective-permute-start | bytes 884744 | tf_op jit(solution)/shard_map/ppermute | solution.py:26
  99.8 15.4 %collective-permute-start.14 = (bf16[4,32,1152]{2,1,0:T(8,128)(2,1)S(1)}, bf16[4,32,1152]{2,1,0:T(8,128)(2,1)S(1)}, u32[]{:S(2)}, u32[]{:S(2)}) collective-permute-start(bf16[4,32,1152]{2,1,0:T(8,128)(2,1)S(1)} %bitcast.16), channel_id=1, source_target_pairs={{0,192},{64,0},{128,64},{192,128},{1,193},{65,1},{129,65},{193,129... | collective-permute-start | bytes 884744 | tf_op jit(solution)/shard_map/ppermute | solution.py:26
  105.1 10.8 %collective-permute-start.11 = (f32[512,128]{1,0:T(8,128)S(1)}, f32[512,128]{1,0:T(8,128)S(1)}, u32[]{:S(2)}, u32[]{:S(2)}) collective-permute-start(f32[512,128]{1,0:T(8,128)S(1)} %get-tuple-element.65.refs_0_), channel_id=1, source_target_pairs={{0,4},{4,0},{1,5},{5,1},{2,6},{6,2},{3,7},{7,3},{8,12},{12,8},{9,1... | collective-permute-start | bytes 786440 | tf_op jit(solution)/shard_map/ppermute | solution.py:26
  108.9 13.4 %collective-permute-start.15 = (bf16[4,32,1152]{2,1,0:T(8,128)(2,1)S(1)}, bf16[4,32,1152]{2,1,0:T(8,128)(2,1)}, u32[]{:S(2)}, u32[]{:S(2)}) collective-permute-start(bf16[4,32,1152]{2,1,0:T(8,128)(2,1)S(1)} %bitcast.18), channel_id=1, source_target_pairs={{0,4},{4,0},{1,5},{5,1},{2,6},{6,2},{3,7},{7,3},{8,12},{12,8},{9,1... | collective-permute-start | bytes 884744 | tf_op jit(solution)/shard_map/ppermute | solution.py:26
  109.0 13.3 %collective-permute-start.16 = (bf16[4,32,1152]{2,1,0:T(8,128)(2,1)S(1)}, bf16[4,32,1152]{2,1,0:T(8,128)(2,1)}, u32[]{:S(2)}, u32[]{:S(2)}) collective-permute-start(bf16[4,32,1152]{2,1,0:T(8,128)(2,1)S(1)} %collective-permute-done.12.refs_2_), channel_id=1, source_target_pairs={{0,4},{4,0},{1,5},{5,1},{2,6},{6,2},{3,7},{7,3},{8,12},{12,8},{9,1... | collective-permute-start | bytes 884744 | tf_op jit(solution)/shard_map/ppermute | solution.py:26
  115.2 7.1 %collective-permute-start.17 = (bf16[4,32,1152]{2,1,0:T(8,128)(2,1)S(1)}, bf16[4,32,1152]{2,1,0:T(8,128)(2,1)}, u32[]{:S(2)}, u32[]{:S(2)}) collective-permute-start(bf16[4,32,1152]{2,1,0:T(8,128)(2,1)S(1)} %collective-permute-done.13.refs_3_), channel_id=1, source_target_pairs={{0,4},{4,0},{1,5},{5,1},{2,6},{6,2},{3,7},{7,3},{8,12},{12,8},{9,1... | collective-permute-start | bytes 884744 | tf_op jit(solution)/shard_map/ppermute | solution.py:26
  115.2 7.1 %collective-permute-start.18 = (bf16[4,32,1152]{2,1,0:T(8,128)(2,1)S(1)}, bf16[4,32,1152]{2,1,0:T(8,128)(2,1)}, u32[]{:S(2)}, u32[]{:S(2)}) collective-permute-start(bf16[4,32,1152]{2,1,0:T(8,128)(2,1)S(1)} %collective-permute-done.14.refs_4_), channel_id=1, source_target_pairs={{0,4},{4,0},{1,5},{5,1},{2,6},{6,2},{3,7},{7,3},{8,12},{12,8},{9,1... | collective-permute-start | bytes 884744 | tf_op jit(solution)/shard_map/ppermute | solution.py:26
  116.5 14.7 %all-to-all-start.4 = ((f32[32,4,128]{2,1,0:T(4,128)}), f32[32,4,128]{2,1,0:T(4,128)S(1)}, u32[]{:S(2)}, u32[]{:S(2)}) async-start(f32[32,4,128]{2,1,0:T(4,128)} %get-tuple-element.66), calls=%async_computation.4 | async-start | bytes 131072 | tf_op jit(solution)/shard_map/all_to_all | solution.py:30
  (4 other events, 78.4 us)
